TPU v7x, 32 devices: a whole 2x2x4 slice. The times are simulated.
32 devices in a mesh: wide: 8 (over z, y), narrow: 4 (over x, core).
Axes of the slice: x: 2, y: 2, z: 4, core: 2. Of those that a mesh axis runs over, the one named last changes fastest.
Arguments:
- object_field: float32 [2, 2048, 4096], P(None, 'narrow', 'wide')
- probe: float32 [4, 2, 256, 256], replicated, may hold values from -3 to 3
- patterns: float32 [4, 8, 6, 256, 256], P('narrow', 'wide'), may hold values from 0.1 to 4
- offsets: int32 [4, 8, 6, 2], P('narrow', 'wide'), may hold values from -128 to 384
- counts: int32 [4, 8], P('narrow', 'wide'), may hold values from 1 to 6
Outputs:
- object_new: float32 [2, 2048, 4096], P(None, 'narrow', 'wide')
- probe_new: float32 [4, 2, 256, 256], replicated
Inputs may be any that keep to these rules, and one draw needn't show every extreme that they name: A patch of 256 x 256 pixels at these offsets stays within the tile extended by 128 pixels on each side. `counts`: slots 0 to count - 1 of a tile are live, the others are ignored.
All inputs are finite; a program needn't handle non-finite values.
Results may differ from a plain program's by a relative error of at most 0.0003.
Values sent between devices are 32-bit elements; how exact they have to be, the bound alone decides.
No kernel may reach another device: no remote copies, remote signals or barrier semaphores. Data moves between devices by JAX's collectives and lax.ppermute only.
A program may use at most 128 MiB of HBM per device.

v0:
```python
import jax
import jax.numpy as jnp
from jax import lax
from jax.sharding import PartitionSpec as P

H = 128
BATCHES = 3
POS = 2


def extended(shard, sides, width):
    for axis, dim in sides:
        size, length = (lax.axis_size(axis), shard.shape[dim])
        up = [(i, (i + 1) % size) for i in range(size - 1)]
        down = [(j, i) for i, j in up]
        last = lax.slice_in_dim(shard, length - width, length, axis=dim)
        leading = lax.slice_in_dim(shard, 0, width, axis=dim)
        before = lax.ppermute(last, axis, up)
        after = lax.ppermute(leading, axis, down)
        shard = jnp.concatenate([before, shard, after], axis=dim)
    return shard


def shifted(value, axis, steps):
    count = lax.axis_size(axis)
    leading, last = (max(0, -steps), min(count, count - steps))
    return lax.ppermute(value, axis, [(source, source + steps) for source in range(leading, last)])


def dft_tables(size):
    index = jnp.arange(size, dtype=jnp.int32)
    phase = index[:, None] * index[None, :] % size
    angle = -2.0 * jnp.pi * phase.astype(jnp.float32) / size
    scale = 1.0 / jnp.sqrt(jnp.float32(size))
    return (jnp.cos(angle) * scale, jnp.sin(angle) * scale)


def transform(real_part, imag_part, table_re, table_im):
    high = lax.Precision.HIGHEST
    left_re = jnp.einsum("jk,mkl->mjl", table_re, real_part, precision=high) - jnp.einsum(
        "jk,mkl->mjl", table_im, imag_part, precision=high
    )
    left_im = jnp.einsum("jk,mkl->mjl", table_re, imag_part, precision=high) + jnp.einsum(
        "jk,mkl->mjl", table_im, real_part, precision=high
    )
    out_re = jnp.einsum("mjk,kl->mjl", left_re, table_re, precision=high) - jnp.einsum(
        "mjk,kl->mjl", left_im, table_im, precision=high
    )
    out_im = jnp.einsum("mjk,kl->mjl", left_re, table_im, precision=high) + jnp.einsum(
        "mjk,kl->mjl", left_im, table_re, precision=high
    )
    return (out_re, out_im)


def slot_terms(patch, probe, measured, table_re, table_im):
    probe_re = probe[:, 0]
    probe_im = probe[:, 1]
    obj_re = patch[0]
    obj_im = patch[1]
    psi_re = probe_re * obj_re - probe_im * obj_im
    psi_im = probe_re * obj_im + probe_im * obj_re
    far_re, far_im = transform(psi_re, psi_im, table_re, table_im)
    intensity = jnp.sum(far_re * far_re + far_im * far_im, axis=0)
    keep = 1.0 - jnp.sqrt(measured) / jnp.sqrt(intensity + 0.1)
    back_re, back_im = transform(far_re * keep, far_im * keep, table_re, -table_im)
    grad_re = jnp.sum(probe_re * back_re + probe_im * back_im, axis=0)
    grad_im = jnp.sum(probe_re * back_im - probe_im * back_re, axis=0)
    pgrad_re = obj_re * back_re + obj_im * back_im
    pgrad_im = obj_re * back_im - obj_im * back_re
    square = jnp.sum(obj_re * obj_re + obj_im * obj_im)
    return (jnp.stack([grad_re, grad_im]), jnp.stack([pgrad_re, pgrad_im], axis=1), square)


def local(object_field, probe, patterns, offsets, counts):
    tile = object_field.shape[1]
    size = probe.shape[-1]
    table_re, table_im = dft_tables(size)
    padded = extended(object_field, (("wide", 2), ("narrow", 1)), H)
    gradient = jnp.zeros_like(padded)
    count_here = counts[0, 0]
    zero_at = jnp.zeros((), jnp.int32)
    for minibatch in range(BATCHES):
        probe_grad = jnp.zeros_like(probe)
        coverage = jnp.zeros((), jnp.float32)
        for position in range(POS):
            slot_at = minibatch * POS + position
            row_at = offsets[0, 0, slot_at, 0] + H
            col_at = offsets[0, 0, slot_at, 1] + H
            patch = lax.dynamic_slice(padded, (zero_at, row_at, col_at), (2, size, size))
            measured = patterns[0, 0, slot_at]

            def active(operands):
                return slot_terms(operands[0], operands[1], operands[2], table_re, table_im)

            def inactive(operands):
                return (
                    jnp.zeros((2, size, size), jnp.float32),
                    jnp.zeros_like(probe),
                    jnp.zeros((), jnp.float32),
                )

            obj_grad, pgrad, square = lax.cond(
                slot_at < count_here, active, inactive, (patch, probe, measured)
            )
            old = lax.dynamic_slice(gradient, (zero_at, row_at, col_at), (2, size, size))
            gradient = lax.dynamic_update_slice(gradient, old + obj_grad, (zero_at, row_at, col_at))
            probe_grad = probe_grad + pgrad
            coverage = coverage + square
        summed, total_cover = lax.psum((probe_grad, coverage), ("wide", "narrow"))
        probe = probe - summed / (total_cover / (size * size))
    left_part = gradient[:, :, :H]
    right_part = gradient[:, :, tile + H :]
    from_right = shifted(left_part, "wide", -1)
    from_left = shifted(right_part, "wide", 1)
    gradient = gradient.at[:, :, tile : tile + H].add(from_right)
    gradient = gradient.at[:, :, H : 2 * H].add(from_left)
    upper_part = gradient[:, :H, H : tile + H]
    lower_part = gradient[:, tile + H :, H : tile + H]
    from_below = shifted(upper_part, "narrow", -1)
    from_above = shifted(lower_part, "narrow", 1)
    core = gradient[:, H : tile + H, H : tile + H]
    core = core.at[:, tile - H :, :].add(from_below)
    core = core.at[:, :H, :].add(from_above)
    power = jnp.sum(probe[:, 0] ** 2 + probe[:, 1] ** 2, axis=0)
    top = jnp.max(power)
    return (object_field - 0.5 * core / top, probe)


def solution(mesh):
    placed = (
        P(None, "narrow", "wide"),
        P(),
        P("narrow", "wide", None, None, None),
        P("narrow", "wide", None, None),
        P("narrow", "wide"),
    )
    return jax.shard_map(
        local,
        mesh=mesh,
        in_specs=placed,
        out_specs=(P(None, "narrow", "wide"), P()),
        check_vma=False,
    )
```

profile of v0, /device:TPU:0, one launch (start us, length us, event | category | flops | bytes accessed | tf_op | source)
XLA Modules:
  0.0 763.8 jit_solution(12050789135040865293)
XLA Ops:
  8.6 4.9 collective-permute-start
  14.9 21.1 %collective-permute-done = f32[2,512,128]{2,1,0:T(8,128)S(1)} collective-permute-done((f32[2,512,128]{2,1,0:T(8,128)S(1)}, f32[2,512,128]{2,1,0:T(8,128)S(1)}, u32[]{:S(2)}, u32[]{:S(2)}) %collective-permute-start) | collective-permute-done | bytes 524320 | tf_op jit(solution)/shard_map/ppermute | solution.py:18
  49.2 4.7 pad_maximum_fusion.12
  53.9 37.3 %conditional.6 = (f32[2,256,256]{2,1,0:T(8,128)S(1)}, f32[]{:T(128)}, f32[4,2,256,256]{3,2,1,0:T(8,128)}) conditional(s32[]{:T(128)} %bitcast.174, () %tuple.80, (f32[4,2,256,256]{3,2,1,0:T(8,128)S(1)}, f32[2,768,768]{2,1,0:T(8,128)}, f32[256,256]{1,0:T(8,128)S(1)}, f32[256,256]{1,0:T(8,128)S(1)}, f32[256,256]{1,0:T(8,128)S(1)}, ...), branch_computations={%region_0.1_spmd, %region_1.6_spmd.clone} | conditional | flops 12897091584 | bytes 71303224 | solution.py:102
  54.1 2.0 add_reduce_fusion.14
  67.3 2.1 convolution_subtract_fusion.18
  69.4 2.0 add_reduce_fusion.13
  81.5 2.2 fusion.184
  85.6 2.4 add_bitcast_fusion.4
  91.2 38.0 %conditional.7 = (f32[2,256,256]{2,1,0:T(8,128)S(1)}, f32[]{:T(128)}, f32[4,2,256,256]{3,2,1,0:T(8,128)}) conditional(s32[]{:T(128)} %bitcast.183, () %tuple.82, (f32[4,2,256,256]{3,2,1,0:T(8,128)S(1)}, f32[2,768,768]{2,1,0:T(8,128)}, f32[256,256]{1,0:T(8,128)S(1)}, f32[256,256]{1,0:T(8,128)S(1)}, f32[256,256]{1,0:T(8,128)S(1)}, ...), branch_computations={%region_6.7_spmd, %region_7.12_spmd.clone} | conditional | flops 12897091584 | bytes 71303224 | solution.py:102
  91.2 1.9 add_reduce_fusion.17
  104.4 2.1 convolution_subtract_fusion.22
  106.5 2.0 add_reduce_fusion.16
  118.6 2.2 fusion.225
  122.7 2.4 add_bitcast_fusion.5
  129.2 4.0 add.745
  138.5 47.0 %psum.43 = f32[]{:T(128)} all-reduce(f32[]{:T(128)S(6)} %add.746), channel_id=1, replica_groups=mesh['wide'=8,'narrow'=4] {'wide','narrow'}, use_global_device_ids=true, to_apply=%region_13.14 | all-reduce | flops 1 | bytes 8 | tf_op jit(solution)/shard_map/psum | solution.py:109
  186.2 89.0 %all-reduce.4.cloned.1.call-done = f32[4,2,256,256]{3,2,1,0:T(8,128)} async-done(((f32[4,2,256,256]{3,2,1,0:T(8,128)}), f32[4,2,256,256]{3,2,1,0:T(8,128)}) %all-reduce.4.cloned.1.call-update) | async-done | bytes 2097168 | tf_op jit(solution)/shard_map/psum | solution.py:109
  275.2 2.6 divide_subtract_fusion.3
  277.7 37.3 %conditional.8 = (f32[2,256,256]{2,1,0:T(8,128)}, f32[]{:T(128)}, f32[4,2,256,256]{3,2,1,0:T(8,128)}) conditional(s32[]{:T(128)} %bitcast.188, () %tuple.84, (f32[4,2,256,256]{3,2,1,0:T(8,128)S(1)}, f32[2,768,768]{2,1,0:T(8,128)}, s32[]{:T(128)}, s32[]{:T(128)}, f32[256,256]{1,0:T(8,128)S(1)}, /*index=5*/f32[256,256]{1,0:T(8,128)S(1)}, ...), branch_computations={%region_14.15_spmd, %region_15.20_spmd} | conditional | flops 12897091584 | bytes 71303224 | solution.py:102
  277.7 2.0 add_reduce_fusion.2
  291.0 2.1 convolution_subtract_fusion.2
  293.1 2.0 add_reduce_fusion.1
  305.2 2.2 fusion.20
  309.3 2.4 add_bitcast_fusion
  315.0 12.3 %conditional.9 = (f32[2,256,256]{2,1,0:T(8,128)}, f32[]{:T(128)}, f32[4,2,256,256]{3,2,1,0:T(8,128)}) conditional(s32[]{:T(128)} %bitcast.193, () %tuple.86, (f32[4,2,256,256]{3,2,1,0:T(8,128)S(1)}, f32[2,768,768]{2,1,0:T(8,128)}, s32[]{:T(128)}, s32[]{:T(128)}, f32[256,256]{1,0:T(8,128)S(1)}, /*index=5*/f32[256,256]{1,0:T(8,128)S(1)}, ...), branch_computations={%region_20.21_spmd, %region_21.26_spmd} | conditional | flops 12897091584 | bytes 71303224 | solution.py:102
  327.3 3.8 add.765
  335.9 2.5 broadcast_in_dim.2
  338.4 6.5 dynamic_update_slice.18
  346.4 6.8 dynamic_update_slice.19
  353.3 63.6 %psum.45 = f32[]{:T(128)} all-reduce(f32[]{:T(128)S(6)} %add.766), channel_id=1, replica_groups=mesh['wide'=8,'narrow'=4] {'wide','narrow'}, use_global_device_ids=true, to_apply=%region_27.28 | all-reduce | flops 1 | bytes 8 | tf_op jit(solution)/shard_map/psum | solution.py:109
  419.1 6.6 dynamic_update_slice.20
  427.2 6.7 dynamic_update_slice.21
  433.8 55.4 %all-reduce.6.cloned.1.call-done = f32[4,2,256,256]{3,2,1,0:T(8,128)} async-done(((f32[4,2,256,256]{3,2,1,0:T(8,128)}), f32[4,2,256,256]{3,2,1,0:T(8,128)}) %all-reduce.6.cloned.1.call-update) | async-done | bytes 2097168 | tf_op jit(solution)/shard_map/psum | solution.py:109
  489.2 3.2 divide_subtract_fusion.2
  492.4 11.6 %conditional.10 = (f32[2,256,256]{2,1,0:T(8,128)}, f32[]{:T(128)}, f32[4,2,256,256]{3,2,1,0:T(8,128)}) conditional(s32[]{:T(128)} %bitcast.198, () %tuple.88, (f32[4,2,256,256]{3,2,1,0:T(8,128)}, f32[2,768,768]{2,1,0:T(8,128)}, s32[]{:T(128)}, s32[]{:T(128)}, f32[256,256]{1,0:T(8,128)S(1)}, /*index=5*/f32[256,256]{1,0:T(8,128)S(1)}, ...), branch_computations={%region_28.29_spmd, %region_29.34_spmd} | conditional | flops 12897091584 | bytes 79691856 | solution.py:102
  505.7 6.6 dynamic_update_slice.22
  512.3 5.1 conditional.11
  518.8 6.4 dynamic_update_slice.23
  527.7 78.1 %collective-permute-done.4 = f32[2,768,128]{2,1,0:T(8,128)S(1)} collective-permute-done((f32[2,768,128]{2,1,0:T(8,128)S(1)}, f32[2,768,128]{2,1,0:T(8,128)S(1)}, u32[]{:S(2)}, u32[]{:S(2)}) %collective-permute-start.4) | collective-permute-done | bytes 786464 | tf_op jit(solution)/shard_map/ppermute | solution.py:27
  605.8 2.7 fusion.259
  608.5 4.6 collective-permute-start.5
  613.1 3.8 add.781
  617.0 48.5 %psum.47 = f32[]{:T(128)} all-reduce(f32[]{:T(128)S(6)} %add.782), channel_id=1, replica_groups=mesh['wide'=8,'narrow'=4] {'wide','narrow'}, use_global_device_ids=true, to_apply=%region_41.42 | all-reduce | flops 1 | bytes 8 | tf_op jit(solution)/shard_map/psum | solution.py:109
  666.1 2.2 fusion.248
  668.3 2.3 fusion.258
  673.2 73.7 %all-reduce.8.cloned.1.call-done = f32[4,2,256,256]{3,2,1,0:T(8,128)} async-done(((f32[4,2,256,256]{3,2,1,0:T(8,128)}), f32[4,2,256,256]{3,2,1,0:T(8,128)}) %all-reduce.8.cloned.1.call-update) | async-done | bytes 2097168 | tf_op jit(solution)/shard_map/psum | solution.py:109
  754.6 2.4 divide_subtract_fusion
  (107 shorter events, 112.3 us)
Async XLA Ops:
  7.2 28.8 %copy-start.3 = (f32[2,512,512]{2,1,0:T(8,128)S(1)}, f32[2,512,512]{2,1,0:T(8,128)}, u32[]{:S(2)}) copy-start(f32[2,512,512]{2,1,0:T(8,128)} %param.25) | copy-start | bytes 6291460
  7.2 268.0 %all-reduce.4.cloned.1.call-start = ((), (), s32[]{:S(2)}) async-start(), calls=%async_computation | async-start | bytes 4194304 | tf_op jit(solution)/shard_map/psum | solution.py:109
  8.6 27.3 %collective-permute-start = (f32[2,512,128]{2,1,0:T(8,128)S(1)}, f32[2,512,128]{2,1,0:T(8,128)S(1)}, u32[]{:S(2)}, u32[]{:S(2)}) collective-permute-start(f32[2,512,128]{2,1,0:T(8,128)S(1)} %get-tuple-element.871), channel_id=1, source_target_pairs={{0,4},{4,8},{8,12},{12,16},{16,20},{20,24},{24,28},{1,5},{5,9},{9,... | collective-permute-start | bytes 1572872 | tf_op jit(solution)/shard_map/ppermute | solution.py:18
  13.6 22.6 %collective-permute-start.1 = (f32[2,512,128]{2,1,0:T(8,128)S(1)}, f32[2,512,128]{2,1,0:T(8,128)S(1)}, u32[]{:S(2)}, u32[]{:S(2)}) collective-permute-start(f32[2,512,128]{2,1,0:T(8,128)S(1)} %get-tuple-element.870), channel_id=1, source_target_pairs={{4,0},{8,4},{12,8},{16,12},{20,16},{24,20},{28,24},{5,1},{9,5},{13... | collective-permute-start | bytes 1572872 | tf_op jit(solution)/shard_map/ppermute | solution.py:19
  36.2 5.6 copy-start.8
  36.2 1.7 copy-start.5
  39.2 10.1 %collective-permute-start.2 = (f32[2,128,768]{2,1,0:T(8,128)}, f32[2,128,768]{2,1,0:T(8,128)S(1)}, u32[]{:S(2)}, u32[]{:S(2)}) collective-permute-start(f32[2,128,768]{2,1,0:T(8,128)} %get-tuple-element.868), channel_id=1, source_target_pairs={{0,1},{1,2},{2,3},{4,5},{5,6},{6,7},{8,9},{9,10},{10,11},{12,13},{... | collective-permute-start | bytes 2359304 | tf_op jit(solution)/shard_map/ppermute | solution.py:18
  40.5 8.7 %collective-permute-start.3 = (f32[2,128,768]{2,1,0:T(8,128)}, f32[2,128,768]{2,1,0:T(8,128)}, u32[]{:S(2)}, u32[]{:S(2)}) collective-permute-start(f32[2,128,768]{2,1,0:T(8,128)} %get-tuple-element.869), channel_id=1, source_target_pairs={{1,0},{2,1},{3,2},{5,4},{6,5},{7,6},{9,8},{10,9},{11,10},{13,12},{... | collective-permute-start | bytes 2359304 | tf_op jit(solution)/shard_map/ppermute | solution.py:19
  49.2 4.7 copy-start.2
  129.2 4.0 copy-start.7
  133.3 355.9 %all-reduce.6.cloned.1.call-start = ((), (), s32[]{:S(2)}) async-start(), calls=%async_computation.1 | async-start | bytes 4194304 | tf_op jit(solution)/shard_map/psum | solution.py:109
  331.1 415.8 %all-reduce.8.cloned.1.call-start = ((), (), s32[]{:S(2)}) async-start(), calls=%async_computation.2 | async-start | bytes 4194304 | tf_op jit(solution)/shard_map/psum | solution.py:109
  504.0 8.2 %copy-start = (f32[4,2,256,256]{3,2,1,0:T(8,128)S(1)}, f32[4,2,256,256]{3,2,1,0:T(8,128)}, u32[]{:S(2)}) copy-start(f32[4,2,256,256]{3,2,1,0:T(8,128)} %divide_subtract_fusion.2) | copy-start | bytes 6291460
  526.4 79.4 %collective-permute-start.4 = (f32[2,768,128]{2,1,0:T(8,128)S(1)}, f32[2,768,128]{2,1,0:T(8,128)S(1)}, u32[]{:S(2)}, u32[]{:S(2)}) collective-permute-start(f32[2,768,128]{2,1,0:T(8,128)S(1)} %slice.336), channel_id=1, source_target_pairs={{4,0},{8,4},{12,8},{16,12},{20,16},{24,20},{28,24},{5,1},{9,5},{13... | collective-permute-start | bytes 2359304 | tf_op jit(solution)/shard_map/ppermute | solution.py:27
  608.5 57.6 %collective-permute-start.5 = (f32[2,768,128]{2,1,0:T(8,128)}, f32[2,768,128]{2,1,0:T(8,128)S(1)}, u32[]{:S(2)}, u32[]{:S(2)}) collective-permute-start(f32[2,768,128]{2,1,0:T(8,128)} %get-tuple-element.866), channel_id=1, source_target_pairs={{0,4},{4,8},{8,12},{12,16},{16,20},{20,24},{24,28},{1,5},{5,9},{9,... | collective-permute-start | bytes 2359304 | tf_op jit(solution)/shard_map/ppermute | solution.py:27
  670.6 83.6 %collective-permute-start.7 = (f32[2,128,512]{2,1,0:T(8,128)}, f32[2,128,512]{2,1,0:T(8,128)S(1)}, u32[]{:S(2)}, u32[]{:S(2)}) collective-permute-start(f32[2,128,512]{2,1,0:T(8,128)} %get-tuple-element.864), channel_id=1, source_target_pairs={{0,1},{1,2},{2,3},{4,5},{5,6},{6,7},{8,9},{9,10},{10,11},{12,13},{... | collective-permute-start | bytes 1572872 | tf_op jit(solution)/shard_map/ppermute | solution.py:27
  671.9 80.8 %collective-permute-start.6 = (f32[2,128,512]{2,1,0:T(8,128)}, f32[2,128,512]{2,1,0:T(8,128)}, u32[]{:S(2)}, u32[]{:S(2)}) collective-permute-start(f32[2,128,512]{2,1,0:T(8,128)} %get-tuple-element.865), channel_id=1, source_target_pairs={{1,0},{2,1},{3,2},{5,4},{6,5},{7,6},{9,8},{10,9},{11,10},{13,12},{... | collective-permute-start | bytes 1572872 | tf_op jit(solution)/shard_map/ppermute | solution.py:27
  748.8 1.3 copy-start.6
  752.7 1.9 copy-start.4
Sparse Core Ops, SparseCore 0:
  133.4 141.7 all-reduce.3
  331.3 157.8 all-reduce.5
  617.1 129.8 all-reduce.7
where the time goes:
time: 770 us; the launch traced here: 764 us
  waiting for transfers between devices  317 us (41%)
  blocking collectives  159 us (21%)
  matrix products  92.4 us (12%)
  local copies, waits for them, and re-layouts  64.8 us (8%)
  other arithmetic  52.7 us (7%)
  between operations  31.9 us (4%)
  loops' own time  28.1 us (4%)
  starting transfers between devices  17.4 us (2%)
    psum x3, waiting for transfers between devices, local(): summed, total_cover = lax.psum((probe_grad, coverage), ('wide', 'narrow'))  218 us
    psum x3, blocking collectives, local(): summed, total_cover = lax.psum((probe_grad, coverage), ('wide', 'narrow'))  159 us
    ppermute x4, waiting for transfers between devices, shifted(): lax.ppermute(value, axis, [(source, source + steps) for source in range(l...  78.1 us
    dynamic_update_slice x6, local copies, waits for them, and re-layouts, local(): lax.dynamic_update_slice(gradient, old + obj_grad, (zero_at, row_at, col_...  39.6 us
    another operation x6, loops' own time, local(): lax.cond(slot_at < count_here, active, inactive, (patch, probe, measured))  28.1 us
    ppermute x2, waiting for transfers between devices, extended(): before = lax.ppermute(last, axis, up)  21.1 us
  transfers between devices with their start and end apart: 11, of which 5 were waited for; matrix products, arithmetic and copies ran while one was open for 7% of the time, Pallas kernels for 0%

commit v1 on v0

v1 whole, which is shorter than its diff:
```python
import functools

import jax
import jax.numpy as jnp
import ml_dtypes
import numpy as np
from jax import lax
from jax.experimental import pallas as pl
from jax.experimental.pallas import tpu as pltpu
from jax.sharding import PartitionSpec as P

H = 128
BATCHES = 3
POS = 2
AXES = ("wide", "narrow")
F32 = jnp.float32
BF16 = jnp.bfloat16
VMEM_LIMIT = 48 * 1024 * 1024


def halves(table):
    high = table.astype(ml_dtypes.bfloat16)
    low = (table - high.astype(np.float64)).astype(ml_dtypes.bfloat16)
    return np.stack([high, low])


def dft_tables(size):
    half = size // 2
    k = np.arange(half)
    out = []
    for odd in range(2):
        phase = ((2 * k[:, None] + odd) * k[None, :]) % size
        angle = -2.0 * np.pi * phase / size
        re, im = np.cos(angle) / np.sqrt(size), np.sin(angle) / np.sqrt(size)
        out.append(np.block([[re, -im], [im, re]]))
    return np.stack([halves(t) for t in (out[0], out[1], out[0].T, out[1].T)])


def split(x):
    high = x.astype(BF16)
    return high, (x - high.astype(F32)).astype(BF16)


def dot(a, b):
    return jnp.dot(a, b, preferred_element_type=F32)


def left(tables, which, x):
    high, low = split(x)
    t_high, t_low = tables[which, 0], tables[which, 1]
    return dot(t_high, high) + dot(t_high, low) + dot(t_low, high)


def right(x, tables, which):
    high, low = split(x)
    t_high, t_low = tables[which, 0], tables[which, 1]
    return dot(high, t_high) + dot(low, t_high) + dot(high, t_low)


def forward(tables, re, im):
    h = re.shape[0] // 2
    u = jnp.concatenate([re[:h] + re[h:], im[:h] + im[h:]], 0)
    v = jnp.concatenate([re[:h] - re[h:], im[:h] - im[h:]], 0)
    even, odd = left(tables, 0, u), left(tables, 1, v)

    def columns(op):
        rows = [jnp.concatenate([op(y[:h, :h], y[:h, h:]), op(y[h:, :h], y[h:, h:])], 1) for y in (even, odd)]
        return jnp.concatenate(rows, 0)

    return (
        right(columns(lambda a, b: a + b), tables, 2),
        right(columns(lambda a, b: a - b), tables, 3),
    )


def inverse(tables, even, odd):
    h = even.shape[0] // 2
    a, b = right(even, tables, 0), right(odd, tables, 1)
    s, d = a + b, a - b

    def rows(lo):
        return jnp.concatenate(
            [
                jnp.concatenate([s[lo : lo + h, :h], d[lo : lo + h, :h]], 1),
                jnp.concatenate([s[lo : lo + h, h:], d[lo : lo + h, h:]], 1),
            ],
            0,
        )

    a, b = left(tables, 2, rows(0)), left(tables, 3, rows(h))
    s, d = a + b, a - b
    return jnp.concatenate([s[:h], d[:h]], 0), jnp.concatenate([s[h:], d[h:]], 0)


def spectrum_of(tables, patch, probe, mode):
    size = patch.shape[-1]
    base = mode * 2 * size
    p_re, p_im = probe[base : base + size], probe[base + size : base + 2 * size]
    o_re, o_im = patch[0, 0], patch[0, 1]
    return forward(tables, p_re * o_re - p_im * o_im, p_re * o_im + p_im * o_re)


def power_of(z):
    h = z.shape[-1] // 2
    return z[:, :h] * z[:, :h] + z[:, h:] * z[:, h:]


def gradients(tables, patch, probe, mode, even, odd, keep, pgrad, gpatch):
    size = patch.shape[-1]
    base = mode * 2 * size
    k_even, k_odd = keep[0, 0], keep[0, 1]
    b_re, b_im = inverse(
        tables,
        even * jnp.concatenate([k_even, k_even], 1),
        odd * jnp.concatenate([k_odd, k_odd], 1),
    )
    p_re, p_im = probe[base : base + size], probe[base + size : base + 2 * size]
    o_re, o_im = patch[0, 0], patch[0, 1]
    gpatch[0, 0] += p_re * b_re + p_im * b_im
    gpatch[0, 1] += p_re * b_im - p_im * b_re
    pgrad[base : base + size] += o_re * b_re + o_im * b_im
    pgrad[base + size : base + 2 * size] += o_re * b_im - o_im * b_re


def whole(*shape):
    return pl.BlockSpec(shape, lambda i, *_: (0,) * len(shape))


def per_slot(*shape):
    return pl.BlockSpec((1, *shape), lambda i, *_: (i,) + (0,) * len(shape))


def per_batch_slot(batch, *shape):
    return pl.BlockSpec((1, *shape), lambda i, *_: (batch * POS + i,) + (0,) * len(shape))


def call(body, scalars, operands, in_specs, out_shapes, out_specs, grid, scratch=(), aliases=None, flops=0, moved=0):
    return pl.pallas_call(
        body,
        out_shape=[jax.ShapeDtypeStruct(s, F32) for s in out_shapes],
        grid_spec=pltpu.PrefetchScalarGridSpec(
            num_scalar_prefetch=len(scalars),
            grid=(grid,),
            in_specs=in_specs,
            out_specs=out_specs,
            scratch_shapes=list(scratch),
        ),
        input_output_aliases=aliases or {},
        compiler_params=pltpu.CompilerParams(vmem_limit_bytes=VMEM_LIMIT),
        cost_estimate=pl.CostEstimate(flops=flops, bytes_accessed=moved, transcendentals=0),
    )(*scalars, *operands)


def cut_patches(offsets, tile, sides, size, slots):
    edge = tile.shape[1]
    full = edge + 2 * H

    def body(offs, tile_ref, left_ref, right_ref, top_ref, bottom_ref, out, ext):
        i = pl.program_id(0)

        @pl.when(i == 0)
        def _():
            ext[:, :H] = top_ref[...]
            ext[:, H + edge :] = bottom_ref[...]
            ext[:, H : H + edge, :H] = left_ref[...]
            ext[:, H : H + edge, H : H + edge] = tile_ref[...]
            ext[:, H : H + edge, H + edge :] = right_ref[...]

        row = offs[2 * i] + H
        col = offs[2 * i + 1] + H
        row_at = pl.multiple_of(jnp.minimum(row // 8 * 8, full - size - 8), 8)
        col_at = pl.multiple_of(jnp.minimum(col // 128 * 128, full - size - 128), 128)
        for part in range(2):
            block = ext[part, pl.ds(row_at, size + 8), pl.ds(col_at, size + 128)]
            block = pltpu.roll(block, size + 128 - (col - col_at), 1)[:, :size]
            block = pltpu.roll(block, size + 8 - (row - row_at), 0)[:size]
            out[0, part] = block

    return call(
        body,
        [offsets],
        [tile, *sides],
        [whole(2, edge, edge), whole(2, edge, H), whole(2, edge, H), whole(2, H, full), whole(2, H, full)],
        [(slots, 2, size, size)],
        [per_slot(2, size, size)],
        slots,
        scratch=[pltpu.VMEM((2, full, full), F32)],
        flops=10**6,
        moved=8 * 10**6,
    )[0]


def place_gradients(offsets, counts, patches, gradient, batch, full):
    size = patches.shape[-1]
    first = gradient is None

    def body(offs, counts_ref, patch_ref, *rest):
        out = rest[-1]
        i = pl.program_id(0)

        @pl.when(i == 0)
        def _():
            out[...] = jnp.zeros_like(out) if first else rest[0][...]

        slot = batch * POS + i

        @pl.when(slot < counts_ref[0])
        def _():
            row = offs[2 * slot] + H
            col = offs[2 * slot + 1] + H
            row_at = pl.multiple_of(jnp.minimum(row // 8 * 8, full - size - 8), 8)
            col_at = pl.multiple_of(jnp.minimum(col // 128 * 128, full - size - 128), 128)
            for part in range(2):
                block = patch_ref[0, part]
                block = jnp.concatenate([block, jnp.zeros((8, size), F32)], 0)
                block = pltpu.roll(block, row - row_at, 0)
                block = jnp.concatenate([block, jnp.zeros((size + 8, 128), F32)], 1)
                block = pltpu.roll(block, col - col_at, 1)
                out[part, pl.ds(row_at, size + 8), pl.ds(col_at, size + 128)] += block

    operands, specs = [patches], [per_slot(2, size, size)]
    if not first:
        operands, specs = [*operands, gradient], [*specs, whole(2, full, full)]
    return call(
        body,
        [offsets, counts],
        operands,
        specs,
        [(2, full, full)],
        [whole(2, full, full)],
        POS,
        flops=10**6,
        moved=10**7,
    )[0]


def merge_borders(gradient, from_right, from_left, from_below, from_above, edge):
    full = edge + 2 * H

    def body(g, fr, fl, fb, fa, out):
        out[...] = g[:, H : H + edge, H : H + edge]
        out[:, :, edge - H :] += fr[:, H : H + edge]
        out[:, :, :H] += fl[:, H : H + edge]
        out[:, edge - H :] += fb[...]
        out[:, :H] += fa[...]

    return call(
        body,
        [],
        [gradient, from_right, from_left, from_below, from_above],
        [whole(2, full, full), whole(2, full, H), whole(2, full, H), whole(2, H, edge), whole(2, H, edge)],
        [(2, edge, edge)],
        [whole(2, edge, edge)],
        1,
        flops=10**6,
        moved=10**7,
    )[0]


def forward_kernel(tables, counts, patches, probe, batch):
    size = patches.shape[-1]
    h = size // 2
    modes = probe.shape[0] // (2 * size)

    def body(counts_ref, t, patch, p, z, inten):
        @pl.when(batch * POS + pl.program_id(0) < counts_ref[0])
        def _():
            for m in range(modes):
                even, odd = spectrum_of(t, patch, p, m)
                z[0, m, 0] = even
                z[0, m, 1] = odd
                if m == 0:
                    inten[0, 0] = power_of(even)
                    inten[0, 1] = power_of(odd)
                else:
                    inten[0, 0] += power_of(even)
                    inten[0, 1] += power_of(odd)

    return call(
        body,
        [counts],
        [tables, patches, probe],
        [whole(*tables.shape), per_batch_slot(batch, 2, size, size), whole(*probe.shape)],
        [(POS, modes, 2, size, size), (POS, 2, size, h)],
        [per_slot(modes, 2, size, size), per_slot(2, size, h)],
        POS,
        flops=POS * modes * 24 * size**3,
        moved=4 * 10**6,
    )


def turn_kernel(tables, counts, patches, probe, roots, intensities, batch):
    size = patches.shape[-1]
    h = size // 2
    rows = probe.shape[0]
    modes = rows // (2 * size)
    n = len(intensities)

    def body(counts_ref, t, patch, p, root, *rest):
        parts, (sent, keep, gpatch, z) = rest[:n], rest[n:]
        i = pl.program_id(0)

        @pl.when(i == 0)
        def _():
            sent[...] = jnp.zeros_like(sent)

        gpatch[...] = jnp.zeros_like(gpatch)

        @pl.when(batch * POS + i < counts_ref[0])
        def _():
            for m in range(modes):
                even, odd = spectrum_of(t, patch, p, m)
                z[m, 0] = even
                z[m, 1] = odd
            for e in range(2):
                total = parts[0][0, e]
                for part in parts[1:]:
                    total = total + part[0, e]
                for m in range(modes):
                    total = total + power_of(z[m, e])
                keep[0, e] = 1.0 - root[0, e] * lax.rsqrt(total + 0.1)
            for m in range(modes):
                gradients(t, patch, p, m, z[m, 0], z[m, 1], keep, sent, gpatch)
            o_re, o_im = patch[0, 0], patch[0, 1]
            square = (o_re * o_re + o_im * o_im).reshape(size // 8, 8, size)
            sent[rows:] += jnp.sum(square, axis=0)

    return call(
        body,
        [counts],
        [tables, patches, probe, roots, *intensities],
        [
            whole(*tables.shape),
            per_batch_slot(batch, 2, size, size),
            whole(*probe.shape),
            per_batch_slot(batch, 2, size, h),
        ]
        + [per_slot(2, size, h)] * n,
        [(rows + 8, size), (POS, 2, size, h), (POS, 2, size, size)],
        [whole(rows + 8, size), per_slot(2, size, h), per_slot(2, size, size)],
        POS,
        scratch=[pltpu.VMEM((modes, 2, size, size), F32)],
        flops=POS * modes * 48 * size**3,
        moved=8 * 10**6,
    )


def gradient_kernel(tables, counts, patches, probe, spectra, keep, gpatch, batch):
    size = patches.shape[-1]
    h = size // 2
    modes = probe.shape[0] // (2 * size)

    def body(counts_ref, t, patch, p, z, k, g_in, pgrad, g_out):
        i = pl.program_id(0)

        @pl.when(i == 0)
        def _():
            pgrad[...] = jnp.zeros_like(pgrad)

        g_out[...] = g_in[...]

        @pl.when(batch * POS + i < counts_ref[0])
        def _():
            for m in range(modes):
                gradients(t, patch, p, m, z[0, m, 0], z[0, m, 1], k, pgrad, g_out)

    return call(
        body,
        [counts],
        [tables, patches, probe, spectra, keep, gpatch],
        [
            whole(*tables.shape),
            per_batch_slot(batch, 2, size, size),
            whole(*probe.shape),
            per_slot(modes, 2, size, size),
            per_slot(2, size, h),
            per_slot(2, size, size),
        ],
        [probe.shape, (POS, 2, size, size)],
        [whole(*probe.shape), per_slot(2, size, size)],
        POS,
        flops=POS * modes * 24 * size**3,
        moved=6 * 10**6,
    )


def flips(wide, narrow):
    bits = [(0, 2 << i) for i in range(1, narrow.bit_length() - 2)] + [
        (1 << i, 0) for i in range(1, wide.bit_length() - 1)
    ]

    def exchange(even, odd):
        pairs = []
        for w in range(wide):
            for n in range(narrow):
                dw, dn = odd if n & 1 else even
                pairs.append((w * narrow + n, (w ^ dw) * narrow + (n ^ dn)))
        return functools.partial(lax.ppermute, axis_name=AXES, perm=pairs)

    core = exchange((0, 1), (0, 1))
    first = exchange((0, 2), (1, 0))
    second = exchange((1, 0), (0, 2))
    return core, first, second, [exchange(a, b) for a, b in zip(bits, bits[::-1])]


def shifted(value, axis, steps):
    count = lax.axis_size(axis)
    leading, last = (max(0, -steps), min(count, count - steps))
    return lax.ppermute(value, axis, [(source, source + steps) for source in range(leading, last)])


def local(object_field, probe, patterns, offsets, counts):
    edge = object_field.shape[1]
    modes, _, size, _ = probe.shape
    slots = patterns.shape[2]
    h = size // 2
    full = edge + 2 * H
    wide, narrow = lax.axis_size("wide"), lax.axis_size("narrow")
    w, n = lax.axis_index("wide"), lax.axis_index("narrow")
    core, first, second, rest = flips(wide, narrow)
    offs = offsets.reshape(slots * 2)
    count = counts.reshape(1)

    left_side = shifted(object_field[:, :, edge - H :], "wide", 1)
    right_side = shifted(object_field[:, :, :H], "wide", -1)

    def strip(lo):
        return jnp.concatenate([x[:, lo : lo + H] for x in (left_side, object_field, right_side)], 2)

    top_side = shifted(strip(edge - H), "narrow", 1)
    bottom_side = shifted(strip(0), "narrow", -1)

    tables = jnp.asarray(dft_tables(size))
    order = np.concatenate([np.arange(0, size, 2), np.arange(1, size, 2)])
    pick = jnp.asarray(np.eye(size, dtype=np.float32)[order])
    roots = jnp.einsum("pj,sjk->spk", pick, jnp.sqrt(patterns[0, 0]), precision=lax.Precision.HIGHEST)
    roots = jnp.einsum("spk,qk->spq", roots, pick, precision=lax.Precision.HIGHEST)
    roots = roots.reshape(slots, size, 2, h).transpose(0, 2, 1, 3)

    c = n % 2
    bit_n, bit_w = (n // 2) % 2, w % 2
    b1 = jnp.where(c == 0, bit_n, bit_w)
    b2 = jnp.where(c == 0, bit_w, bit_n)
    ours, theirs = 2 * c, 2 * (1 - c)
    order_of = [ours + b1, ours + 1 - b1, theirs + b2, theirs + 1 - b2]
    rows = modes // 4 * 2 * size
    groups = probe.reshape(4, rows, size)
    p0, p1, p2, p3 = [lax.dynamic_index_in_dim(groups, m, 0, keepdims=False) for m in order_of]

    patches = cut_patches(offs, object_field, (left_side, right_side, top_side, bottom_side), size, slots)

    half, quarter = rows // 2, rows // 4
    gradient = None
    for batch in range(BATCHES):
        z0, i0 = forward_kernel(tables, count, patches, p0, batch)
        z1, i1 = forward_kernel(tables, count, patches, p1, batch)
        p23 = jnp.concatenate([p2, p3], 0)
        sent, keep, gpatch = turn_kernel(tables, count, patches, p23, roots, (i0, i1), batch)
        got = core(sent)
        cover = sent[2 * rows :] + got[2 * rows :]
        g1, gpatch = gradient_kernel(tables, count, patches, p1, z1, keep, gpatch, batch)
        g1 = g1 + got[rows : 2 * rows]
        got_a = first(jnp.concatenate([g1[:half], cover], 0))
        got_b = first(g1[half:])
        g0, gpatch = gradient_kernel(tables, count, patches, p0, z0, keep, gpatch, batch)
        g0 = g0 + got[:rows]
        cover = cover + got_a[half:]
        a = (g0[:half] + got_a[:half]).reshape(2, quarter, size)
        b = (g0[half:] + got_b).reshape(2, quarter, size)

        def part(x, at):
            return lax.dynamic_index_in_dim(x, at, 0, keepdims=False)

        got_a = second(jnp.concatenate([part(a, 1 - b2), cover], 0))
        got_b = second(part(b, 1 - b2))
        a = part(a, b2) + got_a[:quarter]
        b = part(b, b2) + got_b
        cover = cover + got_a[quarter:]
        for exchange in rest:
            got_a = exchange(jnp.concatenate([a, cover], 0))
            got_b = exchange(b)
            a = a + got_a[:quarter]
            cover = cover + got_a[quarter:]
            b = b + got_b
        scale = jnp.sum(cover) / (size * size)
        old_a = part(p0[:half].reshape(2, quarter, size), b2)
        old_b = part(p0[half:].reshape(2, quarter, size), b2)
        a = old_a - a / scale
        b = old_b - b / scale
        got_a = second(a)
        got_b = second(b)

        def join(mine, other):
            return jnp.where(b2 == 0, jnp.concatenate([mine, other], 0), jnp.concatenate([other, mine], 0))

        a, b = join(a, got_a), join(b, got_b)
        got_a, got_b = first(a), first(b)
        p0 = jnp.concatenate([a, b], 0)
        p2 = core(p0)
        p1 = jnp.concatenate([got_a, got_b], 0)
        p3 = core(p1)
        gradient = place_gradients(offs, count, gpatch, gradient, batch, full)

    from_right = shifted(gradient[:, :, :H], "wide", -1)
    from_left = shifted(gradient[:, :, H + edge :], "wide", 1)

    def border(lo):
        inner = gradient[:, lo : lo + H, H : H + edge]
        inner = inner + jnp.pad(from_right[:, lo : lo + H], ((0, 0), (0, 0), (edge - H, 0)))
        return inner + jnp.pad(from_left[:, lo : lo + H], ((0, 0), (0, 0), (0, edge - H)))

    from_below = shifted(border(0), "narrow", -1)
    from_above = shifted(border(H + edge), "narrow", 1)
    inner = merge_borders(gradient, from_right, from_left, from_below, from_above, edge)

    by_group = jnp.stack([p0, p1, p2, p3])
    where = jnp.stack([jnp.argmax(jnp.stack(order_of) == m) for m in range(4)])
    probe_new = jnp.take(by_group, where, axis=0).reshape(probe.shape)
    squares = by_group.reshape(modes, 2, size, size)
    top = jnp.max(jnp.sum(squares[:, 0] ** 2 + squares[:, 1] ** 2, axis=0))
    return (object_field - (0.5 / top) * inner, probe_new)


def solution(mesh):
    placed = (
        P(None, "narrow", "wide"),
        P(),
        P("narrow", "wide", None, None, None),
        P("narrow", "wide", None, None),
        P("narrow", "wide"),
    )
    return jax.shard_map(
        local,
        mesh=mesh,
        in_specs=placed,
        out_specs=(P(None, "narrow", "wide"), P()),
        check_vma=False,
    )
```

time: 770 us -> 338 us (0.44)
  waiting for transfers between devices: 317 us -> 114 us
  blocking collectives: 159 us -> 0 us
  matrix products: 92.4 us -> 4.47 us
  Pallas kernels: 0 us -> 69.3 us
  starting transfers between devices: 17.4 us -> 76.9 us
  local copies, waits for them, and re-layouts: 64.8 us -> 24.5 us
  loops' own time: 28.1 us -> 0 us
  between operations: 31.9 us -> 5.09 us
  other arithmetic: 52.7 us -> 42.6 us
    psum x3 -> x0, waiting for transfers between devices: 218 us -> none  [local(): summed, total_cover = lax.psum((probe_grad, coverage), ('wide', 'narrow'))]
    psum x3 -> x0, blocking collectives: 159 us -> none  [local(): summed, total_cover = lax.psum((probe_grad, coverage), ('wide', 'narrow'))]
    dot_general x48 -> x2, matrix products: 92.4 us -> 4.47 us  [the longest x1 2.7 us: local(): jnp.einsum('spk,qk->spq', roots, pick, precision=lax.Precision.HIGHEST)]
    ppermute x4 -> x45, waiting for transfers between devices: 21.1 us -> 93.3 us  [the longest x3 29.6 us: local(): got_b = second(part(b, 1 - b2))]
    pallas_call x0 -> x20, Pallas kernels: none -> 69.3 us  [call(): pl.pallas_call(body, out_shape=[jax.ShapeDtypeStruct(s, F32) for s in out...]
    ppermute x4 -> x8, waiting for transfers between devices: 78.1 us -> 20.6 us  [shifted(): lax.ppermute(value, axis, [(source, source + steps) for source in range(l...]
    ppermute x4 -> x45, starting transfers between devices: 8.81 us -> 55.4 us  [the longest x6 9.41 us: local(): got_a = exchange(jnp.concatenate([a, cover], 0))]
    dynamic_update_slice x6 -> x0, local copies, waits for them, and re-layouts: 39.6 us -> none  [local(): lax.dynamic_update_slice(gradient, old + obj_grad, (zero_at, row_at, col_...]
  transfers between devices with their start and end apart: 11 -> 53, of which waited for: 5 -> 22; matrix products, arithmetic and copies ran while one was open for 7% -> 12% of each run, Pallas kernels for 0% -> 11%
where the time goes in v1:
time: 338 us; the launch traced here: 337 us
  waiting for transfers between devices  114 us (34%)
  starting transfers between devices  76.9 us (23%)
  Pallas kernels  69.3 us (21%)
  other arithmetic  42.6 us (13%)
  local copies, waits for them, and re-layouts  24.5 us (7%)
  between operations  5.09 us (2%)
  matrix products  4.47 us (1%)
    pallas_call x20, Pallas kernels, call(): pl.pallas_call(body, out_shape=[jax.ShapeDtypeStruct(s, F32) for s in out...  69.3 us
    ppermute x3, waiting for transfers between devices, local(): got_b = second(part(b, 1 - b2))  29.6 us
    ppermute x8, starting transfers between devices, shifted(): lax.ppermute(value, axis, [(source, source + steps) for source in range(l...  21.5 us
    ppermute x8, waiting for transfers between devices, shifted(): lax.ppermute(value, axis, [(source, source + steps) for source in range(l...  20.6 us
    ppermute x3, waiting for transfers between devices, local(): got_b = first(g1[half:])  14.6 us
    ppermute x6, waiting for transfers between devices, local(): got_b = exchange(b)  13.8 us
    ppermute x6, waiting for transfers between devices, local(): got_a, got_b = (first(a), first(b))  11.7 us
    unnamed x72, local copies, waits for them, and re-layouts  10.8 us
  transfers between devices with their start and end apart: 53, of which 22 were waited for; matrix products, arithmetic and copies ran while one was open for 12% of the time, Pallas kernels for 11%

profile of v1, /device:TPU:0, one launch (start us, length us, event | category | flops | bytes accessed | tf_op | source)
XLA Modules:
  0.0 336.8 jit_solution(8692842984416327965)
XLA Ops:
  0.6 2.4 fusion.22
  4.3 5.5 %collective-permute-start = (f32[2,512,128]{2,1,0:T(8,128)}, f32[2,512,128]{2,1,0:T(8,128)S(1)}, u32[]{:S(2)}, u32[]{:S(2)}) collective-permute-start(f32[2,512,128]{2,1,0:T(8,128)} %get-tuple-element.89), channel_id=1, source_target_pairs={{0,4},{4,8},{8,12},{12,16},{16,20},{20,24},{24,28},{1,5},{5,9},{9,... | collective-permute-start | bytes 1572872 | tf_op jit(solution)/shard_map/ppermute | solution.py:409
  10.9 9.1 %collective-permute-done.1.right_ref = f32[2,512,128]{2,1,0:T(8,128)S(1)} collective-permute-done((f32[2,512,128]{2,1,0:T(8,128)}, f32[2,512,128]{2,1,0:T(8,128)S(1)}, u32[]{:S(2)}, u32[]{:S(2)}) %collective-permute-start.1) | collective-permute-done | bytes 524320 | tf_op jit(solution)/shard_map/ppermute | solution.py:409
  20.1 11.5 %collective-permute-done.left_ref = f32[2,512,128]{2,1,0:T(8,128)S(1)} collective-permute-done((f32[2,512,128]{2,1,0:T(8,128)}, f32[2,512,128]{2,1,0:T(8,128)S(1)}, u32[]{:S(2)}, u32[]{:S(2)}) %collective-permute-start) | collective-permute-done | bytes 524320 | tf_op jit(solution)/shard_map/ppermute | solution.py:409
  32.6 2.8 collective-permute-start.2
  39.4 2.7 fusion
  42.1 3.0 copy.13
  48.0 6.5 %shard_map.86.patch = f32[6,2,256,256]{3,2,1,0:T(8,128)} custom-call(s32[12]{0:T(128)S(1)} %reshape.263.offs, f32[2,512,512]{2,1,0:T(8,128)S(1)} %copy-done.2, f32[2,512,128]{2,1,0:T(8,128)S(1)} %copy-done.11, f32[2,512,128]{2,1,0:T(8,128)S(1)} %copy-done.9, f32[2,128,768]{2,1,0:T(8,128)} %collective-permute-done.2.top_ref, ...), custom_call_target="tpu_custom_call" | custom-call | flops 1000000 | bytes 8000000 | tf_op jit(solution)/shard_map/pallas_call | solution.py:138
  54.5 2.7 shard_map.87
  57.2 2.7 shard_map.88
  59.9 7.7 %shard_map.89 = (f32[1032,256]{1,0:T(8,128)S(1)}, f32[2,2,256,128]{3,2,1,0:T(8,128)S(1)}, f32[2,2,256,256]{3,2,1,0:T(8,128)S(1)}) custom-call(s32[1]{0:T(128)} %bitcast.95.counts_ref, bf16[4,2,256,256]{3,2,1,0:T(8,128)(2,1)S(1)} %copy-done, f32[6,2,256,256]{3,2,1,0:T(8,128)} %shard_map.86.patch, f32[1024,256]{1,0:T(8,128)S(1)} %pad_maximum_fusion.2.p, ...), custom_call_target="tpu_custom_call" | custom-call | flops 3221225472 | bytes 8000000 | tf_op jit(solution)/shard_map/pallas_call | solution.py:138
  67.6 2.7 collective-permute-start.4
  70.3 3.1 shard_map.90
  73.4 3.1 shard_map.91
  80.5 7.3 %collective-permute-done.10 = f32[256,256]{1,0:T(8,128)} collective-permute-done((f32[256,256]{1,0:T(8,128)}, f32[256,256]{1,0:T(8,128)}, u32[]{:S(2)}, u32[]{:S(2)}) %collective-permute-start.10) | collective-permute-done | bytes 262176 | tf_op jit(solution)/shard_map/ppermute | solution.py:464
  91.2 2.4 collective-permute-start.6
  93.6 3.3 collective-permute-done.6
  111.7 3.8 %collective-permute-done.12 = f32[128,256]{1,0:T(8,128)} collective-permute-done((f32[128,256]{1,0:T(8,128)}, f32[128,256]{1,0:T(8,128)}, u32[]{:S(2)}, u32[]{:S(2)}) %collective-permute-start.12) | collective-permute-done | bytes 131104 | tf_op jit(solution)/shard_map/ppermute | solution.py:481
  127.8 3.5 %collective-permute-done.14 = f32[128,256]{1,0:T(8,128)S(1)} collective-permute-done((f32[128,256]{1,0:T(8,128)S(1)}, f32[128,256]{1,0:T(8,128)S(1)}, u32[]{:S(2)}, u32[]{:S(2)}) %collective-permute-start.14) | collective-permute-done | bytes 131104 | tf_op jit(solution)/shard_map/ppermute | solution.py:491
  133.8 5.0 %collective-permute-done.17 = f32[256,256]{1,0:T(8,128)S(1)} collective-permute-done((f32[256,256]{1,0:T(8,128)S(1)}, f32[256,256]{1,0:T(8,128)S(1)}, u32[]{:S(2)}, u32[]{:S(2)}) %collective-permute-start.17) | collective-permute-done | bytes 262176 | tf_op jit(solution)/shard_map/ppermute | solution.py:497
  138.9 2.7 shard_map.92
  141.6 2.7 shard_map.93
  144.3 7.7 %shard_map.94 = (f32[1032,256]{1,0:T(8,128)S(1)}, f32[2,2,256,128]{3,2,1,0:T(8,128)S(1)}, f32[2,2,256,256]{3,2,1,0:T(8,128)S(1)}) custom-call(s32[1]{0:T(128)} %bitcast.100.counts_ref, bf16[4,2,256,256]{3,2,1,0:T(8,128)(2,1)S(1)} %copy-done, f32[6,2,256,256]{3,2,1,0:T(8,128)} %shard_map.86.patch, f32[1024,256]{1,0:T(8,128)S(1)} %pad_maximum_fusion.3.p, ...), custom_call_target="tpu_custom_call" | custom-call | flops 3221225472 | bytes 8000000 | tf_op jit(solution)/shard_map/pallas_call | solution.py:138
  152.6 3.1 shard_map.95
  155.7 3.1 shard_map.96
  161.9 7.2 %collective-permute-done.25 = f32[256,256]{1,0:T(8,128)S(1)} collective-permute-done((f32[256,256]{1,0:T(8,128)S(1)}, f32[256,256]{1,0:T(8,128)S(1)}, u32[]{:S(2)}, u32[]{:S(2)}) %collective-permute-start.25) | collective-permute-done | bytes 262176 | tf_op jit(solution)/shard_map/ppermute | solution.py:464
  170.4 4.0 %collective-permute-done.21 = f32[136,256]{1,0:T(8,128)S(1)} collective-permute-done((f32[136,256]{1,0:T(8,128)S(1)}, f32[136,256]{1,0:T(8,128)S(1)}, u32[]{:S(2)}, u32[]{:S(2)}) %collective-permute-start.21) | collective-permute-done | bytes 139296 | tf_op jit(solution)/shard_map/ppermute | solution.py:474
  175.7 3.9 %collective-permute-done.22 = f32[136,256]{1,0:T(8,128)S(1)} collective-permute-done((f32[136,256]{1,0:T(8,128)S(1)}, f32[136,256]{1,0:T(8,128)S(1)}, u32[]{:S(2)}, u32[]{:S(2)}) %collective-permute-start.22) | collective-permute-done | bytes 139296 | tf_op jit(solution)/shard_map/ppermute | solution.py:480
  181.7 3.6 %collective-permute-done.27 = f32[128,256]{1,0:T(8,128)S(1)} collective-permute-done((f32[128,256]{1,0:T(8,128)S(1)}, f32[128,256]{1,0:T(8,128)S(1)}, u32[]{:S(2)}, u32[]{:S(2)}) %collective-permute-start.27) | collective-permute-done | bytes 131104 | tf_op jit(solution)/shard_map/ppermute | solution.py:481
  194.6 2.4 collective-permute-start.29
  197.1 4.3 %collective-permute-done.29 = f32[128,256]{1,0:T(8,128)S(1)} collective-permute-done((f32[128,256]{1,0:T(8,128)S(1)}, f32[128,256]{1,0:T(8,128)S(1)}, u32[]{:S(2)}, u32[]{:S(2)}) %collective-permute-start.29) | collective-permute-done | bytes 131104 | tf_op jit(solution)/shard_map/ppermute | solution.py:491
  203.5 4.4 %collective-permute-done.32 = f32[256,256]{1,0:T(8,128)S(1)} collective-permute-done((f32[256,256]{1,0:T(8,128)S(1)}, f32[256,256]{1,0:T(8,128)S(1)}, u32[]{:S(2)}, u32[]{:S(2)}) %collective-permute-start.32) | collective-permute-done | bytes 262176 | tf_op jit(solution)/shard_map/ppermute | solution.py:497
  211.9 4.5 %shard_map.99 = (f32[1032,256]{1,0:T(8,128)S(1)}, f32[2,2,256,128]{3,2,1,0:T(8,128)S(1)}, f32[2,2,256,256]{3,2,1,0:T(8,128)S(1)}) custom-call(s32[1]{0:T(128)} %bitcast.105.counts_ref, bf16[4,2,256,256]{3,2,1,0:T(8,128)(2,1)S(1)} %copy-done, f32[6,2,256,256]{3,2,1,0:T(8,128)} %shard_map.86.patch, f32[1024,256]{1,0:T(8,128)S(1)} %pad_maximum_fusion.4.p, ...), custom_call_target="tpu_custom_call" | custom-call | flops 3221225472 | bytes 8000000 | tf_op jit(solution)/shard_map/pallas_call | solution.py:138
  228.4 3.9 %shard_map.103.rest_0_ = f32[2,768,768]{2,1,0:T(8,128)S(1)} custom-call(s32[12]{0:T(128)S(1)} %reshape.263.offs, s32[1]{0:T(128)} %bitcast.109.counts_ref, f32[2,2,256,256]{3,2,1,0:T(8,128)S(1)} %copy-done.15, f32[2,768,768]{2,1,0:T(8,128)} %copy-done.3), custom_call_target="tpu_custom_call" | custom-call | flops 1000000 | bytes 10000000 | tf_op jit(solution)/shard_map/pallas_call | solution.py:138
  234.5 3.6 %shard_map.104.g = f32[2,768,768]{2,1,0:T(8,128)S(1)} custom-call(s32[12]{0:T(128)S(1)} %reshape.263.offs, s32[1]{0:T(128)} %bitcast.110.counts_ref, f32[2,2,256,256]{3,2,1,0:T(8,128)S(1)} %get-tuple-element.69.patch_ref, f32[2,768,768]{2,1,0:T(8,128)} %copy-done.4), custom_call_target="tpu_custom_call" | custom-call | flops 1000000 | bytes 10000000 | tf_op jit(solution)/shard_map/pallas_call | solution.py:138
  238.2 3.6 %collective-permute-start.36 = (f32[136,256]{1,0:T(8,128)S(1)}, f32[136,256]{1,0:T(8,128)S(1)}, u32[]{:S(2)}, u32[]{:S(2)}) collective-permute-start(f32[136,256]{1,0:T(8,128)S(1)} %pad_maximum_fusion.19), channel_id=1, source_target_pairs={{0,4},{1,3},{2,6},{3,1},{4,0},{5,7},{6,2},{7,5},{8,12},{9,11},{10,... | collective-permute-start | bytes 417800 | tf_op jit(solution)/shard_map/ppermute | solution.py:474
  244.3 4.9 %collective-permute-start.50 = (f32[2,768,128]{2,1,0:T(8,128)S(1)}, f32[2,768,128]{2,1,0:T(8,128)S(1)}, u32[]{:S(2)}, u32[]{:S(2)}) collective-permute-start(f32[2,768,128]{2,1,0:T(8,128)S(1)} %get-tuple-element.78), channel_id=1, source_target_pairs={{0,4},{4,8},{8,12},{12,16},{16,20},{20,24},{24,28},{1,5},{5,9},{9,... | collective-permute-start | bytes 2359304 | tf_op jit(solution)/shard_map/ppermute | solution.py:409
  249.2 3.8 %collective-permute-start.41 = (f32[128,256]{1,0:T(8,128)S(1)}, f32[128,256]{1,0:T(8,128)S(1)}, u32[]{:S(2)}, u32[]{:S(2)}) collective-permute-start(f32[128,256]{1,0:T(8,128)S(1)} %dynamic-slice_bitcast_fusion.4), channel_id=1, source_target_pairs={{0,4},{1,3},{2,6},{3,1},{4,0},{5,7},{6,2},{7,5},{8,12},{9,11},{10,... | collective-permute-start | bytes 393224 | tf_op jit(solution)/shard_map/ppermute | solution.py:475
  255.4 29.6 %collective-permute-done.41 = f32[128,256]{1,0:T(8,128)S(1)} collective-permute-done((f32[128,256]{1,0:T(8,128)S(1)}, f32[128,256]{1,0:T(8,128)S(1)}, u32[]{:S(2)}, u32[]{:S(2)}) %collective-permute-start.41) | collective-permute-done | bytes 131104 | tf_op jit(solution)/shard_map/ppermute | solution.py:475
  285.2 2.6 collective-permute-start.38
  289.3 3.3 collective-permute-done.42
  297.5 2.6 collective-permute-start.39
  310.5 3.1 collective-permute-start.52
  316.8 2.6 fusion.18
  319.4 2.6 compare_and_fusion
  322.0 2.7 shard_map.105
  327.9 3.5 %multiply_subtract_fusion = f32[2,512,512]{2,1,0:T(8,128)} fusion(f32[2,512,512]{2,1,0:T(8,128)S(1)} %copy-done.2, f32[2,512,512]{2,1,0:T(8,128)} %copy-done.5, f32[]{:T(128)S(6)} %div.65), kind=kLoop, calls=%fused_computation.3 | loop fusion | flops 1048576 | bytes 6291460 | tf_op jit(solution)/shard_map/sub | solution.py:521
  333.6 3.2 broadcast_select_fusion
  (255 shorter events, 111.8 us)
Async XLA Ops:
  3.0 17.0 %collective-permute-start.1 = (f32[2,512,128]{2,1,0:T(8,128)}, f32[2,512,128]{2,1,0:T(8,128)S(1)}, u32[]{:S(2)}, u32[]{:S(2)}) collective-permute-start(f32[2,512,128]{2,1,0:T(8,128)} %get-tuple-element.88), channel_id=1, source_target_pairs={{4,0},{8,4},{12,8},{16,12},{20,16},{24,20},{28,24},{5,1},{9,5},{13... | collective-permute-start | bytes 1572872 | tf_op jit(solution)/shard_map/ppermute | solution.py:409
  4.3 27.2 %collective-permute-start = (f32[2,512,128]{2,1,0:T(8,128)}, f32[2,512,128]{2,1,0:T(8,128)S(1)}, u32[]{:S(2)}, u32[]{:S(2)}) collective-permute-start(f32[2,512,128]{2,1,0:T(8,128)} %get-tuple-element.89), channel_id=1, source_target_pairs={{0,4},{4,8},{8,12},{12,16},{16,20},{20,24},{24,28},{1,5},{5,9},{9,... | collective-permute-start | bytes 1572872 | tf_op jit(solution)/shard_map/ppermute | solution.py:409
  32.6 14.3 %collective-permute-start.2 = (f32[2,128,768]{2,1,0:T(8,128)}, f32[2,128,768]{2,1,0:T(8,128)}, u32[]{:S(2)}, u32[]{:S(2)}) collective-permute-start(f32[2,128,768]{2,1,0:T(8,128)} %pad_maximum_fusion.5), channel_id=1, source_target_pairs={{0,1},{1,2},{2,3},{4,5},{5,6},{6,7},{8,9},{9,10},{10,11},{12,13},{... | collective-permute-start | bytes 2359304 | tf_op jit(solution)/shard_map/ppermute | solution.py:409
  36.3 10.6 %collective-permute-start.3 = (f32[2,128,768]{2,1,0:T(8,128)}, f32[2,128,768]{2,1,0:T(8,128)}, u32[]{:S(2)}, u32[]{:S(2)}) collective-permute-start(f32[2,128,768]{2,1,0:T(8,128)} %pad_maximum_fusion.6), channel_id=1, source_target_pairs={{1,0},{2,1},{3,2},{5,4},{6,5},{7,6},{9,8},{10,9},{11,10},{13,12},{... | collective-permute-start | bytes 2359304 | tf_op jit(solution)/shard_map/ppermute | solution.py:409
  67.6 8.9 %collective-permute-start.4 = (f32[1032,256]{1,0:T(8,128)S(1)}, f32[1032,256]{1,0:T(8,128)S(1)}, u32[]{:S(2)}, u32[]{:S(2)}) collective-permute-start(f32[1032,256]{1,0:T(8,128)S(1)} %get-tuple-element.47), channel_id=1, source_target_pairs={{0,1},{1,0},{2,3},{3,2},{4,5},{5,4},{6,7},{7,6},{8,9},{9,8},{10,11... | collective-permute-start | bytes 3170312 | tf_op jit(solution)/shard_map/ppermute | solution.py:459
  78.4 9.4 %collective-permute-start.5 = (f32[264,256]{1,0:T(8,128)S(1)}, f32[264,256]{1,0:T(8,128)}, u32[]{:S(2)}, u32[]{:S(2)}) collective-permute-start(f32[264,256]{1,0:T(8,128)S(1)} %pad_maximum_fusion.10), channel_id=1, source_target_pairs={{0,2},{1,5},{2,0},{3,7},{4,6},{5,1},{6,4},{7,3},{8,10},{9,13},{10,... | collective-permute-start | bytes 811016 | tf_op jit(solution)/shard_map/ppermute | solution.py:463
  78.8 9.0 %collective-permute-start.10 = (f32[256,256]{1,0:T(8,128)}, f32[256,256]{1,0:T(8,128)}, u32[]{:S(2)}, u32[]{:S(2)}) collective-permute-start(f32[256,256]{1,0:T(8,128)} %get-tuple-element.112), channel_id=1, source_target_pairs={{0,2},{1,5},{2,0},{3,7},{4,6},{5,1},{6,4},{7,3},{8,10},{9,13},{10,... | collective-permute-start | bytes 786440 | tf_op jit(solution)/shard_map/ppermute | solution.py:464
  91.2 5.7 %collective-permute-start.6 = (f32[136,256]{1,0:T(8,128)}, f32[136,256]{1,0:T(8,128)}, u32[]{:S(2)}, u32[]{:S(2)}) collective-permute-start(f32[136,256]{1,0:T(8,128)} %pad_maximum_fusion.13), channel_id=1, source_target_pairs={{0,4},{1,3},{2,6},{3,1},{4,0},{5,7},{6,2},{7,5},{8,12},{9,11},{10,... | collective-permute-start | bytes 417800 | tf_op jit(solution)/shard_map/ppermute | solution.py:474
  98.7 5.5 %collective-permute-start.7 = (f32[136,256]{1,0:T(8,128)S(1)}, f32[136,256]{1,0:T(8,128)S(1)}, u32[]{:S(2)}, u32[]{:S(2)}) collective-permute-start(f32[136,256]{1,0:T(8,128)S(1)} %pad_maximum_fusion.14), channel_id=1, source_target_pairs={{0,8},{1,17},{2,10},{3,19},{4,12},{5,21},{6,14},{7,23},{8,0},{9,25... | collective-permute-start | bytes 417800 | tf_op jit(solution)/shard_map/ppermute | solution.py:480
  100.3 6.8 %collective-permute-start.11 = (f32[128,256]{1,0:T(8,128)S(1)}, f32[128,256]{1,0:T(8,128)S(1)}, u32[]{:S(2)}, u32[]{:S(2)}) collective-permute-start(f32[128,256]{1,0:T(8,128)S(1)} %dynamic-slice_bitcast_fusion.8), channel_id=1, source_target_pairs={{0,4},{1,3},{2,6},{3,1},{4,0},{5,7},{6,2},{7,5},{8,12},{9,11},{10,... | collective-permute-start | bytes 393224 | tf_op jit(solution)/shard_map/ppermute | solution.py:475
  104.9 12.3 %collective-permute-start.8 = (f32[136,256]{1,0:T(8,128)}, f32[136,256]{1,0:T(8,128)}, u32[]{:S(2)}, u32[]{:S(2)}) collective-permute-start(f32[136,256]{1,0:T(8,128)} %pad_maximum_fusion.15), channel_id=1, source_target_pairs={{0,16},{1,9},{2,18},{3,11},{4,20},{5,13},{6,22},{7,15},{8,24},{9,1... | collective-permute-start | bytes 417800 | tf_op jit(solution)/shard_map/ppermute | solution.py:480
  107.8 7.7 %collective-permute-start.12 = (f32[128,256]{1,0:T(8,128)}, f32[128,256]{1,0:T(8,128)}, u32[]{:S(2)}, u32[]{:S(2)}) collective-permute-start(f32[128,256]{1,0:T(8,128)} %bitcast_add_fusion.2), channel_id=1, source_target_pairs={{0,8},{1,17},{2,10},{3,19},{4,12},{5,21},{6,14},{7,23},{8,0},{9,25... | collective-permute-start | bytes 393224 | tf_op jit(solution)/shard_map/ppermute | solution.py:481
  117.1 6.8 %collective-permute-start.13 = (f32[128,256]{1,0:T(8,128)}, f32[128,256]{1,0:T(8,128)}, u32[]{:S(2)}, u32[]{:S(2)}) collective-permute-start(f32[128,256]{1,0:T(8,128)} %add.260), channel_id=1, source_target_pairs={{0,16},{1,9},{2,18},{3,11},{4,20},{5,13},{6,22},{7,15},{8,24},{9,1... | collective-permute-start | bytes 393224 | tf_op jit(solution)/shard_map/ppermute | solution.py:481
  120.9 5.3 %collective-permute-start.9 = (f32[128,256]{1,0:T(8,128)}, f32[128,256]{1,0:T(8,128)}, u32[]{:S(2)}, u32[]{:S(2)}) collective-permute-start(f32[128,256]{1,0:T(8,128)} %fusion.14), channel_id=1, source_target_pairs={{0,4},{1,3},{2,6},{3,1},{4,0},{5,7},{6,2},{7,5},{8,12},{9,11},{10,... | collective-permute-start | bytes 393224 | tf_op jit(solution)/shard_map/ppermute | solution.py:490
  125.0 6.4 %collective-permute-start.14 = (f32[128,256]{1,0:T(8,128)S(1)}, f32[128,256]{1,0:T(8,128)S(1)}, u32[]{:S(2)}, u32[]{:S(2)}) collective-permute-start(f32[128,256]{1,0:T(8,128)S(1)} %bitcast_subtract_fusion.2), channel_id=1, source_target_pairs={{0,4},{1,3},{2,6},{3,1},{4,0},{5,7},{6,2},{7,5},{8,12},{9,11},{10,... | collective-permute-start | bytes 393224 | tf_op jit(solution)/shard_map/ppermute | solution.py:491
  127.4 6.4 %collective-permute-start.16 = (f32[256,256]{1,0:T(8,128)S(1)}, f32[256,256]{1,0:T(8,128)S(1)}, u32[]{:S(2)}, u32[]{:S(2)}) collective-permute-start(f32[256,256]{1,0:T(8,128)S(1)} %maximum_select_fusion), channel_id=1, source_target_pairs={{0,2},{1,5},{2,0},{3,7},{4,6},{5,1},{6,4},{7,3},{8,10},{9,13},{10,... | collective-permute-start | bytes 786440 | tf_op jit(solution)/shard_map/ppermute | solution.py:497
  132.3 6.4 %collective-permute-start.17 = (f32[256,256]{1,0:T(8,128)S(1)}, f32[256,256]{1,0:T(8,128)S(1)}, u32[]{:S(2)}, u32[]{:S(2)}) collective-permute-start(f32[256,256]{1,0:T(8,128)S(1)} %maximum_select_fusion.1), channel_id=1, source_target_pairs={{0,2},{1,5},{2,0},{3,7},{4,6},{5,1},{6,4},{7,3},{8,10},{9,13},{10,... | collective-permute-start | bytes 786440 | tf_op jit(solution)/shard_map/ppermute | solution.py:497
  133.1 11.1 %collective-permute-start.15 = (f32[512,256]{1,0:T(8,128)S(1)}, f32[512,256]{1,0:T(8,128)S(1)}, u32[]{:S(2)}, u32[]{:S(2)}) collective-permute-start(f32[512,256]{1,0:T(8,128)S(1)} %pad_maximum_fusion.7.p), channel_id=1, source_target_pairs={{0,1},{1,0},{2,3},{3,2},{4,5},{5,4},{6,7},{7,6},{8,9},{9,8},{10,11... | collective-permute-start | bytes 1572872 | tf_op jit(solution)/shard_map/ppermute | solution.py:499
  138.8 5.5 %collective-permute-start.18 = (f32[512,256]{1,0:T(8,128)S(1)}, f32[512,256]{1,0:T(8,128)S(1)}, u32[]{:S(2)}, u32[]{:S(2)}) collective-permute-start(f32[512,256]{1,0:T(8,128)S(1)} %constant_dynamic-update-slice_fusion.p), channel_id=1, source_target_pairs={{0,1},{1,0},{2,3},{3,2},{4,5},{5,4},{6,7},{7,6},{8,9},{9,8},{10,11... | collective-permute-start | bytes 1572872 | tf_op jit(solution)/shard_map/ppermute | solution.py:501
  152.1 6.7 %collective-permute-start.19 = (f32[1032,256]{1,0:T(8,128)S(1)}, f32[1032,256]{1,0:T(8,128)S(1)}, u32[]{:S(2)}, u32[]{:S(2)}) collective-permute-start(f32[1032,256]{1,0:T(8,128)S(1)} %get-tuple-element.57), channel_id=1, source_target_pairs={{0,1},{1,0},{2,3},{3,2},{4,5},{5,4},{6,7},{7,6},{8,9},{9,8},{10,11... | collective-permute-start | bytes 3170312 | tf_op jit(solution)/shard_map/ppermute | solution.py:459
  159.8 9.3 %collective-permute-start.20 = (f32[264,256]{1,0:T(8,128)S(1)}, f32[264,256]{1,0:T(8,128)S(1)}, u32[]{:S(2)}, u32[]{:S(2)}) collective-permute-start(f32[264,256]{1,0:T(8,128)S(1)} %pad_maximum_fusion.11), channel_id=1, source_target_pairs={{0,2},{1,5},{2,0},{3,7},{4,6},{5,1},{6,4},{7,3},{8,10},{9,13},{10,... | collective-permute-start | bytes 811016 | tf_op jit(solution)/shard_map/ppermute | solution.py:463
  159.9 9.3 %collective-permute-start.25 = (f32[256,256]{1,0:T(8,128)S(1)}, f32[256,256]{1,0:T(8,128)S(1)}, u32[]{:S(2)}, u32[]{:S(2)}) collective-permute-start(f32[256,256]{1,0:T(8,128)S(1)} %get-tuple-element.109), channel_id=1, source_target_pairs={{0,2},{1,5},{2,0},{3,7},{4,6},{5,1},{6,4},{7,3},{8,10},{9,13},{10,... | collective-permute-start | bytes 786440 | tf_op jit(solution)/shard_map/ppermute | solution.py:464
  174.6 5.7 %collective-permute-start.26 = (f32[128,256]{1,0:T(8,128)S(1)}, f32[128,256]{1,0:T(8,128)S(1)}, u32[]{:S(2)}, u32[]{:S(2)}) collective-permute-start(f32[128,256]{1,0:T(8,128)S(1)} %dynamic-slice_bitcast_fusion.6), channel_id=1, source_target_pairs={{0,4},{1,3},{2,6},{3,1},{4,0},{5,7},{6,2},{7,5},{8,12},{9,11},{10,... | collective-permute-start | bytes 393224 | tf_op jit(solution)/shard_map/ppermute | solution.py:475
  179.6 8.7 %collective-permute-start.23 = (f32[136,256]{1,0:T(8,128)S(1)}, f32[136,256]{1,0:T(8,128)S(1)}, u32[]{:S(2)}, u32[]{:S(2)}) collective-permute-start(f32[136,256]{1,0:T(8,128)S(1)} %pad_maximum_fusion.18), channel_id=1, source_target_pairs={{0,16},{1,9},{2,18},{3,11},{4,20},{5,13},{6,22},{7,15},{8,24},{9,1... | collective-permute-start | bytes 417800 | tf_op jit(solution)/shard_map/ppermute | solution.py:480
  186.0 7.6 %collective-permute-start.28 = (f32[128,256]{1,0:T(8,128)}, f32[128,256]{1,0:T(8,128)}, u32[]{:S(2)}, u32[]{:S(2)}) collective-permute-start(f32[128,256]{1,0:T(8,128)} %add.275), channel_id=1, source_target_pairs={{0,16},{1,9},{2,18},{3,11},{4,20},{5,13},{6,22},{7,15},{8,24},{9,1... | collective-permute-start | bytes 393224 | tf_op jit(solution)/shard_map/ppermute | solution.py:481
  191.2 5.8 %collective-permute-start.24 = (f32[128,256]{1,0:T(8,128)S(1)}, f32[128,256]{1,0:T(8,128)S(1)}, u32[]{:S(2)}, u32[]{:S(2)}) collective-permute-start(f32[128,256]{1,0:T(8,128)S(1)} %fusion.12), channel_id=1, source_target_pairs={{0,4},{1,3},{2,6},{3,1},{4,0},{5,7},{6,2},{7,5},{8,12},{9,11},{10,... | collective-permute-start | bytes 393224 | tf_op jit(solution)/shard_map/ppermute | solution.py:490
  194.6 6.8 %collective-permute-start.29 = (f32[128,256]{1,0:T(8,128)S(1)}, f32[128,256]{1,0:T(8,128)S(1)}, u32[]{:S(2)}, u32[]{:S(2)}) collective-permute-start(f32[128,256]{1,0:T(8,128)S(1)} %bitcast_subtract_fusion.1), channel_id=1, source_target_pairs={{0,4},{1,3},{2,6},{3,1},{4,0},{5,7},{6,2},{7,5},{8,12},{9,11},{10,... | collective-permute-start | bytes 393224 | tf_op jit(solution)/shard_map/ppermute | solution.py:491
  197.0 6.4 %collective-permute-start.31 = (f32[256,256]{1,0:T(8,128)S(1)}, f32[256,256]{1,0:T(8,128)S(1)}, u32[]{:S(2)}, u32[]{:S(2)}) collective-permute-start(f32[256,256]{1,0:T(8,128)S(1)} %maximum_select_fusion.2), channel_id=1, source_target_pairs={{0,2},{1,5},{2,0},{3,7},{4,6},{5,1},{6,4},{7,3},{8,10},{9,13},{10,... | collective-permute-start | bytes 786440 | tf_op jit(solution)/shard_map/ppermute | solution.py:497
  201.4 6.4 %collective-permute-start.32 = (f32[256,256]{1,0:T(8,128)S(1)}, f32[256,256]{1,0:T(8,128)S(1)}, u32[]{:S(2)}, u32[]{:S(2)}) collective-permute-start(f32[256,256]{1,0:T(8,128)S(1)} %maximum_select_fusion.3), channel_id=1, source_target_pairs={{0,2},{1,5},{2,0},{3,7},{4,6},{5,1},{6,4},{7,3},{8,10},{9,13},{10,... | collective-permute-start | bytes 786440 | tf_op jit(solution)/shard_map/ppermute | solution.py:497
  201.5 10.2 %collective-permute-start.30 = (f32[512,256]{1,0:T(8,128)S(1)}, f32[512,256]{1,0:T(8,128)S(1)}, u32[]{:S(2)}, u32[]{:S(2)}) collective-permute-start(f32[512,256]{1,0:T(8,128)S(1)} %pad_maximum_fusion.8.p), channel_id=1, source_target_pairs={{0,1},{1,0},{2,3},{3,2},{4,5},{5,4},{6,7},{7,6},{8,9},{9,8},{10,11... | collective-permute-start | bytes 1572872 | tf_op jit(solution)/shard_map/ppermute | solution.py:499
  221.0 17.1 %collective-permute-start.35 = (f32[264,256]{1,0:T(8,128)S(1)}, f32[264,256]{1,0:T(8,128)S(1)}, u32[]{:S(2)}, u32[]{:S(2)}) collective-permute-start(f32[264,256]{1,0:T(8,128)S(1)} %pad_maximum_fusion.12), channel_id=1, source_target_pairs={{0,2},{1,5},{2,0},{3,7},{4,6},{5,1},{6,4},{7,3},{8,10},{9,13},{10,... | collective-permute-start | bytes 811016 | tf_op jit(solution)/shard_map/ppermute | solution.py:463
  221.1 17.0 %collective-permute-start.40 = (f32[256,256]{1,0:T(8,128)S(1)}, f32[256,256]{1,0:T(8,128)S(1)}, u32[]{:S(2)}, u32[]{:S(2)}) collective-permute-start(f32[256,256]{1,0:T(8,128)S(1)} %get-tuple-element.104), channel_id=1, source_target_pairs={{0,2},{1,5},{2,0},{3,7},{4,6},{5,1},{6,4},{7,3},{8,10},{9,13},{10,... | collective-permute-start | bytes 786440 | tf_op jit(solution)/shard_map/ppermute | solution.py:464
  238.2 14.8 %collective-permute-start.36 = (f32[136,256]{1,0:T(8,128)S(1)}, f32[136,256]{1,0:T(8,128)S(1)}, u32[]{:S(2)}, u32[]{:S(2)}) collective-permute-start(f32[136,256]{1,0:T(8,128)S(1)} %pad_maximum_fusion.19), channel_id=1, source_target_pairs={{0,4},{1,3},{2,6},{3,1},{4,0},{5,7},{6,2},{7,5},{8,12},{9,11},{10,... | collective-permute-start | bytes 417800 | tf_op jit(solution)/shard_map/ppermute | solution.py:474
  242.8 60.6 %collective-permute-start.49 = (f32[2,768,128]{2,1,0:T(8,128)}, f32[2,768,128]{2,1,0:T(8,128)S(1)}, u32[]{:S(2)}, u32[]{:S(2)}) collective-permute-start(f32[2,768,128]{2,1,0:T(8,128)} %get-tuple-element.79), channel_id=1, source_target_pairs={{4,0},{8,4},{12,8},{16,12},{20,16},{24,20},{28,24},{5,1},{9,5},{13... | collective-permute-start | bytes 2359304 | tf_op jit(solution)/shard_map/ppermute | solution.py:409
  244.3 43.5 %collective-permute-start.50 = (f32[2,768,128]{2,1,0:T(8,128)S(1)}, f32[2,768,128]{2,1,0:T(8,128)S(1)}, u32[]{:S(2)}, u32[]{:S(2)}) collective-permute-start(f32[2,768,128]{2,1,0:T(8,128)S(1)} %get-tuple-element.78), channel_id=1, source_target_pairs={{0,4},{4,8},{8,12},{12,16},{16,20},{20,24},{24,28},{1,5},{5,9},{9,... | collective-permute-start | bytes 2359304 | tf_op jit(solution)/shard_map/ppermute | solution.py:409
  249.2 35.8 %collective-permute-start.41 = (f32[128,256]{1,0:T(8,128)S(1)}, f32[128,256]{1,0:T(8,128)S(1)}, u32[]{:S(2)}, u32[]{:S(2)}) collective-permute-start(f32[128,256]{1,0:T(8,128)S(1)} %dynamic-slice_bitcast_fusion.4), channel_id=1, source_target_pairs={{0,4},{1,3},{2,6},{3,1},{4,0},{5,7},{6,2},{7,5},{8,12},{9,11},{10,... | collective-permute-start | bytes 393224 | tf_op jit(solution)/shard_map/ppermute | solution.py:475
  253.1 32.0 %collective-permute-start.37 = (f32[136,256]{1,0:T(8,128)S(1)}, f32[136,256]{1,0:T(8,128)S(1)}, u32[]{:S(2)}, u32[]{:S(2)}) collective-permute-start(f32[136,256]{1,0:T(8,128)S(1)} %pad_maximum_fusion.20), channel_id=1, source_target_pairs={{0,8},{1,17},{2,10},{3,19},{4,12},{5,21},{6,14},{7,23},{8,0},{9,25... | collective-permute-start | bytes 417800 | tf_op jit(solution)/shard_map/ppermute | solution.py:480
  285.0 7.6 %collective-permute-start.42 = (f32[128,256]{1,0:T(8,128)S(1)}, f32[128,256]{1,0:T(8,128)S(1)}, u32[]{:S(2)}, u32[]{:S(2)}) collective-permute-start(f32[128,256]{1,0:T(8,128)S(1)} %bitcast_add_fusion), channel_id=1, source_target_pairs={{0,8},{1,17},{2,10},{3,19},{4,12},{5,21},{6,14},{7,23},{8,0},{9,25... | collective-permute-start | bytes 393224 | tf_op jit(solution)/shard_map/ppermute | solution.py:481
  285.2 9.4 %collective-permute-start.38 = (f32[136,256]{1,0:T(8,128)S(1)}, f32[136,256]{1,0:T(8,128)S(1)}, u32[]{:S(2)}, u32[]{:S(2)}) collective-permute-start(f32[136,256]{1,0:T(8,128)S(1)} %pad_maximum_fusion.21), channel_id=1, source_target_pairs={{0,16},{1,9},{2,18},{3,11},{4,20},{5,13},{6,22},{7,15},{8,24},{9,1... | collective-permute-start | bytes 417800 | tf_op jit(solution)/shard_map/ppermute | solution.py:480
  293.3 6.8 %collective-permute-start.43 = (f32[128,256]{1,0:T(8,128)}, f32[128,256]{1,0:T(8,128)}, u32[]{:S(2)}, u32[]{:S(2)}) collective-permute-start(f32[128,256]{1,0:T(8,128)} %add.290), channel_id=1, source_target_pairs={{0,16},{1,9},{2,18},{3,11},{4,20},{5,13},{6,22},{7,15},{8,24},{9,1... | collective-permute-start | bytes 393224 | tf_op jit(solution)/shard_map/ppermute | solution.py:481
  297.5 6.8 %collective-permute-start.39 = (f32[128,256]{1,0:T(8,128)S(1)}, f32[128,256]{1,0:T(8,128)S(1)}, u32[]{:S(2)}, u32[]{:S(2)}) collective-permute-start(f32[128,256]{1,0:T(8,128)S(1)} %fusion.10), channel_id=1, source_target_pairs={{0,4},{1,3},{2,6},{3,1},{4,0},{5,7},{6,2},{7,5},{8,12},{9,11},{10,... | collective-permute-start | bytes 393224 | tf_op jit(solution)/shard_map/ppermute | solution.py:490
  301.1 5.7 %collective-permute-start.44 = (f32[128,256]{1,0:T(8,128)S(1)}, f32[128,256]{1,0:T(8,128)S(1)}, u32[]{:S(2)}, u32[]{:S(2)}) collective-permute-start(f32[128,256]{1,0:T(8,128)S(1)} %bitcast_subtract_fusion), channel_id=1, source_target_pairs={{0,4},{1,3},{2,6},{3,1},{4,0},{5,7},{6,2},{7,5},{8,12},{9,11},{10,... | collective-permute-start | bytes 393224 | tf_op jit(solution)/shard_map/ppermute | solution.py:491
  304.4 10.8 %collective-permute-start.45 = (f32[256,256]{1,0:T(8,128)S(1)}, f32[256,256]{1,0:T(8,128)S(1)}, u32[]{:S(2)}, u32[]{:S(2)}) collective-permute-start(f32[256,256]{1,0:T(8,128)S(1)} %maximum_select_fusion.4), channel_id=1, source_target_pairs={{0,2},{1,5},{2,0},{3,7},{4,6},{5,1},{6,4},{7,3},{8,10},{9,13},{10,... | collective-permute-start | bytes 786440 | tf_op jit(solution)/shard_map/ppermute | solution.py:497
  306.8 8.4 %collective-permute-start.46 = (f32[256,256]{1,0:T(8,128)S(1)}, f32[256,256]{1,0:T(8,128)S(1)}, u32[]{:S(2)}, u32[]{:S(2)}) collective-permute-start(f32[256,256]{1,0:T(8,128)S(1)} %maximum_select_fusion.5), channel_id=1, source_target_pairs={{0,2},{1,5},{2,0},{3,7},{4,6},{5,1},{6,4},{7,3},{8,10},{9,13},{10,... | collective-permute-start | bytes 786440 | tf_op jit(solution)/shard_map/ppermute | solution.py:497
  309.2 12.8 %collective-permute-start.51 = (f32[2,128,512]{2,1,0:T(8,128)S(1)}, f32[2,128,512]{2,1,0:T(8,128)S(1)}, u32[]{:S(2)}, u32[]{:S(2)}) collective-permute-start(f32[2,128,512]{2,1,0:T(8,128)S(1)} %get-tuple-element.77), channel_id=1, source_target_pairs={{1,0},{2,1},{3,2},{5,4},{6,5},{7,6},{9,8},{10,9},{11,10},{13,12},{... | collective-permute-start | bytes 1572872 | tf_op jit(solution)/shard_map/ppermute | solution.py:409
  310.5 11.5 %collective-permute-start.52 = (f32[2,128,512]{2,1,0:T(8,128)S(1)}, f32[2,128,512]{2,1,0:T(8,128)S(1)}, u32[]{:S(2)}, u32[]{:S(2)}) collective-permute-start(f32[2,128,512]{2,1,0:T(8,128)S(1)} %get-tuple-element.76), channel_id=1, source_target_pairs={{0,1},{1,2},{2,3},{4,5},{5,6},{6,7},{8,9},{9,10},{10,11},{12,13},{... | collective-permute-start | bytes 1572872 | tf_op jit(solution)/shard_map/ppermute | solution.py:409
  314.4 10.3 %collective-permute-start.47 = (f32[512,256]{1,0:T(8,128)S(1)}, f32[512,256]{1,0:T(8,128)S(1)}, u32[]{:S(2)}, u32[]{:S(2)}) collective-permute-start(f32[512,256]{1,0:T(8,128)S(1)} %get-tuple-element.101), channel_id=1, source_target_pairs={{0,1},{1,0},{2,3},{3,2},{4,5},{5,4},{6,7},{7,6},{8,9},{9,8},{10,11... | collective-permute-start | bytes 1572872 | tf_op jit(solution)/shard_map/ppermute | solution.py:499
  315.2 9.5 %collective-permute-start.48 = (f32[512,256]{1,0:T(8,128)S(1)}, f32[512,256]{1,0:T(8,128)S(1)}, u32[]{:S(2)}, u32[]{:S(2)}) collective-permute-start(f32[512,256]{1,0:T(8,128)S(1)} %constant_dynamic-update-slice_fusion.4), channel_id=1, source_target_pairs={{0,1},{1,0},{2,3},{3,2},{4,5},{5,4},{6,7},{7,6},{8,9},{9,8},{10,11... | collective-permute-start | bytes 1572872 | tf_op jit(solution)/shard_map/ppermute | solution.py:501
  (39 other events, 272.6 us)

commit v2 on v1

v2 whole, which is shorter than its diff:
```python
import functools

import jax
import jax.numpy as jnp
import ml_dtypes
import numpy as np
from jax import lax
from jax.experimental import pallas as pl
from jax.experimental.pallas import tpu as pltpu
from jax.sharding import PartitionSpec as P

H = 128
BATCHES = 3
POS = 2
AXES = ("wide", "narrow")
F32 = jnp.float32
BF16 = jnp.bfloat16
VMEM_LIMIT = 48 * 1024 * 1024


def halves(table):
    high = table.astype(ml_dtypes.bfloat16)
    low = (table - high.astype(np.float64)).astype(ml_dtypes.bfloat16)
    return np.stack([high, low])


def dft_tables(size):
    half = size // 2
    k = np.arange(half)
    out = []
    for odd in range(2):
        phase = ((2 * k[:, None] + odd) * k[None, :]) % size
        angle = -2.0 * np.pi * phase / size
        re, im = np.cos(angle) / np.sqrt(size), np.sin(angle) / np.sqrt(size)
        out.append(np.block([[re, -im], [im, re]]))
    return np.stack([halves(t) for t in (out[0], out[1], out[0].T, out[1].T)])


def split(x):
    high = x.astype(BF16)
    return high, (x - high.astype(F32)).astype(BF16)


def dot(a, b):
    return jnp.dot(a, b, preferred_element_type=F32)


def left(tables, which, x):
    high, low = split(x)
    t_high, t_low = tables[which, 0], tables[which, 1]
    return dot(t_high, high) + dot(t_high, low) + dot(t_low, high)


def right(x, tables, which):
    high, low = split(x)
    t_high, t_low = tables[which, 0], tables[which, 1]
    return dot(high, t_high) + dot(low, t_high) + dot(high, t_low)


def forward(tables, re, im):
    h = re.shape[0] // 2
    u = jnp.concatenate([re[:h] + re[h:], im[:h] + im[h:]], 0)
    v = jnp.concatenate([re[:h] - re[h:], im[:h] - im[h:]], 0)
    even, odd = left(tables, 0, u), left(tables, 1, v)

    def columns(op):
        rows = [jnp.concatenate([op(y[:h, :h], y[:h, h:]), op(y[h:, :h], y[h:, h:])], 1) for y in (even, odd)]
        return jnp.concatenate(rows, 0)

    return (
        right(columns(lambda a, b: a + b), tables, 2),
        right(columns(lambda a, b: a - b), tables, 3),
    )


def inverse(tables, even, odd):
    h = even.shape[0] // 2
    a, b = right(even, tables, 0), right(odd, tables, 1)
    s, d = a + b, a - b

    def rows(lo):
        return jnp.concatenate(
            [
                jnp.concatenate([s[lo : lo + h, :h], d[lo : lo + h, :h]], 1),
                jnp.concatenate([s[lo : lo + h, h:], d[lo : lo + h, h:]], 1),
            ],
            0,
        )

    a, b = left(tables, 2, rows(0)), left(tables, 3, rows(h))
    s, d = a + b, a - b
    return jnp.concatenate([s[:h], d[:h]], 0), jnp.concatenate([s[h:], d[h:]], 0)


def power_of(z):
    h = z.shape[-1] // 2
    return z[:, :h] * z[:, :h] + z[:, h:] * z[:, h:]


def place_of(which, bit, h):
    return pl.multiple_of(jnp.where(bit == which, 0, h), h)


def rows_of(ref, bit):
    h = ref.shape[0] // 2
    return jnp.concatenate([ref[pl.ds(place_of(which, bit, h), h)] for which in range(2)], 0)


def add_rows(ref, base, bit, value):
    h = value.shape[0] // 2
    for which in range(2):
        ref[pl.ds(base + place_of(which, bit, h), h)] += value[which * h : (which + 1) * h]


def illuminated(tables, patch, probe):
    (p_re, p_im), (o_re, o_im) = probe, (patch[0, 0], patch[0, 1])
    return forward(tables, p_re * o_re - p_im * o_im, p_re * o_im + p_im * o_re)


def gradients(tables, patch, probe, spectrum, keep, pgrad, base, bit, gpatch):
    size = patch.shape[-1]
    k_even, k_odd = keep[0, 0], keep[0, 1]
    b_re, b_im = inverse(
        tables,
        spectrum[0] * jnp.concatenate([k_even, k_even], 1),
        spectrum[1] * jnp.concatenate([k_odd, k_odd], 1),
    )
    (p_re, p_im), (o_re, o_im) = probe, (patch[0, 0], patch[0, 1])
    gpatch[0, 0] += p_re * b_re + p_im * b_im
    gpatch[0, 1] += p_re * b_im - p_im * b_re
    add_rows(pgrad, base, bit, o_re * b_re + o_im * b_im)
    add_rows(pgrad, base + size, bit, o_re * b_im - o_im * b_re)


def whole(*shape):
    return pl.BlockSpec(shape, lambda i, *_: (0,) * len(shape))


def per_slot(*shape):
    return pl.BlockSpec((1, *shape), lambda i, *_: (i,) + (0,) * len(shape))


def per_batch_slot(batch, *shape):
    return pl.BlockSpec((1, *shape), lambda i, *_: (batch * POS + i,) + (0,) * len(shape))


def call(body, scalars, operands, in_specs, out_shapes, out_specs, grid, scratch=(), aliases=None, flops=0, moved=0):
    return pl.pallas_call(
        body,
        out_shape=[jax.ShapeDtypeStruct(s, F32) for s in out_shapes],
        grid_spec=pltpu.PrefetchScalarGridSpec(
            num_scalar_prefetch=len(scalars),
            grid=(grid,),
            in_specs=in_specs,
            out_specs=out_specs,
            scratch_shapes=list(scratch),
        ),
        input_output_aliases=aliases or {},
        compiler_params=pltpu.CompilerParams(vmem_limit_bytes=VMEM_LIMIT),
        cost_estimate=pl.CostEstimate(flops=flops, bytes_accessed=moved, transcendentals=0),
    )(*scalars, *operands)


def corner_of(offs, slot, full, size):
    row = offs[2 * slot] + H
    col = offs[2 * slot + 1] + H
    row_at = pl.multiple_of(jnp.minimum(row // 8 * 8, full - size - 8), 8)
    col_at = pl.multiple_of(jnp.minimum(col // 128 * 128, full - size - 128), 128)
    return row_at, col_at, row - row_at, col - col_at


def cut_patches(offsets, info, tile, sides, size, slots):
    edge = tile.shape[1]
    full = edge + 2 * H

    def body(offs, info_ref, tile_ref, left_ref, right_ref, top_ref, bottom_ref, out, cover, ext):
        i = pl.program_id(0)

        @pl.when(i == 0)
        def _():
            cover[...] = jnp.zeros_like(cover)
            ext[:, :H] = top_ref[...]
            ext[:, H + edge :] = bottom_ref[...]
            ext[:, H : H + edge, :H] = left_ref[...]
            ext[:, H : H + edge, H : H + edge] = tile_ref[...]
            ext[:, H : H + edge, H + edge :] = right_ref[...]

        @pl.when(i < info_ref[0])
        def _():
            row_at, col_at, row, col = corner_of(offs, i, full, size)
            total = jnp.zeros((1, size), F32)
            for part in range(2):
                block = ext[part, pl.ds(row_at, size + 8), pl.ds(col_at, size + 128)]
                block = pltpu.roll(block, size + 128 - col, 1)[:, :size]
                block = pltpu.roll(block, size + 8 - row, 0)[:size]
                out[0, part] = block
                total = total + jnp.sum(block * block, axis=0, keepdims=True)
            here = lax.broadcasted_iota(jnp.int32, cover.shape, 0) == i // POS
            cover[...] += jnp.where(here, total, 0.0)

    return call(
        body,
        [offsets, info],
        [tile, *sides],
        [whole(2, edge, edge), whole(2, edge, H), whole(2, edge, H), whole(2, H, full), whole(2, H, full)],
        [(slots, 2, size, size), (8, size)],
        [per_slot(2, size, size), whole(8, size)],
        slots,
        scratch=[pltpu.VMEM((2, full, full), F32)],
        flops=10**6,
        moved=8 * 10**6,
    )


def place_gradients(offsets, info, patches, after, edge):
    size = patches[0].shape[-1]
    full = edge + 2 * H
    n = len(patches)

    def body(offs, info_ref, *refs):
        patch_refs, (core, upper, lower, left_part, right_part, ext) = refs[:n], refs[n + len(after) :]
        i = pl.program_id(0)

        @pl.when(i == 0)
        def _():
            ext[...] = jnp.zeros_like(ext)

        for batch in range(n):

            @pl.when((i // POS == batch) & (i < info_ref[0]))
            def _():
                row_at, col_at, row, col = corner_of(offs, i, full, size)
                for part in range(2):
                    block = patch_refs[batch][0, part]
                    block = jnp.concatenate([block, jnp.zeros((8, size), F32)], 0)
                    block = pltpu.roll(block, row, 0)
                    block = jnp.concatenate([block, jnp.zeros((size + 8, 128), F32)], 1)
                    block = pltpu.roll(block, col, 1)
                    ext[part, pl.ds(row_at, size + 8), pl.ds(col_at, size + 128)] += block

        @pl.when(i == n * POS - 1)
        def _():
            core[...] = ext[:, H : H + edge, H : H + edge]
            upper[...] = ext[:, :H]
            lower[...] = ext[:, H + edge :]
            left_part[...] = ext[:, H : H + edge, :H]
            right_part[...] = ext[:, H : H + edge, H + edge :]

    def spec(batch):
        return pl.BlockSpec((1, 2, size, size), lambda i, *_: (jnp.clip(i - batch * POS, 0, POS - 1), 0, 0, 0))

    shapes = [(2, edge, edge), (2, H, full), (2, H, full), (2, edge, H), (2, edge, H)]
    return call(
        body,
        [offsets, info],
        [*patches, *after],
        [spec(batch) for batch in range(n)] + [pl.BlockSpec(memory_space=pl.ANY)] * len(after),
        shapes,
        [whole(*shape) for shape in shapes],
        n * POS,
        scratch=[pltpu.VMEM((2, full, full), F32)],
        flops=10**6,
        moved=10**7,
    )


def merge_borders(core, from_right, from_left, from_below, from_above):
    edge = core.shape[1]

    def body(g, fr, fl, fb, fa, out):
        out[...] = g[...]
        out[:, edge - H :] += fb[:, :, H : H + edge]
        out[:, :H] += fa[:, :, H : H + edge]
        out[:, :, edge - H :] += fr[...]
        out[:, :, :H] += fl[...]

    operands = [core, from_right, from_left, from_below, from_above]
    return call(
        body,
        [],
        operands,
        [whole(*x.shape) for x in operands],
        [core.shape],
        [whole(*core.shape)],
        1,
        flops=10**6,
        moved=10**7,
    )[0]


def turn_kernel(tables, info, patches, probes, roots, cover, batch):
    size = patches.shape[-1]
    h = size // 2
    rows = 4 * size
    extra = 0 if cover is None else cover.shape[0]

    def body(info_ref, t, patch, root, *rest):
        p, rest = rest[:8], rest[8:]
        if extra:
            cover_ref, rest = rest[0], rest[1:]
        sent, keep, gpatch, z, scratch = rest
        i = pl.program_id(0)

        @pl.when(i == 0)
        def _():
            sent[:rows] = jnp.zeros((rows, size), F32)
            if extra:
                sent[rows:] = cover_ref[...]

        gpatch[...] = jnp.zeros_like(gpatch)

        @pl.when(batch * POS + i < info_ref[0])
        def _():
            bits = [info_ref[2], info_ref[2], info_ref[1], info_ref[1]]
            totals = [0.0, 0.0]
            for m in range(4):
                pair = illuminated(t, patch, (rows_of(p[2 * m], bits[m]), rows_of(p[2 * m + 1], bits[m])))
                for e in range(2):
                    if m < 2:
                        z[0, m, e] = pair[e]
                    else:
                        scratch[m - 2, e] = pair[e]
                    totals[e] = totals[e] + power_of(pair[e])
            for e in range(2):
                keep[0, e] = 1.0 - root[0, e] * lax.rsqrt(totals[e] + 0.1)
            for m in range(2, 4):
                probe = (rows_of(p[2 * m], bits[m]), rows_of(p[2 * m + 1], bits[m]))
                spectrum = (scratch[m - 2, 0], scratch[m - 2, 1])
                gradients(t, patch, probe, spectrum, keep, sent, (m - 2) * 2 * size, bits[m], gpatch)

    operands = [tables, patches, roots, *probes]
    specs = [
        whole(*tables.shape),
        per_batch_slot(batch, 2, size, size),
        per_batch_slot(batch, 2, size, h),
    ] + [whole(size, size)] * 8
    if extra:
        operands, specs = [*operands, cover], [*specs, whole(*cover.shape)]
    return call(
        body,
        [info],
        operands,
        specs,
        [(rows + extra, size), (POS, 2, size, h), (POS, 2, size, size), (POS, 2, 2, size, size)],
        [whole(rows + extra, size), per_slot(2, size, h), per_slot(2, size, size), per_slot(2, 2, size, size)],
        POS,
        scratch=[pltpu.VMEM((2, 2, size, size), F32)],
        flops=POS * 6 * 24 * size**3,
        moved=8 * 10**6,
    )


def back_kernel(tables, info, patches, probes, spectra, keep, gpatch, batch):
    size = patches.shape[-1]
    h = size // 2

    def body(info_ref, t, patch, z, k, g_in, *rest):
        p, (g0, g1, g_out) = rest[:4], rest[4:]
        i = pl.program_id(0)

        @pl.when(i == 0)
        def _():
            g0[...] = jnp.zeros_like(g0)
            g1[...] = jnp.zeros_like(g1)

        g_out[...] = g_in[...]

        @pl.when(batch * POS + i < info_ref[0])
        def _():
            bit = info_ref[2]
            for m, out in ((1, g1), (0, g0)):
                probe = (rows_of(p[2 * m], bit), rows_of(p[2 * m + 1], bit))
                gradients(t, patch, probe, (z[0, m, 0], z[0, m, 1]), k, out, 0, bit, g_out)

    return call(
        body,
        [info],
        [tables, patches, spectra, keep, gpatch, *probes[:4]],
        [
            whole(*tables.shape),
            per_batch_slot(batch, 2, size, size),
            per_slot(2, 2, size, size),
            per_slot(2, size, h),
            per_slot(2, size, size),
        ]
        + [whole(size, size)] * 4,
        [(2 * size, size), (2 * size, size), (POS, 2, size, size)],
        [whole(2 * size, size), whole(2 * size, size), per_slot(2, size, size)],
        POS,
        flops=POS * 2 * 24 * size**3,
        moved=6 * 10**6,
    )


def finish_kernel(info, probes, field, inner):
    size = probes[0].shape[0]
    edge = field.shape[1]
    chunk = edge // 4

    def body(info_ref, *refs):
        p, (o, g, probe_out, object_out, power) = refs[:8], refs[8:]
        i = pl.program_id(0)
        for m in range(4):

            @pl.when(i == m)
            def _():
                bit = info_ref[2] if m < 2 else info_ref[1]
                re, im = rows_of(p[2 * m], bit), rows_of(p[2 * m + 1], bit)
                probe_out[0, 0], probe_out[0, 1] = re, im
                square = re * re + im * im
                power[...] = square if m == 0 else power[...] + square

        @pl.when(i >= 4)
        def _():
            top = jnp.max(power[...], keepdims=True)
            object_out[...] = o[...] - g[...] * (0.5 / top)[None]

    spec = pl.BlockSpec((2, chunk, edge), lambda i, *_: (0, jnp.maximum(i - 4, 0), 0))
    return call(
        body,
        [info],
        [*probes, field, inner],
        [whole(size, size)] * 8 + [spec, spec],
        [(4, 2, size, size), field.shape],
        [pl.BlockSpec((1, 2, size, size), lambda i, info_ref: (info_ref[3 + jnp.minimum(i, 3)], 0, 0, 0)), spec],
        8,
        scratch=[pltpu.VMEM((size, size), F32)],
        flops=10**6,
        moved=10**7,
    )


def flips(wide, narrow):
    bits = [(0, 2 << i) for i in range(1, narrow.bit_length() - 2)] + [
        (1 << i, 0) for i in range(1, wide.bit_length() - 1)
    ]

    def exchange(even, odd):
        pairs = []
        for w in range(wide):
            for n in range(narrow):
                dw, dn = odd if n & 1 else even
                pairs.append((w * narrow + n, (w ^ dw) * narrow + (n ^ dn)))
        return functools.partial(lax.ppermute, axis_name=AXES, perm=pairs)

    core = exchange((0, 1), (0, 1))
    first = exchange((0, 2), (1, 0))
    second = exchange((1, 0), (0, 2))
    return core, first, second, [exchange(a, b) for a, b in zip(bits, bits[::-1])]


def shifted(value, axis, steps):
    count = lax.axis_size(axis)
    leading, last = (max(0, -steps), min(count, count - steps))
    return lax.ppermute(value, axis, [(source, source + steps) for source in range(leading, last)])


def local(object_field, probe, patterns, offsets, counts):
    edge = object_field.shape[1]
    size = probe.shape[-1]
    slots = patterns.shape[2]
    h = size // 2
    wide, narrow = lax.axis_size("wide"), lax.axis_size("narrow")
    w, n = lax.axis_index("wide"), lax.axis_index("narrow")
    core, first, second, rest = flips(wide, narrow)
    offs = offsets.reshape(slots * 2)

    left_side = shifted(object_field[:, :, edge - H :], "wide", 1)
    right_side = shifted(object_field[:, :, :H], "wide", -1)

    def strip(lo):
        return jnp.concatenate([x[:, lo : lo + H] for x in (left_side, object_field, right_side)], 2)

    top_side = shifted(strip(edge - H), "narrow", 1)
    bottom_side = shifted(strip(0), "narrow", -1)

    tables = jnp.asarray(dft_tables(size))
    order = np.concatenate([np.arange(0, size, 2), np.arange(1, size, 2)])
    pick = jnp.asarray(np.eye(size, dtype=np.float32)[order])
    roots = jnp.einsum("pj,sjk->spk", pick, jnp.sqrt(patterns[0, 0]), precision=lax.Precision.HIGHEST)
    roots = jnp.einsum("spk,qk->spq", roots, pick, precision=lax.Precision.HIGHEST)
    roots = roots.reshape(slots, size, 2, h).transpose(0, 2, 1, 3)

    c = n % 2
    bit_n, bit_w = (n // 2) % 2, w % 2
    b1 = jnp.where(c == 0, bit_n, bit_w)
    b2 = jnp.where(c == 0, bit_w, bit_n)
    ours, theirs = 2 * c, 2 * (1 - c)
    order_of = [ours + b1, ours + 1 - b1, theirs + b2, theirs + 1 - b2]
    info = jnp.stack([counts[0, 0], b1, b2, *order_of]).astype(jnp.int32)
    split_rows = probe.reshape(4, 2, 2, h, size)
    probes = []
    for m, bit in zip(order_of, (b2, b2, b1, b1)):
        for part in range(2):
            mine = lax.dynamic_slice(split_rows, (m, part, bit, 0, 0), (1, 1, 1, h, size))
            other = lax.dynamic_slice(split_rows, (m, part, 1 - bit, 0, 0), (1, 1, 1, h, size))
            probes.append(jnp.concatenate([mine.reshape(h, size), other.reshape(h, size)], 0))

    sides = (left_side, right_side, top_side, bottom_side)
    patches, cover = cut_patches(offs, info, object_field, sides, size, slots)

    patch_gradients = []
    for batch in range(BATCHES):
        extra = cover if batch == 0 else None

        def ride(x):
            return x if extra is None else jnp.concatenate([x, extra], 0)

        sent, keep, gpatch, z = turn_kernel(tables, info, patches, probes, roots, extra, batch)
        got = core(sent)
        g0, g1, gpatch = back_kernel(tables, info, patches, probes, z, keep, gpatch, batch)
        patch_gradients.append(gpatch)
        if extra is not None:
            extra = extra + got[4 * size :]
        sent_a = g1[:size] + got[2 * size : 3 * size]
        sent_b = g1[size:] + got[3 * size : 4 * size]
        if batch == BATCHES - 1:
            placed = place_gradients(offs, info, patch_gradients, (sent_a, sent_b), edge)
        got_a = first(ride(sent_a))
        got_b = first(sent_b)
        sent_a = g0[h:size] + got[h:size] + got_a[h:size]
        sent_b = g0[size + h :] + got[size + h : 2 * size] + got_b[h:]
        a = g0[:h] + got[:h] + got_a[:h]
        b = g0[size : size + h] + got[size : size + h] + got_b[:h]
        if extra is not None:
            extra = extra + got_a[size:]
        got_a = second(ride(sent_a))
        got_b = second(sent_b)
        a = a + got_a[:h]
        b = b + got_b
        if extra is not None:
            extra = extra + got_a[h:]
        for exchange in rest:
            got_a = exchange(ride(a))
            got_b = exchange(b)
            a = a + got_a[:h]
            b = b + got_b
            if extra is not None:
                extra = extra + got_a[h:]
        if extra is not None:
            scales = jnp.sum(extra, axis=1) / (size * size)
        a = probes[0][:h] - a / scales[batch]
        b = probes[1][:h] - b / scales[batch]
        a = jnp.concatenate([a, second(a)], 0)
        b = jnp.concatenate([b, second(b)], 0)
        own = [a, b, first(a), first(b)]
        probes = own + [core(x) for x in own]

    inside, upper, lower, left_part, right_part = placed
    from_below = shifted(upper, "narrow", -1)
    from_above = shifted(lower, "narrow", 1)

    def border(part, lo):
        below = jnp.pad(from_below[:, :, lo : lo + H], ((0, 0), (edge - H, 0), (0, 0)))
        above = jnp.pad(from_above[:, :, lo : lo + H], ((0, 0), (0, edge - H), (0, 0)))
        return part + below + above

    from_right = shifted(border(left_part, 0), "wide", -1)
    from_left = shifted(border(right_part, H + edge), "wide", 1)
    inner = merge_borders(inside, from_right, from_left, from_below, from_above)
    probe_new, object_new = finish_kernel(info, probes, object_field, inner)
    return (object_new, probe_new)


def solution(mesh):
    placed = (
        P(None, "narrow", "wide"),
        P(),
        P("narrow", "wide", None, None, None),
        P("narrow", "wide", None, None),
        P("narrow", "wide"),
    )
    return jax.shard_map(
        local,
        mesh=mesh,
        in_specs=placed,
        out_specs=(P(None, "narrow", "wide"), P()),
        check_vma=False,
    )
```

time: 338 us -> 293 us (0.87)
  other arithmetic: 42.6 us -> 7.07 us
  starting transfers between devices: 76.9 us -> 110 us
  local copies, waits for them, and re-layouts: 24.5 us -> 8.62 us
  waiting for transfers between devices: 114 us -> 101 us
  Pallas kernels: 69.3 us -> 56.9 us
    ppermute x36 -> x42, starting transfers between devices: 44.7 us -> 76.7 us  [the longest x12 25.8 us: local(): probes = own + [core(x) for x in own]]
    ppermute x36 -> x42, waiting for transfers between devices: 79.5 us -> 61.5 us  [the longest x3 12.8 us: local(): got_b = first(sent_b)]
    pallas_call x20 -> x10, Pallas kernels: 69.3 us -> 56.9 us  [call(): pl.pallas_call(body, out_shape=[jax.ShapeDtypeStruct(s, F32) for s in out...]
    unnamed x72 -> x15, local copies, waits for them, and re-layouts: 10.8 us -> 1.42 us
    select_n x8 -> x0, other arithmetic: 7.99 us -> none  [the longest x2 5.77 us: local(): probe_new = jnp.take(by_group, where, axis=0).reshape(probe.shape)]
    add x28 -> x18, other arithmetic: 7.44 us -> 0.56 us  [the longest x3 0.21 us: local(): sent_b = g1[size:] + got[3 * size:4 * size]]
    ppermute x6, waiting for transfers between devices: 13.8 us -> 20.2 us  [local(): got_b = exchange(b)]
    sub x7 -> x6, other arithmetic: 10.2 us -> 3.97 us  [the longest x3 1.98 us: local(): a = probes[0][:h] - a / scales[batch]]
  transfers between devices with their start and end apart: 53 -> 59, of which waited for: 22 -> 29; matrix products, arithmetic and copies ran while one was open for 12% -> 6% of each run, Pallas kernels for 11% -> 7%
where the time goes in v2:
time: 293 us; the launch traced here: 290 us
  starting transfers between devices  110 us (38%)
  waiting for transfers between devices  101 us (34%)
  Pallas kernels  56.9 us (19%)
  local copies, waits for them, and re-layouts  8.62 us (3%)
  other arithmetic  7.07 us (2%)
  matrix products  4.5 us (2%)
    pallas_call x10, Pallas kernels, call(): pl.pallas_call(body, out_shape=[jax.ShapeDtypeStruct(s, F32) for s in out...  56.9 us
    ppermute x12, starting transfers between devices, local(): probes = own + [core(x) for x in own]  25.8 us
    ppermute x6, waiting for transfers between devices, local(): got_b = exchange(b)  20.2 us
    ppermute x8, waiting for transfers between devices, shifted(): lax.ppermute(value, axis, [(source, source + steps) for source in range(l...  19.4 us
    ppermute x8, starting transfers between devices, shifted(): lax.ppermute(value, axis, [(source, source + steps) for source in range(l...  18.5 us
    ppermute x3, waiting for transfers between devices, local(): got_b = first(sent_b)  12.8 us
    ppermute x3, starting transfers between devices, local(): got_b = second(sent_b)  12.7 us
    ppermute x6, waiting for transfers between devices, local(): own = [a, b, first(a), first(b)]  10.7 us
  transfers between devices with their start and end apart: 59, of which 29 were waited for; matrix products, arithmetic and copies ran while one was open for 6% of the time, Pallas kernels for 7%

profile of v2, /device:TPU:0, one launch (start us, length us, event | category | flops | bytes accessed | tf_op | source)
XLA Modules:
  0.0 290.1 jit_solution(17907197258427031249)
XLA Ops:
  3.5 5.5 %collective-permute-start = (f32[2,512,128]{2,1,0:T(8,128)S(1)}, f32[2,512,128]{2,1,0:T(8,128)S(1)}, u32[]{:S(2)}, u32[]{:S(2)}) collective-permute-start(f32[2,512,128]{2,1,0:T(8,128)S(1)} %get-tuple-element.81), channel_id=1, source_target_pairs={{0,4},{4,8},{8,12},{12,16},{16,20},{20,24},{24,28},{1,5},{5,9},{9,... | collective-permute-start | bytes 1572872 | tf_op jit(solution)/shard_map/ppermute | solution.py:455
  11.0 8.1 %collective-permute-done.1.right_ref = f32[2,512,128]{2,1,0:T(8,128)S(1)} collective-permute-done((f32[2,512,128]{2,1,0:T(8,128)S(1)}, f32[2,512,128]{2,1,0:T(8,128)S(1)}, u32[]{:S(2)}, u32[]{:S(2)}) %collective-permute-start.1) | collective-permute-done | bytes 524320 | tf_op jit(solution)/shard_map/ppermute | solution.py:455
  19.0 11.4 %collective-permute-done.left_ref = f32[2,512,128]{2,1,0:T(8,128)S(1)} collective-permute-done((f32[2,512,128]{2,1,0:T(8,128)S(1)}, f32[2,512,128]{2,1,0:T(8,128)S(1)}, u32[]{:S(2)}, u32[]{:S(2)}) %collective-permute-start) | collective-permute-done | bytes 524320 | tf_op jit(solution)/shard_map/ppermute | solution.py:455
  31.4 2.8 collective-permute-start.2
  36.5 2.7 fusion
  40.1 3.0 %copy.11 = f32[6,256,2,128]{3,1,2,0:T(8,128)} copy(f32[6,256,2,128]{1,3,2,0:T(8,128)} %bitcast.55) | data formatting | bytes 3145728 | tf_op jit(solution)/shard_map/reshape | solution.py:482
  45.2 6.0 %shard_map.86 = (f32[6,2,256,256]{3,2,1,0:T(8,128)}, f32[8,256]{1,0:T(8,128)S(1)}) custom-call(s32[12]{0:T(128)S(1)} %reshape.64.offs, s32[7]{0:T(128)S(1)} %stack.27.info_ref, f32[2,512,512]{2,1,0:T(8,128)S(1)} %copy-done, f32[2,512,128]{2,1,0:T(8,128)S(1)} %collective-permute-done.left_ref, f32[2,512,128]{2,1,0:T(8,128)S(1)} %collective-permute-done.1.right_ref, ...), custom_call_target="tpu_custom_call" | custom-call | flops 1000000 | bytes 8000000 | tf_op jit(solution)/shard_map/pallas_call | solution.py:148
  51.2 12.2 %shard_map.87 = (f32[1032,256]{1,0:T(8,128)S(1)}, f32[2,2,256,128]{3,2,1,0:T(8,128)S(1)}, f32[2,2,256,256]{3,2,1,0:T(8,128)S(1)}, f32[2,2,2,256,256]{4,3,2,1,0:T(8,128)}) custom-call(s32[7]{0:T(128)S(1)} %stack.27.info_ref, bf16[4,2,256,256]{3,2,1,0:T(8,128)(2,1)S(1)} %copy-done.1, f32[6,2,256,256]{3,2,1,0:T(8,128)} %get-tuple-element.32.patch, ...), custom_call_target="tpu_custom_call" | custom-call | flops 4831838208 | bytes 8000000 | tf_op jit(solution)/shard_map/pallas_call | solution.py:148
  63.4 4.4 %collective-permute-start.4 = (f32[1032,256]{1,0:T(8,128)S(1)}, f32[1032,256]{1,0:T(8,128)S(1)}, u32[]{:S(2)}, u32[]{:S(2)}) collective-permute-start(f32[1032,256]{1,0:T(8,128)S(1)} %get-tuple-element.38), channel_id=1, source_target_pairs={{0,1},{1,0},{2,3},{3,2},{4,5},{5,4},{6,7},{7,6},{8,9},{9,8},{10,11... | collective-permute-start | bytes 3170312 | tf_op jit(solution)/shard_map/ppermute | solution.py:510
  67.7 6.0 %shard_map.88 = (f32[512,256]{1,0:T(8,128)S(1)}, f32[512,256]{1,0:T(8,128)S(1)}, f32[2,2,256,256]{3,2,1,0:T(8,128)S(1)}) custom-call(s32[7]{0:T(128)S(1)} %stack.27.info_ref, bf16[4,2,256,256]{3,2,1,0:T(8,128)(2,1)S(1)} %copy-done.1, f32[6,2,256,256]{3,2,1,0:T(8,128)} %get-tuple-element.32.patch, f32[2,2,2,256,256]{4,3,2,1,0:T(8,128)} %get-tuple-element.34.z, ...), custom_call_target="tpu_custom_call" | custom-call | flops 1610612736 | bytes 6000000 | tf_op jit(solution)/shard_map/pallas_call | solution.py:148
  76.0 4.3 %collective-permute-done.10 = f32[256,256]{1,0:T(8,128)S(1)} collective-permute-done((f32[256,256]{1,0:T(8,128)S(1)}, f32[256,256]{1,0:T(8,128)S(1)}, u32[]{:S(2)}, u32[]{:S(2)}) %collective-permute-start.10) | collective-permute-done | bytes 262176 | tf_op jit(solution)/shard_map/ppermute | solution.py:520
  80.3 3.0 %collective-permute-start.11 = (f32[128,256]{1,0:T(8,128)S(1)}, f32[128,256]{1,0:T(8,128)S(1)}, u32[]{:S(2)}, u32[]{:S(2)}) collective-permute-start(f32[128,256]{1,0:T(8,128)S(1)} %slice_add_fusion.22), channel_id=1, source_target_pairs={{0,4},{1,3},{2,6},{3,1},{4,0},{5,7},{6,2},{7,5},{8,12},{9,11},{10,... | collective-permute-start | bytes 393224 | tf_op jit(solution)/shard_map/ppermute | solution.py:528
  83.3 2.9 %collective-permute-done.11 = f32[128,256]{1,0:T(8,128)S(1)} collective-permute-done((f32[128,256]{1,0:T(8,128)S(1)}, f32[128,256]{1,0:T(8,128)S(1)}, u32[]{:S(2)}, u32[]{:S(2)}) %collective-permute-start.11) | collective-permute-done | bytes 131104 | tf_op jit(solution)/shard_map/ppermute | solution.py:528
  88.5 3.0 %collective-permute-done.6 = f32[136,256]{1,0:T(8,128)S(1)} collective-permute-done((f32[136,256]{1,0:T(8,128)S(1)}, f32[136,256]{1,0:T(8,128)S(1)}, u32[]{:S(2)}, u32[]{:S(2)}) %collective-permute-start.6) | collective-permute-done | bytes 139296 | tf_op jit(solution)/shard_map/ppermute | solution.py:527
  93.2 3.5 %collective-permute-done.7 = f32[136,256]{1,0:T(8,128)S(1)} collective-permute-done((f32[136,256]{1,0:T(8,128)S(1)}, f32[136,256]{1,0:T(8,128)S(1)}, u32[]{:S(2)}, u32[]{:S(2)}) %collective-permute-start.7) | collective-permute-done | bytes 139296 | tf_op jit(solution)/shard_map/ppermute | solution.py:534
  96.7 2.3 collective-permute-start.8
  99.0 6.6 %collective-permute-done.12 = f32[128,256]{1,0:T(8,128)S(1)} collective-permute-done((f32[128,256]{1,0:T(8,128)S(1)}, f32[128,256]{1,0:T(8,128)S(1)}, u32[]{:S(2)}, u32[]{:S(2)}) %collective-permute-start.12) | collective-permute-done | bytes 131104 | tf_op jit(solution)/shard_map/ppermute | solution.py:535
  109.6 2.8 collective-permute-done.13
  113.9 5.2 %collective-permute-done.14 = f32[128,256]{1,0:T(8,128)S(1)} collective-permute-done((f32[128,256]{1,0:T(8,128)S(1)}, f32[128,256]{1,0:T(8,128)S(1)}, u32[]{:S(2)}, u32[]{:S(2)}) %collective-permute-start.14) | collective-permute-done | bytes 131104 | tf_op jit(solution)/shard_map/ppermute | solution.py:545
  120.3 5.3 %collective-permute-done.16.rest_3_ = f32[256,256]{1,0:T(8,128)S(1)} collective-permute-done((f32[256,256]{1,0:T(8,128)S(1)}, f32[256,256]{1,0:T(8,128)S(1)}, u32[]{:S(2)}, u32[]{:S(2)}) %collective-permute-start.16) | collective-permute-done | bytes 262176 | tf_op jit(solution)/shard_map/ppermute | solution.py:546
  127.2 7.8 %shard_map.89 = (f32[1024,256]{1,0:T(8,128)S(1)}, f32[2,2,256,128]{3,2,1,0:T(8,128)S(1)}, f32[2,2,256,256]{3,2,1,0:T(8,128)S(1)}, f32[2,2,2,256,256]{4,3,2,1,0:T(8,128)}) custom-call(s32[7]{0:T(128)S(1)} %stack.27.info_ref, bf16[4,2,256,256]{3,2,1,0:T(8,128)(2,1)S(1)} %copy-done.1, f32[6,2,256,256]{3,2,1,0:T(8,128)} %get-tuple-element.32.patch, ...), custom_call_target="tpu_custom_call" | custom-call | flops 4831838208 | bytes 8000000 | tf_op jit(solution)/shard_map/pallas_call | solution.py:148
  135.1 4.4 %shard_map.90 = (f32[512,256]{1,0:T(8,128)S(1)}, f32[512,256]{1,0:T(8,128)S(1)}, f32[2,2,256,256]{3,2,1,0:T(8,128)S(1)}) custom-call(s32[7]{0:T(128)S(1)} %stack.27.info_ref, bf16[4,2,256,256]{3,2,1,0:T(8,128)(2,1)S(1)} %copy-done.1, f32[6,2,256,256]{3,2,1,0:T(8,128)} %get-tuple-element.32.patch, f32[2,2,2,256,256]{4,3,2,1,0:T(8,128)} %get-tuple-element.40.z, ...), custom_call_target="tpu_custom_call" | custom-call | flops 1610612736 | bytes 6000000 | tf_op jit(solution)/shard_map/pallas_call | solution.py:148
  139.6 2.9 %collective-permute-start.27 = (f32[256,256]{1,0:T(8,128)S(1)}, f32[256,256]{1,0:T(8,128)S(1)}, u32[]{:S(2)}, u32[]{:S(2)}) collective-permute-start(f32[256,256]{1,0:T(8,128)S(1)} %get-tuple-element.92), channel_id=1, source_target_pairs={{0,2},{1,5},{2,0},{3,7},{4,6},{5,1},{6,4},{7,3},{8,10},{9,13},{10,... | collective-permute-start | bytes 786440 | tf_op jit(solution)/shard_map/ppermute | solution.py:520
  142.6 4.3 %collective-permute-done.27 = f32[256,256]{1,0:T(8,128)S(1)} collective-permute-done((f32[256,256]{1,0:T(8,128)S(1)}, f32[256,256]{1,0:T(8,128)S(1)}, u32[]{:S(2)}, u32[]{:S(2)}) %collective-permute-start.27) | collective-permute-done | bytes 262176 | tf_op jit(solution)/shard_map/ppermute | solution.py:520
  146.9 6.8 %collective-permute-start.28 = (f32[128,256]{1,0:T(8,128)S(1)}, f32[128,256]{1,0:T(8,128)S(1)}, u32[]{:S(2)}, u32[]{:S(2)}) collective-permute-start(f32[128,256]{1,0:T(8,128)S(1)} %slice_add_fusion.14), channel_id=1, source_target_pairs={{0,4},{1,3},{2,6},{3,1},{4,0},{5,7},{6,2},{7,5},{8,12},{9,11},{10,... | collective-permute-start | bytes 393224 | tf_op jit(solution)/shard_map/ppermute | solution.py:528
  153.7 2.9 %collective-permute-done.28 = f32[128,256]{1,0:T(8,128)S(1)} collective-permute-done((f32[128,256]{1,0:T(8,128)S(1)}, f32[128,256]{1,0:T(8,128)S(1)}, u32[]{:S(2)}, u32[]{:S(2)}) %collective-permute-start.28) | collective-permute-done | bytes 131104 | tf_op jit(solution)/shard_map/ppermute | solution.py:528
  158.8 2.9 %collective-permute-done.23 = f32[128,256]{1,0:T(8,128)S(1)} collective-permute-done((f32[128,256]{1,0:T(8,128)S(1)}, f32[128,256]{1,0:T(8,128)S(1)}, u32[]{:S(2)}, u32[]{:S(2)}) %collective-permute-start.23) | collective-permute-done | bytes 131104 | tf_op jit(solution)/shard_map/ppermute | solution.py:527
  162.2 3.5 %collective-permute-done.29 = f32[128,256]{1,0:T(8,128)S(1)} collective-permute-done((f32[128,256]{1,0:T(8,128)S(1)}, f32[128,256]{1,0:T(8,128)S(1)}, u32[]{:S(2)}, u32[]{:S(2)}) %collective-permute-start.29) | collective-permute-done | bytes 131104 | tf_op jit(solution)/shard_map/ppermute | solution.py:535
  165.8 2.7 collective-permute-done.24
  169.3 3.1 %collective-permute-done.30 = f32[128,256]{1,0:T(8,128)S(1)} collective-permute-done((f32[128,256]{1,0:T(8,128)S(1)}, f32[128,256]{1,0:T(8,128)S(1)}, u32[]{:S(2)}, u32[]{:S(2)}) %collective-permute-start.30) | collective-permute-done | bytes 131104 | tf_op jit(solution)/shard_map/ppermute | solution.py:535
  179.7 3.1 %collective-permute-done.26 = f32[128,256]{1,0:T(8,128)S(1)} collective-permute-done((f32[128,256]{1,0:T(8,128)S(1)}, f32[128,256]{1,0:T(8,128)S(1)}, u32[]{:S(2)}, u32[]{:S(2)}) %collective-permute-start.26) | collective-permute-done | bytes 131104 | tf_op jit(solution)/shard_map/ppermute | solution.py:544
  185.8 3.5 %collective-permute-done.32.rest_2_ = f32[256,256]{1,0:T(8,128)S(1)} collective-permute-done((f32[256,256]{1,0:T(8,128)S(1)}, f32[256,256]{1,0:T(8,128)S(1)}, u32[]{:S(2)}, u32[]{:S(2)}) %collective-permute-start.32) | collective-permute-done | bytes 262176 | tf_op jit(solution)/shard_map/ppermute | solution.py:546
  190.8 3.1 %shard_map.91 = (f32[1024,256]{1,0:T(8,128)S(1)}, f32[2,2,256,128]{3,2,1,0:T(8,128)S(1)}, f32[2,2,256,256]{3,2,1,0:T(8,128)S(1)}, f32[2,2,2,256,256]{4,3,2,1,0:T(8,128)}) custom-call(s32[7]{0:T(128)S(1)} %stack.27.info_ref, bf16[4,2,256,256]{3,2,1,0:T(8,128)(2,1)S(1)} %copy-done.1, f32[6,2,256,256]{3,2,1,0:T(8,128)} %get-tuple-element.32.patch, ...), custom_call_target="tpu_custom_call" | custom-call | flops 4831838208 | bytes 8000000 | tf_op jit(solution)/shard_map/pallas_call | solution.py:148
  194.0 2.5 shard_map.92
  196.6 6.0 %collective-permute-start.44 = (f32[256,256]{1,0:T(8,128)S(1)}, f32[256,256]{1,0:T(8,128)S(1)}, u32[]{:S(2)}, u32[]{:S(2)}) collective-permute-start(f32[256,256]{1,0:T(8,128)S(1)} %get-tuple-element.88.refs_4_), channel_id=1, source_target_pairs={{0,2},{1,5},{2,0},{3,7},{4,6},{5,1},{6,4},{7,3},{8,10},{9,13},{10,... | collective-permute-start | bytes 786440 | tf_op jit(solution)/shard_map/ppermute | solution.py:520
  202.7 4.3 %collective-permute-done.44 = f32[256,256]{1,0:T(8,128)S(1)} collective-permute-done((f32[256,256]{1,0:T(8,128)S(1)}, f32[256,256]{1,0:T(8,128)S(1)}, u32[]{:S(2)}, u32[]{:S(2)}) %collective-permute-start.44) | collective-permute-done | bytes 262176 | tf_op jit(solution)/shard_map/ppermute | solution.py:520
  207.0 2.9 collective-permute-start.45
  209.9 3.1 %collective-permute-done.45 = f32[128,256]{1,0:T(8,128)S(1)} collective-permute-done((f32[128,256]{1,0:T(8,128)S(1)}, f32[128,256]{1,0:T(8,128)S(1)}, u32[]{:S(2)}, u32[]{:S(2)}) %collective-permute-start.45) | collective-permute-done | bytes 131104 | tf_op jit(solution)/shard_map/ppermute | solution.py:528
  215.0 5.8 %shard_map.93 = (f32[2,512,512]{2,1,0:T(8,128)}, f32[2,128,768]{2,1,0:T(8,128)S(1)}, f32[2,128,768]{2,1,0:T(8,128)S(1)}, f32[2,512,128]{2,1,0:T(8,128)S(1)}, f32[2,512,128]{2,1,0:T(8,128)S(1)}) custom-call(s32[12]{0:T(128)S(1)} %reshape.64.offs, s32[7]{0:T(128)S(1)} %stack.27.info_ref, f32[2,2,256,256]{3,2,1,0:T(8,128)S(1)} %get-tuple-element.52.refs_0_, ...), custom_call_target="tpu_custom_call" | custom-call | flops 1000000 | bytes 10000000 | tf_op jit(solution)/shard_map/pallas_call | solution.py:148
  222.1 6.1 %collective-permute-start.46 = (f32[128,256]{1,0:T(8,128)S(1)}, f32[128,256]{1,0:T(8,128)S(1)}, u32[]{:S(2)}, u32[]{:S(2)}) collective-permute-start(f32[128,256]{1,0:T(8,128)S(1)} %get-tuple-element.86), channel_id=1, source_target_pairs={{0,8},{1,17},{2,10},{3,19},{4,12},{5,21},{6,14},{7,23},{8,0},{9,25... | collective-permute-start | bytes 393224 | tf_op jit(solution)/shard_map/ppermute | solution.py:535
  228.2 4.2 %collective-permute-done.46 = f32[128,256]{1,0:T(8,128)S(1)} collective-permute-done((f32[128,256]{1,0:T(8,128)S(1)}, f32[128,256]{1,0:T(8,128)S(1)}, u32[]{:S(2)}, u32[]{:S(2)}) %collective-permute-start.46) | collective-permute-done | bytes 131104 | tf_op jit(solution)/shard_map/ppermute | solution.py:535
  232.5 3.8 %collective-permute-start.47 = (f32[128,256]{1,0:T(8,128)S(1)}, f32[128,256]{1,0:T(8,128)S(1)}, u32[]{:S(2)}, u32[]{:S(2)}) collective-permute-start(f32[128,256]{1,0:T(8,128)S(1)} %add.318), channel_id=1, source_target_pairs={{0,16},{1,9},{2,18},{3,11},{4,20},{5,13},{6,22},{7,15},{8,24},{9,1... | collective-permute-start | bytes 393224 | tf_op jit(solution)/shard_map/ppermute | solution.py:535
  238.5 3.1 %collective-permute-start.42 = (f32[128,256]{1,0:T(8,128)S(1)}, f32[128,256]{1,0:T(8,128)S(1)}, u32[]{:S(2)}, u32[]{:S(2)}) collective-permute-start(f32[128,256]{1,0:T(8,128)S(1)} %add.310), channel_id=1, source_target_pairs={{0,16},{1,9},{2,18},{3,11},{4,20},{5,13},{6,22},{7,15},{8,24},{9,1... | collective-permute-start | bytes 393224 | tf_op jit(solution)/shard_map/ppermute | solution.py:534
  248.2 2.6 collective-permute-start.58
  252.2 2.4 collective-permute-start.49
  254.6 4.1 %collective-permute-start.52 = (f32[256,256]{1,0:T(8,128)S(1)}, f32[256,256]{1,0:T(8,128)S(1)}, u32[]{:S(2)}, u32[]{:S(2)}) collective-permute-start(f32[256,256]{1,0:T(8,128)S(1)} %pad_maximum_fusion.16.refs_1_), channel_id=1, source_target_pairs={{0,1},{1,0},{2,3},{3,2},{4,5},{5,4},{6,7},{7,6},{8,9},{9,8},{10,11... | collective-permute-start | bytes 786440 | tf_op jit(solution)/shard_map/ppermute | solution.py:547
  258.9 20.6 %collective-permute-start.54 = (f32[256,256]{1,0:T(8,128)S(1)}, f32[256,256]{1,0:T(8,128)S(1)}, u32[]{:S(2)}, u32[]{:S(2)}) collective-permute-start(f32[256,256]{1,0:T(8,128)S(1)} %collective-permute-done.50.refs_3_), channel_id=1, source_target_pairs={{0,1},{1,0},{2,3},{3,2},{4,5},{5,4},{6,7},{7,6},{8,9},{9,8},{10,11... | collective-permute-start | bytes 786440 | tf_op jit(solution)/shard_map/ppermute | solution.py:547
  282.9 7.2 %shard_map.95 = (f32[4,2,256,256]{3,2,1,0:T(8,128)}, f32[2,512,512]{2,1,0:T(8,128)}) custom-call(s32[7]{0:T(128)S(1)} %stack.27.info_ref, f32[256,256]{1,0:T(8,128)S(1)} %pad_maximum_fusion.15.refs_0_, f32[256,256]{1,0:T(8,128)S(1)} %pad_maximum_fusion.16.refs_1_, f32[256,256]{1,0:T(8,128)S(1)} %collective-permute-done.49.refs_2_, ...), custom_call_target="tpu_custom_call" | custom-call | flops 1000000 | bytes 10000000 | tf_op jit(solution)/shard_map/pallas_call | solution.py:148
  (156 shorter events, 57.6 us)
Async XLA Ops:
  2.1 16.9 %collective-permute-start.1 = (f32[2,512,128]{2,1,0:T(8,128)S(1)}, f32[2,512,128]{2,1,0:T(8,128)S(1)}, u32[]{:S(2)}, u32[]{:S(2)}) collective-permute-start(f32[2,512,128]{2,1,0:T(8,128)S(1)} %get-tuple-element.80), channel_id=1, source_target_pairs={{4,0},{8,4},{12,8},{16,12},{20,16},{24,20},{28,24},{5,1},{9,5},{13... | collective-permute-start | bytes 1572872 | tf_op jit(solution)/shard_map/ppermute | solution.py:455
  3.5 26.9 %collective-permute-start = (f32[2,512,128]{2,1,0:T(8,128)S(1)}, f32[2,512,128]{2,1,0:T(8,128)S(1)}, u32[]{:S(2)}, u32[]{:S(2)}) collective-permute-start(f32[2,512,128]{2,1,0:T(8,128)S(1)} %get-tuple-element.81), channel_id=1, source_target_pairs={{0,4},{4,8},{8,12},{12,16},{16,20},{20,24},{24,28},{1,5},{5,9},{9,... | collective-permute-start | bytes 1572872 | tf_op jit(solution)/shard_map/ppermute | solution.py:455
  31.4 13.8 %collective-permute-start.2 = (f32[2,128,768]{2,1,0:T(8,128)}, f32[2,128,768]{2,1,0:T(8,128)}, u32[]{:S(2)}, u32[]{:S(2)}) collective-permute-start(f32[2,128,768]{2,1,0:T(8,128)} %pad_maximum_fusion), channel_id=1, source_target_pairs={{0,1},{1,2},{2,3},{4,5},{5,6},{6,7},{8,9},{9,10},{10,11},{12,13},{... | collective-permute-start | bytes 2359304 | tf_op jit(solution)/shard_map/ppermute | solution.py:455
  35.1 10.1 %collective-permute-start.3 = (f32[2,128,768]{2,1,0:T(8,128)}, f32[2,128,768]{2,1,0:T(8,128)}, u32[]{:S(2)}, u32[]{:S(2)}) collective-permute-start(f32[2,128,768]{2,1,0:T(8,128)} %pad_maximum_fusion.1), channel_id=1, source_target_pairs={{1,0},{2,1},{3,2},{5,4},{6,5},{7,6},{9,8},{10,9},{11,10},{13,12},{... | collective-permute-start | bytes 2359304 | tf_op jit(solution)/shard_map/ppermute | solution.py:455
  63.4 10.4 %collective-permute-start.4 = (f32[1032,256]{1,0:T(8,128)S(1)}, f32[1032,256]{1,0:T(8,128)S(1)}, u32[]{:S(2)}, u32[]{:S(2)}) collective-permute-start(f32[1032,256]{1,0:T(8,128)S(1)} %get-tuple-element.38), channel_id=1, source_target_pairs={{0,1},{1,0},{2,3},{3,2},{4,5},{5,4},{6,7},{7,6},{8,9},{9,8},{10,11... | collective-permute-start | bytes 3170312 | tf_op jit(solution)/shard_map/ppermute | solution.py:510
  73.8 6.4 %collective-permute-start.10 = (f32[256,256]{1,0:T(8,128)S(1)}, f32[256,256]{1,0:T(8,128)S(1)}, u32[]{:S(2)}, u32[]{:S(2)}) collective-permute-start(f32[256,256]{1,0:T(8,128)S(1)} %get-tuple-element.84), channel_id=1, source_target_pairs={{0,2},{1,5},{2,0},{3,7},{4,6},{5,1},{6,4},{7,3},{8,10},{9,13},{10,... | collective-permute-start | bytes 786440 | tf_op jit(solution)/shard_map/ppermute | solution.py:520
  74.0 9.4 %collective-permute-start.5 = (f32[264,256]{1,0:T(8,128)S(1)}, f32[264,256]{1,0:T(8,128)S(1)}, u32[]{:S(2)}, u32[]{:S(2)}) collective-permute-start(f32[264,256]{1,0:T(8,128)S(1)} %pad_maximum_fusion.2), channel_id=1, source_target_pairs={{0,2},{1,5},{2,0},{3,7},{4,6},{5,1},{6,4},{7,3},{8,10},{9,13},{10,... | collective-permute-start | bytes 811016 | tf_op jit(solution)/shard_map/ppermute | solution.py:519
  80.3 6.0 %collective-permute-start.11 = (f32[128,256]{1,0:T(8,128)S(1)}, f32[128,256]{1,0:T(8,128)S(1)}, u32[]{:S(2)}, u32[]{:S(2)}) collective-permute-start(f32[128,256]{1,0:T(8,128)S(1)} %slice_add_fusion.22), channel_id=1, source_target_pairs={{0,4},{1,3},{2,6},{3,1},{4,0},{5,7},{6,2},{7,5},{8,12},{9,11},{10,... | collective-permute-start | bytes 393224 | tf_op jit(solution)/shard_map/ppermute | solution.py:528
  96.7 9.1 %collective-permute-start.8 = (f32[136,256]{1,0:T(8,128)S(1)}, f32[136,256]{1,0:T(8,128)S(1)}, u32[]{:S(2)}, u32[]{:S(2)}) collective-permute-start(f32[136,256]{1,0:T(8,128)S(1)} %pad_maximum_fusion.19), channel_id=1, source_target_pairs={{0,16},{1,9},{2,18},{3,11},{4,20},{5,13},{6,22},{7,15},{8,24},{9,1... | collective-permute-start | bytes 417800 | tf_op jit(solution)/shard_map/ppermute | solution.py:534
  99.0 6.6 %collective-permute-start.12 = (f32[128,256]{1,0:T(8,128)S(1)}, f32[128,256]{1,0:T(8,128)S(1)}, u32[]{:S(2)}, u32[]{:S(2)}) collective-permute-start(f32[128,256]{1,0:T(8,128)S(1)} %get-tuple-element.82), channel_id=1, source_target_pairs={{0,8},{1,17},{2,10},{3,19},{4,12},{5,21},{6,14},{7,23},{8,0},{9,25... | collective-permute-start | bytes 393224 | tf_op jit(solution)/shard_map/ppermute | solution.py:535
  105.6 6.7 %collective-permute-start.13 = (f32[128,256]{1,0:T(8,128)S(1)}, f32[128,256]{1,0:T(8,128)S(1)}, u32[]{:S(2)}, u32[]{:S(2)}) collective-permute-start(f32[128,256]{1,0:T(8,128)S(1)} %add.286), channel_id=1, source_target_pairs={{0,16},{1,9},{2,18},{3,11},{4,20},{5,13},{6,22},{7,15},{8,24},{9,1... | collective-permute-start | bytes 393224 | tf_op jit(solution)/shard_map/ppermute | solution.py:535
  107.3 6.6 %collective-permute-start.9 = (f32[128,256]{1,0:T(8,128)S(1)}, f32[128,256]{1,0:T(8,128)S(1)}, u32[]{:S(2)}, u32[]{:S(2)}) collective-permute-start(f32[128,256]{1,0:T(8,128)S(1)} %fusion.11), channel_id=1, source_target_pairs={{0,4},{1,3},{2,6},{3,1},{4,0},{5,7},{6,2},{7,5},{8,12},{9,11},{10,... | collective-permute-start | bytes 393224 | tf_op jit(solution)/shard_map/ppermute | solution.py:544
  113.0 6.2 %collective-permute-start.14 = (f32[128,256]{1,0:T(8,128)S(1)}, f32[128,256]{1,0:T(8,128)S(1)}, u32[]{:S(2)}, u32[]{:S(2)}) collective-permute-start(f32[128,256]{1,0:T(8,128)S(1)} %divide_subtract_fusion.4), channel_id=1, source_target_pairs={{0,4},{1,3},{2,6},{3,1},{4,0},{5,7},{6,2},{7,5},{8,12},{9,11},{10,... | collective-permute-start | bytes 393224 | tf_op jit(solution)/shard_map/ppermute | solution.py:545
  113.9 6.4 %collective-permute-start.15 = (f32[256,256]{1,0:T(8,128)S(1)}, f32[256,256]{1,0:T(8,128)S(1)}, u32[]{:S(2)}, u32[]{:S(2)}) collective-permute-start(f32[256,256]{1,0:T(8,128)S(1)} %pad_maximum_fusion.11.rest_0_), channel_id=1, source_target_pairs={{0,2},{1,5},{2,0},{3,7},{4,6},{5,1},{6,4},{7,3},{8,10},{9,13},{10,... | collective-permute-start | bytes 786440 | tf_op jit(solution)/shard_map/ppermute | solution.py:546
  119.2 6.4 %collective-permute-start.16 = (f32[256,256]{1,0:T(8,128)S(1)}, f32[256,256]{1,0:T(8,128)S(1)}, u32[]{:S(2)}, u32[]{:S(2)}) collective-permute-start(f32[256,256]{1,0:T(8,128)S(1)} %pad_maximum_fusion.12.rest_1_), channel_id=1, source_target_pairs={{0,2},{1,5},{2,0},{3,7},{4,6},{5,1},{6,4},{7,3},{8,10},{9,13},{10,... | collective-permute-start | bytes 786440 | tf_op jit(solution)/shard_map/ppermute | solution.py:546
  119.3 6.4 %collective-permute-start.17 = (f32[256,256]{1,0:T(8,128)S(1)}, f32[256,256]{1,0:T(8,128)S(1)}, u32[]{:S(2)}, u32[]{:S(2)}) collective-permute-start(f32[256,256]{1,0:T(8,128)S(1)} %pad_maximum_fusion.11.rest_0_), channel_id=1, source_target_pairs={{0,1},{1,0},{2,3},{3,2},{4,5},{5,4},{6,7},{7,6},{8,9},{9,8},{10,11... | collective-permute-start | bytes 786440 | tf_op jit(solution)/shard_map/ppermute | solution.py:547
  119.3 6.3 %collective-permute-start.18 = (f32[256,256]{1,0:T(8,128)S(1)}, f32[256,256]{1,0:T(8,128)S(1)}, u32[]{:S(2)}, u32[]{:S(2)}) collective-permute-start(f32[256,256]{1,0:T(8,128)S(1)} %pad_maximum_fusion.12.rest_1_), channel_id=1, source_target_pairs={{0,1},{1,0},{2,3},{3,2},{4,5},{5,4},{6,7},{7,6},{8,9},{9,8},{10,11... | collective-permute-start | bytes 786440 | tf_op jit(solution)/shard_map/ppermute | solution.py:547
  120.3 5.3 %collective-permute-start.19 = (f32[256,256]{1,0:T(8,128)S(1)}, f32[256,256]{1,0:T(8,128)S(1)}, u32[]{:S(2)}, u32[]{:S(2)}) collective-permute-start(f32[256,256]{1,0:T(8,128)S(1)} %collective-permute-done.15.rest_2_), channel_id=1, source_target_pairs={{0,1},{1,0},{2,3},{3,2},{4,5},{5,4},{6,7},{7,6},{8,9},{9,8},{10,11... | collective-permute-start | bytes 786440 | tf_op jit(solution)/shard_map/ppermute | solution.py:547
  139.6 7.3 %collective-permute-start.27 = (f32[256,256]{1,0:T(8,128)S(1)}, f32[256,256]{1,0:T(8,128)S(1)}, u32[]{:S(2)}, u32[]{:S(2)}) collective-permute-start(f32[256,256]{1,0:T(8,128)S(1)} %get-tuple-element.92), channel_id=1, source_target_pairs={{0,2},{1,5},{2,0},{3,7},{4,6},{5,1},{6,4},{7,3},{8,10},{9,13},{10,... | collective-permute-start | bytes 786440 | tf_op jit(solution)/shard_map/ppermute | solution.py:520
  142.5 11.2 %collective-permute-start.22 = (f32[256,256]{1,0:T(8,128)S(1)}, f32[256,256]{1,0:T(8,128)S(1)}, u32[]{:S(2)}, u32[]{:S(2)}) collective-permute-start(f32[256,256]{1,0:T(8,128)S(1)} %get-tuple-element.93), channel_id=1, source_target_pairs={{0,2},{1,5},{2,0},{3,7},{4,6},{5,1},{6,4},{7,3},{8,10},{9,13},{10,... | collective-permute-start | bytes 786440 | tf_op jit(solution)/shard_map/ppermute | solution.py:519
  146.9 9.8 %collective-permute-start.28 = (f32[128,256]{1,0:T(8,128)S(1)}, f32[128,256]{1,0:T(8,128)S(1)}, u32[]{:S(2)}, u32[]{:S(2)}) collective-permute-start(f32[128,256]{1,0:T(8,128)S(1)} %slice_add_fusion.14), channel_id=1, source_target_pairs={{0,4},{1,3},{2,6},{3,1},{4,0},{5,7},{6,2},{7,5},{8,12},{9,11},{10,... | collective-permute-start | bytes 393224 | tf_op jit(solution)/shard_map/ppermute | solution.py:528
  158.8 6.9 %collective-permute-start.29 = (f32[128,256]{1,0:T(8,128)S(1)}, f32[128,256]{1,0:T(8,128)S(1)}, u32[]{:S(2)}, u32[]{:S(2)}) collective-permute-start(f32[128,256]{1,0:T(8,128)S(1)} %get-tuple-element.90), channel_id=1, source_target_pairs={{0,8},{1,17},{2,10},{3,19},{4,12},{5,21},{6,14},{7,23},{8,0},{9,25... | collective-permute-start | bytes 393224 | tf_op jit(solution)/shard_map/ppermute | solution.py:535
  161.8 6.7 %collective-permute-start.24 = (f32[128,256]{1,0:T(8,128)S(1)}, f32[128,256]{1,0:T(8,128)S(1)}, u32[]{:S(2)}, u32[]{:S(2)}) collective-permute-start(f32[128,256]{1,0:T(8,128)S(1)} %fusion.8), channel_id=1, source_target_pairs={{0,8},{1,17},{2,10},{3,19},{4,12},{5,21},{6,14},{7,23},{8,0},{9,25... | collective-permute-start | bytes 393224 | tf_op jit(solution)/shard_map/ppermute | solution.py:534
  165.7 6.7 %collective-permute-start.30 = (f32[128,256]{1,0:T(8,128)S(1)}, f32[128,256]{1,0:T(8,128)S(1)}, u32[]{:S(2)}, u32[]{:S(2)}) collective-permute-start(f32[128,256]{1,0:T(8,128)S(1)} %add.302), channel_id=1, source_target_pairs={{0,16},{1,9},{2,18},{3,11},{4,20},{5,13},{6,22},{7,15},{8,24},{9,1... | collective-permute-start | bytes 393224 | tf_op jit(solution)/shard_map/ppermute | solution.py:535
  168.5 7.0 %collective-permute-start.25 = (f32[128,256]{1,0:T(8,128)S(1)}, f32[128,256]{1,0:T(8,128)S(1)}, u32[]{:S(2)}, u32[]{:S(2)}) collective-permute-start(f32[128,256]{1,0:T(8,128)S(1)} %add.294), channel_id=1, source_target_pairs={{0,16},{1,9},{2,18},{3,11},{4,20},{5,13},{6,22},{7,15},{8,24},{9,1... | collective-permute-start | bytes 393224 | tf_op jit(solution)/shard_map/ppermute | solution.py:534
  173.1 6.2 %collective-permute-start.31 = (f32[128,256]{1,0:T(8,128)S(1)}, f32[128,256]{1,0:T(8,128)S(1)}, u32[]{:S(2)}, u32[]{:S(2)}) collective-permute-start(f32[128,256]{1,0:T(8,128)S(1)} %divide_subtract_fusion.2), channel_id=1, source_target_pairs={{0,4},{1,3},{2,6},{3,1},{4,0},{5,7},{6,2},{7,5},{8,12},{9,11},{10,... | collective-permute-start | bytes 393224 | tf_op jit(solution)/shard_map/ppermute | solution.py:545
  176.2 6.6 %collective-permute-start.26 = (f32[128,256]{1,0:T(8,128)S(1)}, f32[128,256]{1,0:T(8,128)S(1)}, u32[]{:S(2)}, u32[]{:S(2)}) collective-permute-start(f32[128,256]{1,0:T(8,128)S(1)} %divide_subtract_fusion.3), channel_id=1, source_target_pairs={{0,4},{1,3},{2,6},{3,1},{4,0},{5,7},{6,2},{7,5},{8,12},{9,11},{10,... | collective-permute-start | bytes 393224 | tf_op jit(solution)/shard_map/ppermute | solution.py:544
  179.3 6.4 %collective-permute-start.33 = (f32[256,256]{1,0:T(8,128)S(1)}, f32[256,256]{1,0:T(8,128)S(1)}, u32[]{:S(2)}, u32[]{:S(2)}) collective-permute-start(f32[256,256]{1,0:T(8,128)S(1)} %pad_maximum_fusion.14.rest_1_), channel_id=1, source_target_pairs={{0,2},{1,5},{2,0},{3,7},{4,6},{5,1},{6,4},{7,3},{8,10},{9,13},{10,... | collective-permute-start | bytes 786440 | tf_op jit(solution)/shard_map/ppermute | solution.py:546
  182.8 6.4 %collective-permute-start.32 = (f32[256,256]{1,0:T(8,128)S(1)}, f32[256,256]{1,0:T(8,128)S(1)}, u32[]{:S(2)}, u32[]{:S(2)}) collective-permute-start(f32[256,256]{1,0:T(8,128)S(1)} %pad_maximum_fusion.13.rest_0_), channel_id=1, source_target_pairs={{0,2},{1,5},{2,0},{3,7},{4,6},{5,1},{6,4},{7,3},{8,10},{9,13},{10,... | collective-permute-start | bytes 786440 | tf_op jit(solution)/shard_map/ppermute | solution.py:546
  196.6 10.4 %collective-permute-start.44 = (f32[256,256]{1,0:T(8,128)S(1)}, f32[256,256]{1,0:T(8,128)S(1)}, u32[]{:S(2)}, u32[]{:S(2)}) collective-permute-start(f32[256,256]{1,0:T(8,128)S(1)} %get-tuple-element.88.refs_4_), channel_id=1, source_target_pairs={{0,2},{1,5},{2,0},{3,7},{4,6},{5,1},{6,4},{7,3},{8,10},{9,13},{10,... | collective-permute-start | bytes 786440 | tf_op jit(solution)/shard_map/ppermute | solution.py:520
  202.6 7.3 %collective-permute-start.39 = (f32[256,256]{1,0:T(8,128)S(1)}, f32[256,256]{1,0:T(8,128)S(1)}, u32[]{:S(2)}, u32[]{:S(2)}) collective-permute-start(f32[256,256]{1,0:T(8,128)S(1)} %get-tuple-element.89.refs_3_), channel_id=1, source_target_pairs={{0,2},{1,5},{2,0},{3,7},{4,6},{5,1},{6,4},{7,3},{8,10},{9,13},{10,... | collective-permute-start | bytes 786440 | tf_op jit(solution)/shard_map/ppermute | solution.py:519
  207.0 6.0 %collective-permute-start.45 = (f32[128,256]{1,0:T(8,128)S(1)}, f32[128,256]{1,0:T(8,128)S(1)}, u32[]{:S(2)}, u32[]{:S(2)}) collective-permute-start(f32[128,256]{1,0:T(8,128)S(1)} %slice_add_fusion.6), channel_id=1, source_target_pairs={{0,4},{1,3},{2,6},{3,1},{4,0},{5,7},{6,2},{7,5},{8,12},{9,11},{10,... | collective-permute-start | bytes 393224 | tf_op jit(solution)/shard_map/ppermute | solution.py:528
  213.0 15.1 %collective-permute-start.40 = (f32[128,256]{1,0:T(8,128)S(1)}, f32[128,256]{1,0:T(8,128)S(1)}, u32[]{:S(2)}, u32[]{:S(2)}) collective-permute-start(f32[128,256]{1,0:T(8,128)S(1)} %get-tuple-element.87), channel_id=1, source_target_pairs={{0,4},{1,3},{2,6},{3,1},{4,0},{5,7},{6,2},{7,5},{8,12},{9,11},{10,... | collective-permute-start | bytes 393224 | tf_op jit(solution)/shard_map/ppermute | solution.py:527
  220.8 27.3 %collective-permute-start.55 = (f32[2,128,768]{2,1,0:T(8,128)S(1)}, f32[2,128,768]{2,1,0:T(8,128)S(1)}, u32[]{:S(2)}, u32[]{:S(2)}) collective-permute-start(f32[2,128,768]{2,1,0:T(8,128)S(1)} %get-tuple-element.57), channel_id=1, source_target_pairs={{1,0},{2,1},{3,2},{5,4},{6,5},{7,6},{9,8},{10,9},{11,10},{13,12},{... | collective-permute-start | bytes 2359304 | tf_op jit(solution)/shard_map/ppermute | solution.py:455
  222.1 10.4 %collective-permute-start.46 = (f32[128,256]{1,0:T(8,128)S(1)}, f32[128,256]{1,0:T(8,128)S(1)}, u32[]{:S(2)}, u32[]{:S(2)}) collective-permute-start(f32[128,256]{1,0:T(8,128)S(1)} %get-tuple-element.86), channel_id=1, source_target_pairs={{0,8},{1,17},{2,10},{3,19},{4,12},{5,21},{6,14},{7,23},{8,0},{9,25... | collective-permute-start | bytes 393224 | tf_op jit(solution)/shard_map/ppermute | solution.py:535
  228.1 10.3 %collective-permute-start.41 = (f32[128,256]{1,0:T(8,128)S(1)}, f32[128,256]{1,0:T(8,128)S(1)}, u32[]{:S(2)}, u32[]{:S(2)}) collective-permute-start(f32[128,256]{1,0:T(8,128)S(1)} %fusion.6), channel_id=1, source_target_pairs={{0,8},{1,17},{2,10},{3,19},{4,12},{5,21},{6,14},{7,23},{8,0},{9,25... | collective-permute-start | bytes 393224 | tf_op jit(solution)/shard_map/ppermute | solution.py:534
  232.5 9.2 %collective-permute-start.47 = (f32[128,256]{1,0:T(8,128)S(1)}, f32[128,256]{1,0:T(8,128)S(1)}, u32[]{:S(2)}, u32[]{:S(2)}) collective-permute-start(f32[128,256]{1,0:T(8,128)S(1)} %add.318), channel_id=1, source_target_pairs={{0,16},{1,9},{2,18},{3,11},{4,20},{5,13},{6,22},{7,15},{8,24},{9,1... | collective-permute-start | bytes 393224 | tf_op jit(solution)/shard_map/ppermute | solution.py:535
  236.3 11.8 %collective-permute-start.56 = (f32[2,128,768]{2,1,0:T(8,128)S(1)}, f32[2,128,768]{2,1,0:T(8,128)S(1)}, u32[]{:S(2)}, u32[]{:S(2)}) collective-permute-start(f32[2,128,768]{2,1,0:T(8,128)S(1)} %get-tuple-element.58), channel_id=1, source_target_pairs={{0,1},{1,2},{2,3},{4,5},{5,6},{6,7},{8,9},{9,10},{10,11},{12,13},{... | collective-permute-start | bytes 2359304 | tf_op jit(solution)/shard_map/ppermute | solution.py:455
  238.5 7.3 %collective-permute-start.42 = (f32[128,256]{1,0:T(8,128)S(1)}, f32[128,256]{1,0:T(8,128)S(1)}, u32[]{:S(2)}, u32[]{:S(2)}) collective-permute-start(f32[128,256]{1,0:T(8,128)S(1)} %add.310), channel_id=1, source_target_pairs={{0,16},{1,9},{2,18},{3,11},{4,20},{5,13},{6,22},{7,15},{8,24},{9,1... | collective-permute-start | bytes 393224 | tf_op jit(solution)/shard_map/ppermute | solution.py:534
  242.3 5.4 %collective-permute-start.48 = (f32[128,256]{1,0:T(8,128)S(1)}, f32[128,256]{1,0:T(8,128)S(1)}, u32[]{:S(2)}, u32[]{:S(2)}) collective-permute-start(f32[128,256]{1,0:T(8,128)S(1)} %divide_subtract_fusion), channel_id=1, source_target_pairs={{0,4},{1,3},{2,6},{3,1},{4,0},{5,7},{6,2},{7,5},{8,12},{9,11},{10,... | collective-permute-start | bytes 393224 | tf_op jit(solution)/shard_map/ppermute | solution.py:545
  246.5 5.6 %collective-permute-start.43 = (f32[128,256]{1,0:T(8,128)S(1)}, f32[128,256]{1,0:T(8,128)S(1)}, u32[]{:S(2)}, u32[]{:S(2)}) collective-permute-start(f32[128,256]{1,0:T(8,128)S(1)} %divide_subtract_fusion.1), channel_id=1, source_target_pairs={{0,4},{1,3},{2,6},{3,1},{4,0},{5,7},{6,2},{7,5},{8,12},{9,11},{10,... | collective-permute-start | bytes 393224 | tf_op jit(solution)/shard_map/ppermute | solution.py:544
  247.7 10.9 %collective-permute-start.50 = (f32[256,256]{1,0:T(8,128)S(1)}, f32[256,256]{1,0:T(8,128)S(1)}, u32[]{:S(2)}, u32[]{:S(2)}) collective-permute-start(f32[256,256]{1,0:T(8,128)S(1)} %pad_maximum_fusion.16.refs_1_), channel_id=1, source_target_pairs={{0,2},{1,5},{2,0},{3,7},{4,6},{5,1},{6,4},{7,3},{8,10},{9,13},{10,... | collective-permute-start | bytes 786440 | tf_op jit(solution)/shard_map/ppermute | solution.py:546
  248.2 31.4 %collective-permute-start.58 = (f32[2,512,128]{2,1,0:T(8,128)S(1)}, f32[2,512,128]{2,1,0:T(8,128)S(1)}, u32[]{:S(2)}, u32[]{:S(2)}) collective-permute-start(f32[2,512,128]{2,1,0:T(8,128)S(1)} %pad_add_fusion), channel_id=1, source_target_pairs={{0,4},{4,8},{8,12},{12,16},{16,20},{20,24},{24,28},{1,5},{5,9},{9,... | collective-permute-start | bytes 1572872 | tf_op jit(solution)/shard_map/ppermute | solution.py:455
  250.8 28.7 %collective-permute-start.57 = (f32[2,512,128]{2,1,0:T(8,128)S(1)}, f32[2,512,128]{2,1,0:T(8,128)S(1)}, u32[]{:S(2)}, u32[]{:S(2)}) collective-permute-start(f32[2,512,128]{2,1,0:T(8,128)S(1)} %pad_add_fusion.1), channel_id=1, source_target_pairs={{4,0},{8,4},{12,8},{16,12},{20,16},{24,20},{28,24},{5,1},{9,5},{13... | collective-permute-start | bytes 1572872 | tf_op jit(solution)/shard_map/ppermute | solution.py:455
  252.2 6.8 %collective-permute-start.49 = (f32[256,256]{1,0:T(8,128)S(1)}, f32[256,256]{1,0:T(8,128)S(1)}, u32[]{:S(2)}, u32[]{:S(2)}) collective-permute-start(f32[256,256]{1,0:T(8,128)S(1)} %pad_maximum_fusion.15.refs_0_), channel_id=1, source_target_pairs={{0,2},{1,5},{2,0},{3,7},{4,6},{5,1},{6,4},{7,3},{8,10},{9,13},{10,... | collective-permute-start | bytes 786440 | tf_op jit(solution)/shard_map/ppermute | solution.py:546
  254.6 28.3 %collective-permute-start.52 = (f32[256,256]{1,0:T(8,128)S(1)}, f32[256,256]{1,0:T(8,128)S(1)}, u32[]{:S(2)}, u32[]{:S(2)}) collective-permute-start(f32[256,256]{1,0:T(8,128)S(1)} %pad_maximum_fusion.16.refs_1_), channel_id=1, source_target_pairs={{0,1},{1,0},{2,3},{3,2},{4,5},{5,4},{6,7},{7,6},{8,9},{9,8},{10,11... | collective-permute-start | bytes 786440 | tf_op jit(solution)/shard_map/ppermute | solution.py:547
  258.7 24.2 %collective-permute-start.51 = (f32[256,256]{1,0:T(8,128)S(1)}, f32[256,256]{1,0:T(8,128)S(1)}, u32[]{:S(2)}, u32[]{:S(2)}) collective-permute-start(f32[256,256]{1,0:T(8,128)S(1)} %pad_maximum_fusion.15.refs_0_), channel_id=1, source_target_pairs={{0,1},{1,0},{2,3},{3,2},{4,5},{5,4},{6,7},{7,6},{8,9},{9,8},{10,11... | collective-permute-start | bytes 786440 | tf_op jit(solution)/shard_map/ppermute | solution.py:547
  258.9 23.9 %collective-permute-start.54 = (f32[256,256]{1,0:T(8,128)S(1)}, f32[256,256]{1,0:T(8,128)S(1)}, u32[]{:S(2)}, u32[]{:S(2)}) collective-permute-start(f32[256,256]{1,0:T(8,128)S(1)} %collective-permute-done.50.refs_3_), channel_id=1, source_target_pairs={{0,1},{1,0},{2,3},{3,2},{4,5},{5,4},{6,7},{7,6},{8,9},{9,8},{10,11... | collective-permute-start | bytes 786440 | tf_op jit(solution)/shard_map/ppermute | solution.py:547
  (18 other events, 93.9 us)

commit v3 on v2

--- a/solution.py
+++ b/solution.py
@@ -169,30 +169,91 @@
     return row_at, col_at, row - row_at, col - col_at
 
 
+def shift_in(block, row, col):
+    rows, columns = block.shape
+    turn = lax.rem(128 - col, 128)
+    tiles = [pltpu.roll(block[:, at : at + 128], turn, 1) for at in range(0, columns, 128)]
+    here = lax.broadcasted_iota(jnp.int32, (rows, 128), 1) < 128 - col
+    block = jnp.concatenate([jnp.where(here, a, b) for a, b in zip(tiles, tiles[1:])], 1)
+    block = pltpu.roll(block.reshape(rows // 8, 8, columns - 128), lax.rem(8 - row, 8), 1)
+    here = lax.broadcasted_iota(jnp.int32, (rows // 8 - 1, 8, columns - 128), 1) < 8 - row
+    return jnp.where(here, block[:-1], block[1:]).reshape(rows - 8, columns - 128)
+
+
+def shift_out(block, row, col):
+    rows, columns = block.shape
+    block = pltpu.roll(block.reshape(rows // 8, 8, columns), lax.rem(row, 8), 1)
+    zero = jnp.zeros((1, 8, columns), F32)
+    here = lax.broadcasted_iota(jnp.int32, (rows // 8 + 1, 8, columns), 1) >= row
+    block = jnp.where(here, jnp.concatenate([block, zero], 0), jnp.concatenate([zero, block], 0))
+    block = block.reshape(rows + 8, columns)
+    zero = jnp.zeros((rows + 8, 128), F32)
+    tiles = [zero] + [pltpu.roll(block[:, at : at + 128], lax.rem(col, 128), 1) for at in range(0, columns, 128)] + [zero]
+    here = lax.broadcasted_iota(jnp.int32, (rows + 8, 128), 1) >= col
+    return jnp.concatenate([jnp.where(here, b, a) for a, b in zip(tiles, tiles[1:])], 1)
+
+
+def cut_corners(left_side, right_side, after):
+    edge = left_side.shape[1]
+
+    def body(left_ref, right_ref, *rest):
+        leading, last = rest[-2:]
+        for ref, rows in ((leading, slice(0, H)), (last, slice(edge - H, edge))):
+            ref[:, :, :H] = left_ref[:, rows]
+            ref[:, :, H:] = right_ref[:, rows]
+
+    return call(
+        body,
+        [],
+        [left_side, right_side, *after],
+        [whole(2, edge, H)] * 2 + [pl.BlockSpec(memory_space=pl.ANY)] * len(after),
+        [(2, H, 2 * H)] * 2,
+        [whole(2, H, 2 * H)] * 2,
+        1,
+        flops=10**5,
+        moved=2 * 10**6,
+    )
+
+
 def cut_patches(offsets, info, tile, sides, size, slots):
     edge = tile.shape[1]
     full = edge + 2 * H
-
-    def body(offs, info_ref, tile_ref, left_ref, right_ref, top_ref, bottom_ref, out, cover, ext):
+    low, mid, high = slice(0, H), slice(H, H + edge), slice(H + edge, full)
+    first_half, second_half, everything = slice(0, H), slice(H, 2 * H), slice(None)
+    pieces = [
+        (0, everything, mid, mid),
+        (1, everything, mid, low),
+        (2, everything, mid, high),
+        (3, everything, low, mid),
+        (4, everything, high, mid),
+        (5, first_half, low, low),
+        (5, second_half, low, high),
+        (6, first_half, high, low),
+        (6, second_half, high, high),
+    ]
+
+    def body(offs, info_ref, *refs):
+        sources, (out, cover, ext, sems) = refs[:7], refs[7:]
         i = pl.program_id(0)
 
         @pl.when(i == 0)
         def _():
+            copies = [
+                pltpu.make_async_copy(sources[k].at[:, :, part], ext.at[:, rows, columns], sems.at[j])
+                for j, (k, part, rows, columns) in enumerate(pieces)
+            ]
+            for copy in copies:
+                copy.start()
             cover[...] = jnp.zeros_like(cover)
-            ext[:, :H] = top_ref[...]
-            ext[:, H + edge :] = bottom_ref[...]
-            ext[:, H : H + edge, :H] = left_ref[...]
-            ext[:, H : H + edge, H : H + edge] = tile_ref[...]
-            ext[:, H : H + edge, H + edge :] = right_ref[...]
+            for copy in copies:
+                copy.wait()
 
         @pl.when(i < info_ref[0])
         def _():
             row_at, col_at, row, col = corner_of(offs, i, full, size)
             total = jnp.zeros((1, size), F32)
             for part in range(2):
-                block = ext[part, pl.ds(row_at, size + 8), pl.ds(col_at, size + 128)]
-                block = pltpu.roll(block, size + 128 - col, 1)[:, :size]
-                block = pltpu.roll(block, size + 8 - row, 0)[:size]
+                block = shift_in(ext[part, pl.ds(row_at, size + 8), pl.ds(col_at, size + 128)], row, col)
                 out[0, part] = block
                 total = total + jnp.sum(block * block, axis=0, keepdims=True)
             here = lax.broadcasted_iota(jnp.int32, cover.shape, 0) == i // POS
@@ -202,11 +263,11 @@
         body,
         [offsets, info],
         [tile, *sides],
-        [whole(2, edge, edge), whole(2, edge, H), whole(2, edge, H), whole(2, H, full), whole(2, H, full)],
+        [pl.BlockSpec(memory_space=pl.ANY)] * 7,
         [(slots, 2, size, size), (8, size)],
         [per_slot(2, size, size), whole(8, size)],
         slots,
-        scratch=[pltpu.VMEM((2, full, full), F32)],
+        scratch=[pltpu.VMEM((2, full, full), F32), pltpu.SemaphoreType.DMA((len(pieces),))],
         flops=10**6,
         moved=8 * 10**6,
     )
@@ -231,11 +292,7 @@
             def _():
                 row_at, col_at, row, col = corner_of(offs, i, full, size)
                 for part in range(2):
-                    block = patch_refs[batch][0, part]
-                    block = jnp.concatenate([block, jnp.zeros((8, size), F32)], 0)
-                    block = pltpu.roll(block, row, 0)
-                    block = jnp.concatenate([block, jnp.zeros((size + 8, 128), F32)], 1)
-                    block = pltpu.roll(block, col, 1)
+                    block = shift_out(patch_refs[batch][0, part], row, col)
                     ext[part, pl.ds(row_at, size + 8), pl.ds(col_at, size + 128)] += block
 
         @pl.when(i == n * POS - 1)
@@ -264,28 +321,27 @@
     )
 
 
-def merge_borders(core, from_right, from_left, from_below, from_above):
-    edge = core.shape[1]
-
-    def body(g, fr, fl, fb, fa, out):
-        out[...] = g[...]
-        out[:, edge - H :] += fb[:, :, H : H + edge]
-        out[:, :H] += fa[:, :, H : H + edge]
-        out[:, :, edge - H :] += fr[...]
-        out[:, :, :H] += fl[...]
-
-    operands = [core, from_right, from_left, from_below, from_above]
+def side_borders(left_part, right_part, from_below, from_above, after):
+    edge = left_part.shape[1]
+    full = from_below.shape[2]
+
+    def body(left_ref, right_ref, below, above, *rest):
+        for ref, out, at in ((left_ref, rest[-2], 0), (right_ref, rest[-1], H + edge)):
+            out[...] = ref[...]
+            out[:, edge - H :] += below[:, :, at : at + H]
+            out[:, :H] += above[:, :, at : at + H]
+
     return call(
         body,
         [],
-        operands,
-        [whole(*x.shape) for x in operands],
-        [core.shape],
-        [whole(*core.shape)],
+        [left_part, right_part, from_below, from_above, *after],
+        [whole(2, edge, H)] * 2 + [whole(2, H, full)] * 2 + [pl.BlockSpec(memory_space=pl.ANY)] * len(after),
+        [(2, edge, H)] * 2,
+        [whole(2, edge, H)] * 2,
         1,
-        flops=10**6,
-        moved=10**7,
-    )[0]
+        flops=10**5,
+        moved=4 * 10**6,
+    )
 
 
 def turn_kernel(tables, info, patches, probes, roots, cover, batch):
@@ -350,55 +406,52 @@
     )
 
 
-def back_kernel(tables, info, patches, probes, spectra, keep, gpatch, batch):
+def back_kernel(tables, info, patches, probe, spectra, keep, gpatch, batch, mode, after):
     size = patches.shape[-1]
     h = size // 2
 
-    def body(info_ref, t, patch, z, k, g_in, *rest):
-        p, (g0, g1, g_out) = rest[:4], rest[4:]
+    def body(info_ref, t, patch, z, k, g_in, p_re, p_im, *rest):
+        pgrad, g_out = rest[len(after) :]
         i = pl.program_id(0)
 
         @pl.when(i == 0)
         def _():
-            g0[...] = jnp.zeros_like(g0)
-            g1[...] = jnp.zeros_like(g1)
+            pgrad[...] = jnp.zeros_like(pgrad)
 
         g_out[...] = g_in[...]
 
         @pl.when(batch * POS + i < info_ref[0])
         def _():
             bit = info_ref[2]
-            for m, out in ((1, g1), (0, g0)):
-                probe = (rows_of(p[2 * m], bit), rows_of(p[2 * m + 1], bit))
-                gradients(t, patch, probe, (z[0, m, 0], z[0, m, 1]), k, out, 0, bit, g_out)
+            pair = (rows_of(p_re, bit), rows_of(p_im, bit))
+            gradients(t, patch, pair, (z[0, 0, 0], z[0, 0, 1]), k, pgrad, 0, bit, g_out)
 
     return call(
         body,
         [info],
-        [tables, patches, spectra, keep, gpatch, *probes[:4]],
+        [tables, patches, spectra, keep, gpatch, *probe, *after],
         [
             whole(*tables.shape),
             per_batch_slot(batch, 2, size, size),
-            per_slot(2, 2, size, size),
+            pl.BlockSpec((1, 1, 2, size, size), lambda i, *_: (i, mode, 0, 0, 0)),
             per_slot(2, size, h),
             per_slot(2, size, size),
         ]
-        + [whole(size, size)] * 4,
-        [(2 * size, size), (2 * size, size), (POS, 2, size, size)],
-        [whole(2 * size, size), whole(2 * size, size), per_slot(2, size, size)],
+        + [whole(size, size)] * 2
+        + [pl.BlockSpec(memory_space=pl.ANY)] * len(after),
+        [(2 * size, size), (POS, 2, size, size)],
+        [whole(2 * size, size), per_slot(2, size, size)],
         POS,
-        flops=POS * 2 * 24 * size**3,
-        moved=6 * 10**6,
-    )
-
-
-def finish_kernel(info, probes, field, inner):
+        flops=POS * 24 * size**3,
+        moved=4 * 10**6,
+    )
+
+
+def probe_kernel(info, probes):
     size = probes[0].shape[0]
-    edge = field.shape[1]
-    chunk = edge // 4
 
     def body(info_ref, *refs):
-        p, (o, g, probe_out, object_out, power) = refs[:8], refs[8:]
+        p, (probe_out, top, power) = refs[:8], refs[8:]
         i = pl.program_id(0)
         for m in range(4):
 
@@ -410,24 +463,57 @@
                 square = re * re + im * im
                 power[...] = square if m == 0 else power[...] + square
 
-        @pl.when(i >= 4)
-        def _():
-            top = jnp.max(power[...], keepdims=True)
-            object_out[...] = o[...] - g[...] * (0.5 / top)[None]
-
-    spec = pl.BlockSpec((2, chunk, edge), lambda i, *_: (0, jnp.maximum(i - 4, 0), 0))
+        @pl.when(i == 3)
+        def _():
+            top[...] = jnp.broadcast_to(jnp.max(power[...], keepdims=True), top.shape)
+
     return call(
         body,
         [info],
-        [*probes, field, inner],
-        [whole(size, size)] * 8 + [spec, spec],
-        [(4, 2, size, size), field.shape],
-        [pl.BlockSpec((1, 2, size, size), lambda i, info_ref: (info_ref[3 + jnp.minimum(i, 3)], 0, 0, 0)), spec],
-        8,
+        probes,
+        [whole(size, size)] * 8,
+        [(4, 2, size, size), (8, 128)],
+        [pl.BlockSpec((1, 2, size, size), lambda i, info_ref: (info_ref[3 + i], 0, 0, 0)), whole(8, 128)],
+        4,
         scratch=[pltpu.VMEM((size, size), F32)],
         flops=10**6,
-        moved=10**7,
-    )
+        moved=4 * 10**6,
+    )
+
+
+def object_kernel(top, field, core, from_right, from_left, from_below, from_above):
+    edge = field.shape[1]
+    full = from_below.shape[2]
+    steps = edge // H
+
+    def body(top_ref, o, g, fr, fl, fb, fa, out):
+        i = pl.program_id(0)
+        step = (0.5 / top_ref[:1, :1])[None]
+        out[...] = o[...] - step * g[...]
+        out[:, :, edge - H :] -= step * fr[...]
+        out[:, :, :H] -= step * fl[...]
+
+        @pl.when(i == steps - 1)
+        def _():
+            out[...] -= step * fb[:, :, H : H + edge]
+
+        @pl.when(i == 0)
+        def _():
+            out[...] -= step * fa[:, :, H : H + edge]
+
+    band = pl.BlockSpec((2, H, edge), lambda i: (0, i, 0))
+    side = pl.BlockSpec((2, H, H), lambda i: (0, i, 0))
+    return call(
+        body,
+        [],
+        [top, field, core, from_right, from_left, from_below, from_above],
+        [whole(8, 128), band, band, side, side, whole(2, H, full), whole(2, H, full)],
+        [field.shape],
+        [band],
+        steps,
+        flops=10**6,
+        moved=8 * 10**6,
+    )[0]
 
 
 def flips(wide, narrow):
@@ -467,12 +553,8 @@
 
     left_side = shifted(object_field[:, :, edge - H :], "wide", 1)
     right_side = shifted(object_field[:, :, :H], "wide", -1)
-
-    def strip(lo):
-        return jnp.concatenate([x[:, lo : lo + H] for x in (left_side, object_field, right_side)], 2)
-
-    top_side = shifted(strip(edge - H), "narrow", 1)
-    bottom_side = shifted(strip(0), "narrow", -1)
+    top_side = shifted(object_field[:, edge - H :], "narrow", 1)
+    bottom_side = shifted(object_field[:, :H], "narrow", -1)
 
     tables = jnp.asarray(dft_tables(size))
     order = np.concatenate([np.arange(0, size, 2), np.arange(1, size, 2)])
@@ -496,7 +578,10 @@
             other = lax.dynamic_slice(split_rows, (m, part, 1 - bit, 0, 0), (1, 1, 1, h, size))
             probes.append(jnp.concatenate([mine.reshape(h, size), other.reshape(h, size)], 0))
 
-    sides = (left_side, right_side, top_side, bottom_side)
+    leading, last = cut_corners(left_side, right_side, (roots, *probes))
+    top_corners = shifted(last, "narrow", 1)
+    bottom_corners = shifted(leading, "narrow", -1)
+    sides = (left_side, right_side, top_side, bottom_side, top_corners, bottom_corners)
     patches, cover = cut_patches(offs, info, object_field, sides, size, slots)
 
     patch_gradients = []
@@ -508,16 +593,15 @@
 
         sent, keep, gpatch, z = turn_kernel(tables, info, patches, probes, roots, extra, batch)
         got = core(sent)
-        g0, g1, gpatch = back_kernel(tables, info, patches, probes, z, keep, gpatch, batch)
-        patch_gradients.append(gpatch)
+        g1, gpatch = back_kernel(tables, info, patches, probes[2:4], z, keep, gpatch, batch, 1, ())
         if extra is not None:
             extra = extra + got[4 * size :]
         sent_a = g1[:size] + got[2 * size : 3 * size]
         sent_b = g1[size:] + got[3 * size : 4 * size]
-        if batch == BATCHES - 1:
-            placed = place_gradients(offs, info, patch_gradients, (sent_a, sent_b), edge)
         got_a = first(ride(sent_a))
         got_b = first(sent_b)
+        g0, gpatch = back_kernel(tables, info, patches, probes[:2], z, keep, gpatch, batch, 0, (sent_a, sent_b))
+        patch_gradients.append(gpatch)
         sent_a = g0[h:size] + got[h:size] + got_a[h:size]
         sent_b = g0[size + h :] + got[size + h : 2 * size] + got_b[h:]
         a = g0[:h] + got[:h] + got_a[:h]
@@ -530,6 +614,10 @@
         b = b + got_b
         if extra is not None:
             extra = extra + got_a[h:]
+        if batch == BATCHES - 1:
+            inside, upper, lower, left_part, right_part = place_gradients(offs, info, patch_gradients, (a, b), edge)
+            from_below = shifted(upper, "narrow", -1)
+            from_above = shifted(lower, "narrow", 1)
         for exchange in rest:
             got_a = exchange(ride(a))
             got_b = exchange(b)
@@ -546,19 +634,11 @@
         own = [a, b, first(a), first(b)]
         probes = own + [core(x) for x in own]
 
-    inside, upper, lower, left_part, right_part = placed
-    from_below = shifted(upper, "narrow", -1)
-    from_above = shifted(lower, "narrow", 1)
-
-    def border(part, lo):
-        below = jnp.pad(from_below[:, :, lo : lo + H], ((0, 0), (edge - H, 0), (0, 0)))
-        above = jnp.pad(from_above[:, :, lo : lo + H], ((0, 0), (0, edge - H), (0, 0)))
-        return part + below + above
-
-    from_right = shifted(border(left_part, 0), "wide", -1)
-    from_left = shifted(border(right_part, H + edge), "wide", 1)
-    inner = merge_borders(inside, from_right, from_left, from_below, from_above)
-    probe_new, object_new = finish_kernel(info, probes, object_field, inner)
+    to_left, to_right = side_borders(left_part, right_part, from_below, from_above, own[2:])
+    from_right = shifted(to_left, "wide", -1)
+    from_left = shifted(to_right, "wide", 1)
+    probe_new, top = probe_kernel(info, probes)
+    object_new = object_kernel(top, object_field, inside, from_right, from_left, from_below, from_above)
     return (object_new, probe_new)
 
 

time: 293 us -> 279 us (0.952)
  waiting for transfers between devices: 101 us -> 86 us
  starting transfers between devices: 110 us -> 98 us
  Pallas kernels: 56.9 us -> 66.8 us
    ppermute x12, starting transfers between devices: 25.8 us -> 1.68 us  [local(): probes = own + [core(x) for x in own]]
    ppermute x6, waiting for transfers between devices: 20.2 us -> 9.7 us  [local(): got_b = exchange(b)]
    ppermute x3, waiting for transfers between devices: 12.8 us -> 2.58 us  [local(): got_b = first(sent_b)]
    pallas_call x10 -> x15, Pallas kernels: 56.9 us -> 66.8 us  [call(): pl.pallas_call(body, out_shape=[jax.ShapeDtypeStruct(s, F32) for s in out...]
    ppermute x8 -> x10, starting transfers between devices: 18.5 us -> 27.8 us  [shifted(): lax.ppermute(value, axis, [(source, source + steps) for source in range(l...]
    ppermute x6, starting transfers between devices: 4.51 us -> 11.3 us  [local(): own = [a, b, first(a), first(b)]]
    ppermute x3, starting transfers between devices: 4.64 us -> 0.18 us  [local(): got = core(sent)]
    ppermute x3, starting transfers between devices: 8.99 us -> 13.2 us  [local(): got_b = first(sent_b)]
  transfers between devices with their start and end apart: 59 -> 61, of which waited for: 29 -> 37; matrix products, arithmetic and copies ran while one was open for 6% -> 7% of each run, Pallas kernels for 7% -> 11%
where the time goes in v3:
time: 279 us; the launch traced here: 277 us
  starting transfers between devices  98 us (35%)
  waiting for transfers between devices  86 us (31%)
  Pallas kernels  66.8 us (24%)
  local copies, waits for them, and re-layouts  10.9 us (4%)
  other arithmetic  7.67 us (3%)
  matrix products  5.9 us (2%)
    pallas_call x15, Pallas kernels, call(): pl.pallas_call(body, out_shape=[jax.ShapeDtypeStruct(s, F32) for s in out...  66.8 us
    ppermute x10, starting transfers between devices, shifted(): lax.ppermute(value, axis, [(source, source + steps) for source in range(l...  27.8 us
    ppermute x10, waiting for transfers between devices, shifted(): lax.ppermute(value, axis, [(source, source + steps) for source in range(l...  17.4 us
    ppermute x6, waiting for transfers between devices, local(): own = [a, b, first(a), first(b)]  14.2 us
    ppermute x3, starting transfers between devices, local(): got_b = first(sent_b)  13.2 us
    ppermute x6, waiting for transfers between devices, local(): got_a = exchange(ride(a))  11.8 us
    ppermute x3, starting transfers between devices, local(): got_b = second(sent_b)  11.5 us
    ppermute x6, starting transfers between devices, local(): own = [a, b, first(a), first(b)]  11.3 us
  transfers between devices with their start and end apart: 61, of which 37 were waited for; matrix products, arithmetic and copies ran while one was open for 7% of the time, Pallas kernels for 11%

profile of v3, /device:TPU:0, one launch (start us, length us, event | category | flops | bytes accessed | tf_op | source)
XLA Modules:
  0.0 277.0 jit_solution(8682542156041046218)
XLA Ops:
  0.6 2.4 fusion.14
  4.5 6.3 %collective-permute-start = (f32[2,512,128]{2,1,0:T(8,128)}, f32[2,512,128]{2,1,0:T(8,128)}, u32[]{:S(2)}, u32[]{:S(2)}) collective-permute-start(f32[2,512,128]{2,1,0:T(8,128)} %get-tuple-element.95), channel_id=1, source_target_pairs={{0,4},{4,8},{8,12},{12,16},{16,20},{20,24},{24,28},{1,5},{5,9},{9,... | collective-permute-start | bytes 1572872 | tf_op jit(solution)/shard_map/ppermute | solution.py:541
  13.2 3.8 %collective-permute-start.2 = (f32[2,128,512]{2,1,0:T(8,128)}, f32[2,128,512]{2,1,0:T(8,128)}, u32[]{:S(2)}, u32[]{:S(2)}) collective-permute-start(f32[2,128,512]{2,1,0:T(8,128)} %get-tuple-element.93), channel_id=1, source_target_pairs={{0,1},{1,2},{2,3},{4,5},{5,6},{6,7},{8,9},{9,10},{10,11},{12,13},{... | collective-permute-start | bytes 1572872 | tf_op jit(solution)/shard_map/ppermute | solution.py:541
  17.0 3.2 %fusion.2 = f32[256,6,256]{2,0,1:T(8,128)S(1)} fusion(f32[256,256,1]{1,0,2:T(8,128)S(1)} %copy-done.10, f32[1,1,6,256,256]{4,3,2,1,0:T(8,128)} %param.9), kind=kOutput, calls=%fused_computation.2 | convolution fusion | flops 1207959552 | bytes 3407872 | tf_op jit(solution)/shard_map/pj,sjk->spk/dot_general | solution.py:562
  20.2 2.7 fusion
  22.9 2.5 dynamic-slice_bitcast_fusion.1
  27.0 3.0 %copy.11 = f32[6,256,2,128]{3,1,2,0:T(8,128)} copy(f32[6,256,2,128]{1,3,2,0:T(8,128)} %bitcast.59) | data formatting | bytes 3145728 | tf_op jit(solution)/shard_map/reshape | solution.py:564
  34.7 3.5 %collective-permute-start.4 = (f32[2,128,256]{2,1,0:T(8,128)}, f32[2,128,256]{2,1,0:T(8,128)}, u32[]{:S(2)}, u32[]{:S(2)}) collective-permute-start(f32[2,128,256]{2,1,0:T(8,128)} %get-tuple-element.39), channel_id=1, source_target_pairs={{0,1},{1,2},{2,3},{4,5},{5,6},{6,7},{8,9},{9,10},{10,11},{12,13},{... | collective-permute-start | bytes 786440 | tf_op jit(solution)/shard_map/ppermute | solution.py:541
  42.0 6.0 %shard_map.87 = (f32[6,2,256,256]{3,2,1,0:T(8,128)}, f32[8,256]{1,0:T(8,128)S(1)}) custom-call(s32[12]{0:T(128)S(1)} %reshape.64.offs, s32[7]{0:T(128)S(1)} %stack.27.info_ref, f32[2,512,512]{2,1,0:T(8,128)S(1)} %copy-done.1, f32[2,512,128]{2,1,0:T(8,128)} %collective-permute-done.left_ref.refs_1_, f32[2,512,128]{2,1,0:T(8,128)} %collective-permute-done.1.right_ref.refs_2_, ...), custom_call_target="tpu_custom_call" | custom-call | flops 1000000 | bytes 8000000 | tf_op jit(solution)/shard_map/pallas_call | solution.py:148
  48.1 11.9 %shard_map.88 = (f32[1032,256]{1,0:T(8,128)S(1)}, f32[2,2,256,128]{3,2,1,0:T(8,128)S(1)}, f32[2,2,256,256]{3,2,1,0:T(8,128)S(1)}, f32[2,2,2,256,256]{4,3,2,1,0:T(8,128)}) custom-call(s32[7]{0:T(128)S(1)} %stack.27.info_ref, bf16[4,2,256,256]{3,2,1,0:T(8,128)(2,1)S(1)} %copy-done, f32[6,2,256,256]{3,2,1,0:T(8,128)} %get-tuple-element.41.patch, ...), custom_call_target="tpu_custom_call" | custom-call | flops 4831838208 | bytes 8000000 | tf_op jit(solution)/shard_map/pallas_call | solution.py:148
  60.1 4.0 %shard_map.89 = (f32[512,256]{1,0:T(8,128)S(1)}, f32[2,2,256,256]{3,2,1,0:T(8,128)S(1)}) custom-call(s32[7]{0:T(128)S(1)} %stack.27.info_ref, bf16[4,2,256,256]{3,2,1,0:T(8,128)(2,1)S(1)} %copy-done, f32[6,2,256,256]{3,2,1,0:T(8,128)} %get-tuple-element.41.patch, f32[2,2,2,256,256]{4,3,2,1,0:T(8,128)} %get-tuple-element.43.z, ...), custom_call_target="tpu_custom_call" | custom-call | flops 805306368 | bytes 4000000 | tf_op jit(solution)/shard_map/pallas_call | solution.py:148
  64.2 4.6 %collective-permute-start.12 = (f32[256,256]{1,0:T(8,128)S(1)}, f32[256,256]{1,0:T(8,128)S(1)}, u32[]{:S(2)}, u32[]{:S(2)}) collective-permute-start(f32[256,256]{1,0:T(8,128)S(1)} %get-tuple-element.98.rest_1_), channel_id=1, source_target_pairs={{0,2},{1,5},{2,0},{3,7},{4,6},{5,1},{6,4},{7,3},{8,10},{9,13},{10,... | collective-permute-start | bytes 786440 | tf_op jit(solution)/shard_map/ppermute | solution.py:602
  69.0 4.0 %shard_map.90 = (f32[512,256]{1,0:T(8,128)S(1)}, f32[2,2,256,256]{3,2,1,0:T(8,128)S(1)}) custom-call(s32[7]{0:T(128)S(1)} %stack.27.info_ref, bf16[4,2,256,256]{3,2,1,0:T(8,128)(2,1)S(1)} %copy-done, f32[6,2,256,256]{3,2,1,0:T(8,128)} %get-tuple-element.41.patch, f32[2,2,2,256,256]{4,3,2,1,0:T(8,128)} %get-tuple-element.43.z, ...), custom_call_target="tpu_custom_call" | custom-call | flops 805306368 | bytes 4000000 | tf_op jit(solution)/shard_map/pallas_call | solution.py:148
  73.2 4.0 %collective-permute-start.13 = (f32[128,256]{1,0:T(8,128)S(1)}, f32[128,256]{1,0:T(8,128)S(1)}, u32[]{:S(2)}, u32[]{:S(2)}) collective-permute-start(f32[128,256]{1,0:T(8,128)S(1)} %slice_add_fusion.22), channel_id=1, source_target_pairs={{0,4},{1,3},{2,6},{3,1},{4,0},{5,7},{6,2},{7,5},{8,12},{9,11},{10,... | collective-permute-start | bytes 393224 | tf_op jit(solution)/shard_map/ppermute | solution.py:612
  77.2 2.9 %collective-permute-done.13 = f32[128,256]{1,0:T(8,128)S(1)} collective-permute-done((f32[128,256]{1,0:T(8,128)S(1)}, f32[128,256]{1,0:T(8,128)S(1)}, u32[]{:S(2)}, u32[]{:S(2)}) %collective-permute-start.13) | collective-permute-done | bytes 131104 | tf_op jit(solution)/shard_map/ppermute | solution.py:612
  82.4 3.0 %collective-permute-done.8 = f32[136,256]{1,0:T(8,128)S(1)} collective-permute-done((f32[136,256]{1,0:T(8,128)S(1)}, f32[136,256]{1,0:T(8,128)S(1)}, u32[]{:S(2)}, u32[]{:S(2)}) %collective-permute-start.8) | collective-permute-done | bytes 139296 | tf_op jit(solution)/shard_map/ppermute | solution.py:611
  87.5 3.1 %collective-permute-done.9 = f32[136,256]{1,0:T(8,128)S(1)} collective-permute-done((f32[136,256]{1,0:T(8,128)S(1)}, f32[136,256]{1,0:T(8,128)S(1)}, u32[]{:S(2)}, u32[]{:S(2)}) %collective-permute-start.9) | collective-permute-done | bytes 139296 | tf_op jit(solution)/shard_map/ppermute | solution.py:622
  93.8 4.1 %collective-permute-done.14 = f32[128,256]{1,0:T(8,128)S(1)} collective-permute-done((f32[128,256]{1,0:T(8,128)S(1)}, f32[128,256]{1,0:T(8,128)S(1)}, u32[]{:S(2)}, u32[]{:S(2)}) %collective-permute-start.14) | collective-permute-done | bytes 131104 | tf_op jit(solution)/shard_map/ppermute | solution.py:623
  97.9 2.6 collective-permute-start.15
  102.0 2.1 collective-permute-start.11
  107.0 2.4 collective-permute-start.17
  109.4 2.9 %collective-permute-done.16 = f32[128,256]{1,0:T(8,128)S(1)} collective-permute-done((f32[128,256]{1,0:T(8,128)S(1)}, f32[128,256]{1,0:T(8,128)S(1)}, u32[]{:S(2)}, u32[]{:S(2)}) %collective-permute-start.16) | collective-permute-done | bytes 131104 | tf_op jit(solution)/shard_map/ppermute | solution.py:633
  114.2 4.6 %collective-permute-done.18.rest_3_.p_im = f32[256,256]{1,0:T(8,128)S(1)} collective-permute-done((f32[256,256]{1,0:T(8,128)S(1)}, f32[256,256]{1,0:T(8,128)S(1)}, u32[]{:S(2)}, u32[]{:S(2)}) %collective-permute-start.18) | collective-permute-done | bytes 262176 | tf_op jit(solution)/shard_map/ppermute | solution.py:634
  120.3 12.4 %shard_map.91 = (f32[1024,256]{1,0:T(8,128)S(1)}, f32[2,2,256,128]{3,2,1,0:T(8,128)S(1)}, f32[2,2,256,256]{3,2,1,0:T(8,128)S(1)}, f32[2,2,2,256,256]{4,3,2,1,0:T(8,128)}) custom-call(s32[7]{0:T(128)S(1)} %stack.27.info_ref, bf16[4,2,256,256]{3,2,1,0:T(8,128)(2,1)S(1)} %copy-done, f32[6,2,256,256]{3,2,1,0:T(8,128)} %get-tuple-element.41.patch, ...), custom_call_target="tpu_custom_call" | custom-call | flops 4831838208 | bytes 8000000 | tf_op jit(solution)/shard_map/pallas_call | solution.py:148
  132.7 4.3 %shard_map.92 = (f32[512,256]{1,0:T(8,128)S(1)}, f32[2,2,256,256]{3,2,1,0:T(8,128)S(1)}) custom-call(s32[7]{0:T(128)S(1)} %stack.27.info_ref, bf16[4,2,256,256]{3,2,1,0:T(8,128)(2,1)S(1)} %copy-done, f32[6,2,256,256]{3,2,1,0:T(8,128)} %get-tuple-element.41.patch, f32[2,2,2,256,256]{4,3,2,1,0:T(8,128)} %get-tuple-element.50.z, ...), custom_call_target="tpu_custom_call" | custom-call | flops 805306368 | bytes 4000000 | tf_op jit(solution)/shard_map/pallas_call | solution.py:148
  139.2 4.1 %shard_map.93 = (f32[512,256]{1,0:T(8,128)S(1)}, f32[2,2,256,256]{3,2,1,0:T(8,128)S(1)}) custom-call(s32[7]{0:T(128)S(1)} %stack.27.info_ref, bf16[4,2,256,256]{3,2,1,0:T(8,128)(2,1)S(1)} %copy-done, f32[6,2,256,256]{3,2,1,0:T(8,128)} %get-tuple-element.41.patch, f32[2,2,2,256,256]{4,3,2,1,0:T(8,128)} %get-tuple-element.50.z, ...), custom_call_target="tpu_custom_call" | custom-call | flops 805306368 | bytes 4000000 | tf_op jit(solution)/shard_map/pallas_call | solution.py:148
  156.3 2.9 %collective-permute-start.32 = (f32[128,256]{1,0:T(8,128)S(1)}, f32[128,256]{1,0:T(8,128)S(1)}, u32[]{:S(2)}, u32[]{:S(2)}) collective-permute-start(f32[128,256]{1,0:T(8,128)S(1)} %add.282), channel_id=1, source_target_pairs={{0,16},{1,9},{2,18},{3,11},{4,20},{5,13},{6,22},{7,15},{8,24},{9,1... | collective-permute-start | bytes 393224 | tf_op jit(solution)/shard_map/ppermute | solution.py:623
  165.1 2.6 collective-permute-done.27
  169.6 3.2 %collective-permute-start.35 = (f32[256,256]{1,0:T(8,128)S(1)}, f32[256,256]{1,0:T(8,128)S(1)}, u32[]{:S(2)}, u32[]{:S(2)}) collective-permute-start(f32[256,256]{1,0:T(8,128)S(1)} %pad_maximum_fusion.12.rest_1_.p_im), channel_id=1, source_target_pairs={{0,2},{1,5},{2,0},{3,7},{4,6},{5,1},{6,4},{7,3},{8,10},{9,13},{10,... | collective-permute-start | bytes 786440 | tf_op jit(solution)/shard_map/ppermute | solution.py:634
  174.9 2.3 collective-permute-start.34
  177.7 3.8 %collective-permute-done.34.rest_2_.p_re = f32[256,256]{1,0:T(8,128)S(1)} collective-permute-done((f32[256,256]{1,0:T(8,128)S(1)}, f32[256,256]{1,0:T(8,128)S(1)}, u32[]{:S(2)}, u32[]{:S(2)}) %collective-permute-start.34) | collective-permute-done | bytes 262176 | tf_op jit(solution)/shard_map/ppermute | solution.py:634
  183.1 3.1 %shard_map.94 = (f32[1024,256]{1,0:T(8,128)S(1)}, f32[2,2,256,128]{3,2,1,0:T(8,128)S(1)}, f32[2,2,256,256]{3,2,1,0:T(8,128)S(1)}, f32[2,2,2,256,256]{4,3,2,1,0:T(8,128)}) custom-call(s32[7]{0:T(128)S(1)} %stack.27.info_ref, bf16[4,2,256,256]{3,2,1,0:T(8,128)(2,1)S(1)} %copy-done, f32[6,2,256,256]{3,2,1,0:T(8,128)} %get-tuple-element.41.patch, ...), custom_call_target="tpu_custom_call" | custom-call | flops 4831838208 | bytes 8000000 | tf_op jit(solution)/shard_map/pallas_call | solution.py:148
  186.3 2.1 shard_map.95
  188.9 7.2 %collective-permute-start.46 = (f32[256,256]{1,0:T(8,128)S(1)}, f32[256,256]{1,0:T(8,128)S(1)}, u32[]{:S(2)}, u32[]{:S(2)}) collective-permute-start(f32[256,256]{1,0:T(8,128)S(1)} %get-tuple-element.102.rest_1_), channel_id=1, source_target_pairs={{0,2},{1,5},{2,0},{3,7},{4,6},{5,1},{6,4},{7,3},{8,10},{9,13},{10,... | collective-permute-start | bytes 786440 | tf_op jit(solution)/shard_map/ppermute | solution.py:602
  196.2 2.1 shard_map.96
  198.4 2.1 collective-permute-done.46
  200.5 6.0 %collective-permute-start.47 = (f32[128,256]{1,0:T(8,128)S(1)}, f32[128,256]{1,0:T(8,128)S(1)}, u32[]{:S(2)}, u32[]{:S(2)}) collective-permute-start(f32[128,256]{1,0:T(8,128)S(1)} %slice_add_fusion.6), channel_id=1, source_target_pairs={{0,4},{1,3},{2,6},{3,1},{4,0},{5,7},{6,2},{7,5},{8,12},{9,11},{10,... | collective-permute-start | bytes 393224 | tf_op jit(solution)/shard_map/ppermute | solution.py:612
  206.5 2.9 %collective-permute-done.47 = f32[128,256]{1,0:T(8,128)S(1)} collective-permute-done((f32[128,256]{1,0:T(8,128)S(1)}, f32[128,256]{1,0:T(8,128)S(1)}, u32[]{:S(2)}, u32[]{:S(2)}) %collective-permute-start.47) | collective-permute-done | bytes 131104 | tf_op jit(solution)/shard_map/ppermute | solution.py:612
  219.1 3.7 %shard_map.98 = (f32[2,512,512]{2,1,0:T(8,128)}, f32[2,128,768]{2,1,0:T(8,128)S(1)}, f32[2,128,768]{2,1,0:T(8,128)S(1)}, f32[2,512,128]{2,1,0:T(8,128)S(1)}, f32[2,512,128]{2,1,0:T(8,128)S(1)}) custom-call(s32[12]{0:T(128)S(1)} %reshape.64.offs, s32[7]{0:T(128)S(1)} %stack.27.info_ref, f32[2,2,256,256]{3,2,1,0:T(8,128)S(1)} %get-tuple-element.65.refs_0_, ...), custom_call_target="tpu_custom_call" | custom-call | flops 1000000 | bytes 10000000 | tf_op jit(solution)/shard_map/pallas_call | solution.py:148
  224.0 3.1 %collective-permute-start.58 = (f32[2,128,768]{2,1,0:T(8,128)S(1)}, f32[2,128,768]{2,1,0:T(8,128)S(1)}, u32[]{:S(2)}, u32[]{:S(2)}) collective-permute-start(f32[2,128,768]{2,1,0:T(8,128)S(1)} %get-tuple-element.72), channel_id=1, source_target_pairs={{0,1},{1,2},{2,3},{4,5},{5,6},{6,7},{8,9},{9,10},{10,11},{12,13},{... | collective-permute-start | bytes 2359304 | tf_op jit(solution)/shard_map/ppermute | solution.py:541
  229.5 4.8 %collective-permute-done.44 = f32[128,256]{1,0:T(8,128)S(1)} collective-permute-done((f32[128,256]{1,0:T(8,128)S(1)}, f32[128,256]{1,0:T(8,128)S(1)}, u32[]{:S(2)}, u32[]{:S(2)}) %collective-permute-start.44) | collective-permute-done | bytes 131104 | tf_op jit(solution)/shard_map/ppermute | solution.py:622
  236.6 3.4 %collective-permute-done.45 = f32[128,256]{1,0:T(8,128)S(1)} collective-permute-done((f32[128,256]{1,0:T(8,128)S(1)}, f32[128,256]{1,0:T(8,128)S(1)}, u32[]{:S(2)}, u32[]{:S(2)}) %collective-permute-start.45) | collective-permute-done | bytes 131104 | tf_op jit(solution)/shard_map/ppermute | solution.py:632
  241.5 4.9 %collective-permute-done.51.refs_2_.rest_0_ = f32[256,256]{1,0:T(8,128)S(1)} collective-permute-done((f32[256,256]{1,0:T(8,128)S(1)}, f32[256,256]{1,0:T(8,128)S(1)}, u32[]{:S(2)}, u32[]{:S(2)}) %collective-permute-start.51) | collective-permute-done | bytes 262176 | tf_op jit(solution)/shard_map/ppermute | solution.py:634
  247.8 4.6 %collective-permute-start.60 = (f32[2,512,128]{2,1,0:T(8,128)S(1)}, f32[2,512,128]{2,1,0:T(8,128)S(1)}, u32[]{:S(2)}, u32[]{:S(2)}) collective-permute-start(f32[2,512,128]{2,1,0:T(8,128)S(1)} %get-tuple-element.74), channel_id=1, source_target_pairs={{0,4},{4,8},{8,12},{12,16},{16,20},{20,24},{24,28},{1,5},{5,9},{9,... | collective-permute-start | bytes 1572872 | tf_op jit(solution)/shard_map/ppermute | solution.py:541
  254.7 2.7 shard_map.97
  257.4 4.2 %collective-permute-done.59.fr = f32[2,512,128]{2,1,0:T(8,128)S(1)} collective-permute-done((f32[2,512,128]{2,1,0:T(8,128)S(1)}, f32[2,512,128]{2,1,0:T(8,128)S(1)}, u32[]{:S(2)}, u32[]{:S(2)}) %collective-permute-start.59) | collective-permute-done | bytes 524320 | tf_op jit(solution)/shard_map/ppermute | solution.py:541
  261.6 11.1 %collective-permute-done.60.fl = f32[2,512,128]{2,1,0:T(8,128)S(1)} collective-permute-done((f32[2,512,128]{2,1,0:T(8,128)S(1)}, f32[2,512,128]{2,1,0:T(8,128)S(1)}, u32[]{:S(2)}, u32[]{:S(2)}) %collective-permute-start.60) | collective-permute-done | bytes 524320 | tf_op jit(solution)/shard_map/ppermute | solution.py:541
  272.8 4.2 %shard_map.100 = f32[2,512,512]{2,1,0:T(8,128)} custom-call(f32[8,128]{1,0:T(8,128)S(1)} %get-tuple-element.64.top_ref, f32[2,512,512]{2,1,0:T(8,128)S(1)} %copy-done.1, f32[2,512,512]{2,1,0:T(8,128)} %get-tuple-element.68.g, f32[2,512,128]{2,1,0:T(8,128)S(1)} %collective-permute-done.59.fr, f32[2,512,128]{2,1,0:T(8,128)S(1)} %collective-permute-done.60.fl, ...), custom_call_target="tpu_custom_call" | custom-call | flops 1000000 | bytes 8000000 | tf_op jit(solution)/shard_map/pallas_call | solution.py:148
  (167 shorter events, 77.4 us)
Async XLA Ops:
  3.1 28.2 %collective-permute-start.1 = (f32[2,512,128]{2,1,0:T(8,128)}, f32[2,512,128]{2,1,0:T(8,128)}, u32[]{:S(2)}, u32[]{:S(2)}) collective-permute-start(f32[2,512,128]{2,1,0:T(8,128)} %get-tuple-element.94), channel_id=1, source_target_pairs={{4,0},{8,4},{12,8},{16,12},{20,16},{24,20},{28,24},{5,1},{9,5},{13... | collective-permute-start | bytes 1572872 | tf_op jit(solution)/shard_map/ppermute | solution.py:541
  4.5 27.2 %collective-permute-start = (f32[2,512,128]{2,1,0:T(8,128)}, f32[2,512,128]{2,1,0:T(8,128)}, u32[]{:S(2)}, u32[]{:S(2)}) collective-permute-start(f32[2,512,128]{2,1,0:T(8,128)} %get-tuple-element.95), channel_id=1, source_target_pairs={{0,4},{4,8},{8,12},{12,16},{16,20},{20,24},{24,28},{1,5},{5,9},{9,... | collective-permute-start | bytes 1572872 | tf_op jit(solution)/shard_map/ppermute | solution.py:541
  11.9 28.5 %collective-permute-start.3 = (f32[2,128,512]{2,1,0:T(8,128)}, f32[2,128,512]{2,1,0:T(8,128)}, u32[]{:S(2)}, u32[]{:S(2)}) collective-permute-start(f32[2,128,512]{2,1,0:T(8,128)} %get-tuple-element.92), channel_id=1, source_target_pairs={{1,0},{2,1},{3,2},{5,4},{6,5},{7,6},{9,8},{10,9},{11,10},{13,12},{... | collective-permute-start | bytes 1572872 | tf_op jit(solution)/shard_map/ppermute | solution.py:541
  13.2 27.2 %collective-permute-start.2 = (f32[2,128,512]{2,1,0:T(8,128)}, f32[2,128,512]{2,1,0:T(8,128)}, u32[]{:S(2)}, u32[]{:S(2)}) collective-permute-start(f32[2,128,512]{2,1,0:T(8,128)} %get-tuple-element.93), channel_id=1, source_target_pairs={{0,1},{1,2},{2,3},{4,5},{5,6},{6,7},{8,9},{9,10},{10,11},{12,13},{... | collective-permute-start | bytes 1572872 | tf_op jit(solution)/shard_map/ppermute | solution.py:541
  34.7 5.7 %collective-permute-start.4 = (f32[2,128,256]{2,1,0:T(8,128)}, f32[2,128,256]{2,1,0:T(8,128)}, u32[]{:S(2)}, u32[]{:S(2)}) collective-permute-start(f32[2,128,256]{2,1,0:T(8,128)} %get-tuple-element.39), channel_id=1, source_target_pairs={{0,1},{1,2},{2,3},{4,5},{5,6},{6,7},{8,9},{9,10},{10,11},{12,13},{... | collective-permute-start | bytes 786440 | tf_op jit(solution)/shard_map/ppermute | solution.py:541
  64.2 9.0 %collective-permute-start.12 = (f32[256,256]{1,0:T(8,128)S(1)}, f32[256,256]{1,0:T(8,128)S(1)}, u32[]{:S(2)}, u32[]{:S(2)}) collective-permute-start(f32[256,256]{1,0:T(8,128)S(1)} %get-tuple-element.98.rest_1_), channel_id=1, source_target_pairs={{0,2},{1,5},{2,0},{3,7},{4,6},{5,1},{6,4},{7,3},{8,10},{9,13},{10,... | collective-permute-start | bytes 786440 | tf_op jit(solution)/shard_map/ppermute | solution.py:602
  68.9 8.4 %collective-permute-start.7 = (f32[264,256]{1,0:T(8,128)S(1)}, f32[264,256]{1,0:T(8,128)S(1)}, u32[]{:S(2)}, u32[]{:S(2)}) collective-permute-start(f32[264,256]{1,0:T(8,128)S(1)} %pad_maximum_fusion), channel_id=1, source_target_pairs={{0,2},{1,5},{2,0},{3,7},{4,6},{5,1},{6,4},{7,3},{8,10},{9,13},{10,... | collective-permute-start | bytes 811016 | tf_op jit(solution)/shard_map/ppermute | solution.py:601
  73.2 7.0 %collective-permute-start.13 = (f32[128,256]{1,0:T(8,128)S(1)}, f32[128,256]{1,0:T(8,128)S(1)}, u32[]{:S(2)}, u32[]{:S(2)}) collective-permute-start(f32[128,256]{1,0:T(8,128)S(1)} %slice_add_fusion.22), channel_id=1, source_target_pairs={{0,4},{1,3},{2,6},{3,1},{4,0},{5,7},{6,2},{7,5},{8,12},{9,11},{10,... | collective-permute-start | bytes 393224 | tf_op jit(solution)/shard_map/ppermute | solution.py:612
  80.3 5.1 %collective-permute-start.8 = (f32[136,256]{1,0:T(8,128)S(1)}, f32[136,256]{1,0:T(8,128)S(1)}, u32[]{:S(2)}, u32[]{:S(2)}) collective-permute-start(f32[136,256]{1,0:T(8,128)S(1)} %pad_maximum_fusion.15), channel_id=1, source_target_pairs={{0,4},{1,3},{2,6},{3,1},{4,0},{5,7},{6,2},{7,5},{8,12},{9,11},{10,... | collective-permute-start | bytes 417800 | tf_op jit(solution)/shard_map/ppermute | solution.py:611
  85.5 5.2 %collective-permute-start.9 = (f32[136,256]{1,0:T(8,128)S(1)}, f32[136,256]{1,0:T(8,128)S(1)}, u32[]{:S(2)}, u32[]{:S(2)}) collective-permute-start(f32[136,256]{1,0:T(8,128)S(1)} %pad_maximum_fusion.16), channel_id=1, source_target_pairs={{0,8},{1,17},{2,10},{3,19},{4,12},{5,21},{6,14},{7,23},{8,0},{9,25... | collective-permute-start | bytes 417800 | tf_op jit(solution)/shard_map/ppermute | solution.py:622
  90.7 9.8 %collective-permute-start.10 = (f32[136,256]{1,0:T(8,128)S(1)}, f32[136,256]{1,0:T(8,128)S(1)}, u32[]{:S(2)}, u32[]{:S(2)}) collective-permute-start(f32[136,256]{1,0:T(8,128)S(1)} %pad_maximum_fusion.17), channel_id=1, source_target_pairs={{0,16},{1,9},{2,18},{3,11},{4,20},{5,13},{6,22},{7,15},{8,24},{9,1... | collective-permute-start | bytes 417800 | tf_op jit(solution)/shard_map/ppermute | solution.py:622
  92.0 5.9 %collective-permute-start.14 = (f32[128,256]{1,0:T(8,128)S(1)}, f32[128,256]{1,0:T(8,128)S(1)}, u32[]{:S(2)}, u32[]{:S(2)}) collective-permute-start(f32[128,256]{1,0:T(8,128)S(1)} %get-tuple-element.96), channel_id=1, source_target_pairs={{0,8},{1,17},{2,10},{3,19},{4,12},{5,21},{6,14},{7,23},{8,0},{9,25... | collective-permute-start | bytes 393224 | tf_op jit(solution)/shard_map/ppermute | solution.py:623
  97.9 7.3 %collective-permute-start.15 = (f32[128,256]{1,0:T(8,128)S(1)}, f32[128,256]{1,0:T(8,128)S(1)}, u32[]{:S(2)}, u32[]{:S(2)}) collective-permute-start(f32[128,256]{1,0:T(8,128)S(1)} %add.266), channel_id=1, source_target_pairs={{0,16},{1,9},{2,18},{3,11},{4,20},{5,13},{6,22},{7,15},{8,24},{9,1... | collective-permute-start | bytes 393224 | tf_op jit(solution)/shard_map/ppermute | solution.py:623
  102.0 5.1 %collective-permute-start.11 = (f32[128,256]{1,0:T(8,128)S(1)}, f32[128,256]{1,0:T(8,128)S(1)}, u32[]{:S(2)}, u32[]{:S(2)}) collective-permute-start(f32[128,256]{1,0:T(8,128)S(1)} %fusion.11), channel_id=1, source_target_pairs={{0,4},{1,3},{2,6},{3,1},{4,0},{5,7},{6,2},{7,5},{8,12},{9,11},{10,... | collective-permute-start | bytes 393224 | tf_op jit(solution)/shard_map/ppermute | solution.py:632
  105.9 6.4 %collective-permute-start.16 = (f32[128,256]{1,0:T(8,128)S(1)}, f32[128,256]{1,0:T(8,128)S(1)}, u32[]{:S(2)}, u32[]{:S(2)}) collective-permute-start(f32[128,256]{1,0:T(8,128)S(1)} %divide_subtract_fusion.4), channel_id=1, source_target_pairs={{0,4},{1,3},{2,6},{3,1},{4,0},{5,7},{6,2},{7,5},{8,12},{9,11},{10,... | collective-permute-start | bytes 393224 | tf_op jit(solution)/shard_map/ppermute | solution.py:633
  107.0 7.2 %collective-permute-start.17 = (f32[256,256]{1,0:T(8,128)S(1)}, f32[256,256]{1,0:T(8,128)S(1)}, u32[]{:S(2)}, u32[]{:S(2)}) collective-permute-start(f32[256,256]{1,0:T(8,128)S(1)} %pad_maximum_fusion.9.rest_0_.p_re), channel_id=1, source_target_pairs={{0,2},{1,5},{2,0},{3,7},{4,6},{5,1},{6,4},{7,3},{8,10},{9,13},{10,... | collective-permute-start | bytes 786440 | tf_op jit(solution)/shard_map/ppermute | solution.py:634
  112.4 6.4 %collective-permute-start.18 = (f32[256,256]{1,0:T(8,128)S(1)}, f32[256,256]{1,0:T(8,128)S(1)}, u32[]{:S(2)}, u32[]{:S(2)}) collective-permute-start(f32[256,256]{1,0:T(8,128)S(1)} %pad_maximum_fusion.10.rest_1_.p_im), channel_id=1, source_target_pairs={{0,2},{1,5},{2,0},{3,7},{4,6},{5,1},{6,4},{7,3},{8,10},{9,13},{10,... | collective-permute-start | bytes 786440 | tf_op jit(solution)/shard_map/ppermute | solution.py:634
  113.7 5.1 %collective-permute-start.19 = (f32[256,256]{1,0:T(8,128)S(1)}, f32[256,256]{1,0:T(8,128)S(1)}, u32[]{:S(2)}, u32[]{:S(2)}) collective-permute-start(f32[256,256]{1,0:T(8,128)S(1)} %pad_maximum_fusion.9.rest_0_.p_re), channel_id=1, source_target_pairs={{0,1},{1,0},{2,3},{3,2},{4,5},{5,4},{6,7},{7,6},{8,9},{9,8},{10,11... | collective-permute-start | bytes 786440 | tf_op jit(solution)/shard_map/ppermute | solution.py:635
  113.7 5.1 %collective-permute-start.20 = (f32[256,256]{1,0:T(8,128)S(1)}, f32[256,256]{1,0:T(8,128)S(1)}, u32[]{:S(2)}, u32[]{:S(2)}) collective-permute-start(f32[256,256]{1,0:T(8,128)S(1)} %pad_maximum_fusion.10.rest_1_.p_im), channel_id=1, source_target_pairs={{0,1},{1,0},{2,3},{3,2},{4,5},{5,4},{6,7},{7,6},{8,9},{9,8},{10,11... | collective-permute-start | bytes 786440 | tf_op jit(solution)/shard_map/ppermute | solution.py:635
  137.1 6.4 %collective-permute-start.29 = (f32[256,256]{1,0:T(8,128)S(1)}, f32[256,256]{1,0:T(8,128)S(1)}, u32[]{:S(2)}, u32[]{:S(2)}) collective-permute-start(f32[256,256]{1,0:T(8,128)S(1)} %get-tuple-element.106.rest_1_), channel_id=1, source_target_pairs={{0,2},{1,5},{2,0},{3,7},{4,6},{5,1},{6,4},{7,3},{8,10},{9,13},{10,... | collective-permute-start | bytes 786440 | tf_op jit(solution)/shard_map/ppermute | solution.py:602
  138.4 8.5 %collective-permute-start.24 = (f32[256,256]{1,0:T(8,128)S(1)}, f32[256,256]{1,0:T(8,128)S(1)}, u32[]{:S(2)}, u32[]{:S(2)}) collective-permute-start(f32[256,256]{1,0:T(8,128)S(1)} %get-tuple-element.107.rest_0_), channel_id=1, source_target_pairs={{0,2},{1,5},{2,0},{3,7},{4,6},{5,1},{6,4},{7,3},{8,10},{9,13},{10,... | collective-permute-start | bytes 786440 | tf_op jit(solution)/shard_map/ppermute | solution.py:601
  143.6 5.0 %collective-permute-start.30 = (f32[128,256]{1,0:T(8,128)S(1)}, f32[128,256]{1,0:T(8,128)S(1)}, u32[]{:S(2)}, u32[]{:S(2)}) collective-permute-start(f32[128,256]{1,0:T(8,128)S(1)} %slice_add_fusion.14), channel_id=1, source_target_pairs={{0,4},{1,3},{2,6},{3,1},{4,0},{5,7},{6,2},{7,5},{8,12},{9,11},{10,... | collective-permute-start | bytes 393224 | tf_op jit(solution)/shard_map/ppermute | solution.py:612
  148.7 5.0 %collective-permute-start.25 = (f32[128,256]{1,0:T(8,128)S(1)}, f32[128,256]{1,0:T(8,128)S(1)}, u32[]{:S(2)}, u32[]{:S(2)}) collective-permute-start(f32[128,256]{1,0:T(8,128)S(1)} %get-tuple-element.105), channel_id=1, source_target_pairs={{0,4},{1,3},{2,6},{3,1},{4,0},{5,7},{6,2},{7,5},{8,12},{9,11},{10,... | collective-permute-start | bytes 393224 | tf_op jit(solution)/shard_map/ppermute | solution.py:611
  150.2 6.2 %collective-permute-start.31 = (f32[128,256]{1,0:T(8,128)S(1)}, f32[128,256]{1,0:T(8,128)S(1)}, u32[]{:S(2)}, u32[]{:S(2)}) collective-permute-start(f32[128,256]{1,0:T(8,128)S(1)} %get-tuple-element.104), channel_id=1, source_target_pairs={{0,8},{1,17},{2,10},{3,19},{4,12},{5,21},{6,14},{7,23},{8,0},{9,25... | collective-permute-start | bytes 393224 | tf_op jit(solution)/shard_map/ppermute | solution.py:623
  153.7 6.8 %collective-permute-start.26 = (f32[128,256]{1,0:T(8,128)S(1)}, f32[128,256]{1,0:T(8,128)S(1)}, u32[]{:S(2)}, u32[]{:S(2)}) collective-permute-start(f32[128,256]{1,0:T(8,128)S(1)} %fusion.8), channel_id=1, source_target_pairs={{0,8},{1,17},{2,10},{3,19},{4,12},{5,21},{6,14},{7,23},{8,0},{9,25... | collective-permute-start | bytes 393224 | tf_op jit(solution)/shard_map/ppermute | solution.py:622
  156.3 6.4 %collective-permute-start.32 = (f32[128,256]{1,0:T(8,128)S(1)}, f32[128,256]{1,0:T(8,128)S(1)}, u32[]{:S(2)}, u32[]{:S(2)}) collective-permute-start(f32[128,256]{1,0:T(8,128)S(1)} %add.282), channel_id=1, source_target_pairs={{0,16},{1,9},{2,18},{3,11},{4,20},{5,13},{6,22},{7,15},{8,24},{9,1... | collective-permute-start | bytes 393224 | tf_op jit(solution)/shard_map/ppermute | solution.py:623
  160.6 7.2 %collective-permute-start.27 = (f32[128,256]{1,0:T(8,128)S(1)}, f32[128,256]{1,0:T(8,128)S(1)}, u32[]{:S(2)}, u32[]{:S(2)}) collective-permute-start(f32[128,256]{1,0:T(8,128)S(1)} %add.275), channel_id=1, source_target_pairs={{0,16},{1,9},{2,18},{3,11},{4,20},{5,13},{6,22},{7,15},{8,24},{9,1... | collective-permute-start | bytes 393224 | tf_op jit(solution)/shard_map/ppermute | solution.py:622
  163.4 6.2 %collective-permute-start.33 = (f32[128,256]{1,0:T(8,128)S(1)}, f32[128,256]{1,0:T(8,128)S(1)}, u32[]{:S(2)}, u32[]{:S(2)}) collective-permute-start(f32[128,256]{1,0:T(8,128)S(1)} %divide_subtract_fusion.2), channel_id=1, source_target_pairs={{0,4},{1,3},{2,6},{3,1},{4,0},{5,7},{6,2},{7,5},{8,12},{9,11},{10,... | collective-permute-start | bytes 393224 | tf_op jit(solution)/shard_map/ppermute | solution.py:633
  168.4 6.5 %collective-permute-start.28 = (f32[128,256]{1,0:T(8,128)S(1)}, f32[128,256]{1,0:T(8,128)S(1)}, u32[]{:S(2)}, u32[]{:S(2)}) collective-permute-start(f32[128,256]{1,0:T(8,128)S(1)} %divide_subtract_fusion.3), channel_id=1, source_target_pairs={{0,4},{1,3},{2,6},{3,1},{4,0},{5,7},{6,2},{7,5},{8,12},{9,11},{10,... | collective-permute-start | bytes 393224 | tf_op jit(solution)/shard_map/ppermute | solution.py:632
  169.6 8.1 %collective-permute-start.35 = (f32[256,256]{1,0:T(8,128)S(1)}, f32[256,256]{1,0:T(8,128)S(1)}, u32[]{:S(2)}, u32[]{:S(2)}) collective-permute-start(f32[256,256]{1,0:T(8,128)S(1)} %pad_maximum_fusion.12.rest_1_.p_im), channel_id=1, source_target_pairs={{0,2},{1,5},{2,0},{3,7},{4,6},{5,1},{6,4},{7,3},{8,10},{9,13},{10,... | collective-permute-start | bytes 786440 | tf_op jit(solution)/shard_map/ppermute | solution.py:634
  174.9 6.6 %collective-permute-start.34 = (f32[256,256]{1,0:T(8,128)S(1)}, f32[256,256]{1,0:T(8,128)S(1)}, u32[]{:S(2)}, u32[]{:S(2)}) collective-permute-start(f32[256,256]{1,0:T(8,128)S(1)} %pad_maximum_fusion.11.rest_0_.p_re), channel_id=1, source_target_pairs={{0,2},{1,5},{2,0},{3,7},{4,6},{5,1},{6,4},{7,3},{8,10},{9,13},{10,... | collective-permute-start | bytes 786440 | tf_op jit(solution)/shard_map/ppermute | solution.py:634
  188.9 11.6 %collective-permute-start.46 = (f32[256,256]{1,0:T(8,128)S(1)}, f32[256,256]{1,0:T(8,128)S(1)}, u32[]{:S(2)}, u32[]{:S(2)}) collective-permute-start(f32[256,256]{1,0:T(8,128)S(1)} %get-tuple-element.102.rest_1_), channel_id=1, source_target_pairs={{0,2},{1,5},{2,0},{3,7},{4,6},{5,1},{6,4},{7,3},{8,10},{9,13},{10,... | collective-permute-start | bytes 786440 | tf_op jit(solution)/shard_map/ppermute | solution.py:602
  196.1 10.4 %collective-permute-start.41 = (f32[256,256]{1,0:T(8,128)S(1)}, f32[256,256]{1,0:T(8,128)S(1)}, u32[]{:S(2)}, u32[]{:S(2)}) collective-permute-start(f32[256,256]{1,0:T(8,128)S(1)} %get-tuple-element.103.rest_0_), channel_id=1, source_target_pairs={{0,2},{1,5},{2,0},{3,7},{4,6},{5,1},{6,4},{7,3},{8,10},{9,13},{10,... | collective-permute-start | bytes 786440 | tf_op jit(solution)/shard_map/ppermute | solution.py:601
  200.5 8.9 %collective-permute-start.47 = (f32[128,256]{1,0:T(8,128)S(1)}, f32[128,256]{1,0:T(8,128)S(1)}, u32[]{:S(2)}, u32[]{:S(2)}) collective-permute-start(f32[128,256]{1,0:T(8,128)S(1)} %slice_add_fusion.6), channel_id=1, source_target_pairs={{0,4},{1,3},{2,6},{3,1},{4,0},{5,7},{6,2},{7,5},{8,12},{9,11},{10,... | collective-permute-start | bytes 393224 | tf_op jit(solution)/shard_map/ppermute | solution.py:612
  209.5 5.0 %collective-permute-start.42 = (f32[128,256]{1,0:T(8,128)S(1)}, f32[128,256]{1,0:T(8,128)S(1)}, u32[]{:S(2)}, u32[]{:S(2)}) collective-permute-start(f32[128,256]{1,0:T(8,128)S(1)} %get-tuple-element.101), channel_id=1, source_target_pairs={{0,4},{1,3},{2,6},{3,1},{4,0},{5,7},{6,2},{7,5},{8,12},{9,11},{10,... | collective-permute-start | bytes 393224 | tf_op jit(solution)/shard_map/ppermute | solution.py:611
  211.6 6.1 %collective-permute-start.48 = (f32[128,256]{1,0:T(8,128)S(1)}, f32[128,256]{1,0:T(8,128)S(1)}, u32[]{:S(2)}, u32[]{:S(2)}) collective-permute-start(f32[128,256]{1,0:T(8,128)S(1)} %get-tuple-element.100.refs_4_), channel_id=1, source_target_pairs={{0,8},{1,17},{2,10},{3,19},{4,12},{5,21},{6,14},{7,23},{8,0},{9,25... | collective-permute-start | bytes 393224 | tf_op jit(solution)/shard_map/ppermute | solution.py:623
  214.6 12.5 %collective-permute-start.43 = (f32[128,256]{1,0:T(8,128)S(1)}, f32[128,256]{1,0:T(8,128)S(1)}, u32[]{:S(2)}, u32[]{:S(2)}) collective-permute-start(f32[128,256]{1,0:T(8,128)S(1)} %fusion.6.refs_3_), channel_id=1, source_target_pairs={{0,8},{1,17},{2,10},{3,19},{4,12},{5,21},{6,14},{7,23},{8,0},{9,25... | collective-permute-start | bytes 393224 | tf_op jit(solution)/shard_map/ppermute | solution.py:622
  217.8 10.5 %collective-permute-start.49 = (f32[128,256]{1,0:T(8,128)S(1)}, f32[128,256]{1,0:T(8,128)S(1)}, u32[]{:S(2)}, u32[]{:S(2)}) collective-permute-start(f32[128,256]{1,0:T(8,128)S(1)} %add.298), channel_id=1, source_target_pairs={{0,16},{1,9},{2,18},{3,11},{4,20},{5,13},{6,22},{7,15},{8,24},{9,1... | collective-permute-start | bytes 393224 | tf_op jit(solution)/shard_map/ppermute | solution.py:623
  222.7 23.7 %collective-permute-start.57 = (f32[2,128,768]{2,1,0:T(8,128)S(1)}, f32[2,128,768]{2,1,0:T(8,128)S(1)}, u32[]{:S(2)}, u32[]{:S(2)}) collective-permute-start(f32[2,128,768]{2,1,0:T(8,128)S(1)} %get-tuple-element.71), channel_id=1, source_target_pairs={{1,0},{2,1},{3,2},{5,4},{6,5},{7,6},{9,8},{10,9},{11,10},{13,12},{... | collective-permute-start | bytes 2359304 | tf_op jit(solution)/shard_map/ppermute | solution.py:541
  224.0 22.4 %collective-permute-start.58 = (f32[2,128,768]{2,1,0:T(8,128)S(1)}, f32[2,128,768]{2,1,0:T(8,128)S(1)}, u32[]{:S(2)}, u32[]{:S(2)}) collective-permute-start(f32[2,128,768]{2,1,0:T(8,128)S(1)} %get-tuple-element.72), channel_id=1, source_target_pairs={{0,1},{1,2},{2,3},{4,5},{5,6},{6,7},{8,9},{9,10},{10,11},{12,13},{... | collective-permute-start | bytes 2359304 | tf_op jit(solution)/shard_map/ppermute | solution.py:541
  227.1 7.2 %collective-permute-start.44 = (f32[128,256]{1,0:T(8,128)S(1)}, f32[128,256]{1,0:T(8,128)S(1)}, u32[]{:S(2)}, u32[]{:S(2)}) collective-permute-start(f32[128,256]{1,0:T(8,128)S(1)} %add.291), channel_id=1, source_target_pairs={{0,16},{1,9},{2,18},{3,11},{4,20},{5,13},{6,22},{7,15},{8,24},{9,1... | collective-permute-start | bytes 393224 | tf_op jit(solution)/shard_map/ppermute | solution.py:622
  228.8 6.2 %collective-permute-start.50 = (f32[128,256]{1,0:T(8,128)S(1)}, f32[128,256]{1,0:T(8,128)S(1)}, u32[]{:S(2)}, u32[]{:S(2)}) collective-permute-start(f32[128,256]{1,0:T(8,128)S(1)} %divide_subtract_fusion), channel_id=1, source_target_pairs={{0,4},{1,3},{2,6},{3,1},{4,0},{5,7},{6,2},{7,5},{8,12},{9,11},{10,... | collective-permute-start | bytes 393224 | tf_op jit(solution)/shard_map/ppermute | solution.py:633
  234.9 5.0 %collective-permute-start.45 = (f32[128,256]{1,0:T(8,128)S(1)}, f32[128,256]{1,0:T(8,128)S(1)}, u32[]{:S(2)}, u32[]{:S(2)}) collective-permute-start(f32[128,256]{1,0:T(8,128)S(1)} %divide_subtract_fusion.1), channel_id=1, source_target_pairs={{0,4},{1,3},{2,6},{3,1},{4,0},{5,7},{6,2},{7,5},{8,12},{9,11},{10,... | collective-permute-start | bytes 393224 | tf_op jit(solution)/shard_map/ppermute | solution.py:632
  235.0 6.5 %collective-permute-start.52 = (f32[256,256]{1,0:T(8,128)S(1)}, f32[256,256]{1,0:T(8,128)S(1)}, u32[]{:S(2)}, u32[]{:S(2)}) collective-permute-start(f32[256,256]{1,0:T(8,128)S(1)} %pad_maximum_fusion.14.refs_1_), channel_id=1, source_target_pairs={{0,2},{1,5},{2,0},{3,7},{4,6},{5,1},{6,4},{7,3},{8,10},{9,13},{10,... | collective-permute-start | bytes 786440 | tf_op jit(solution)/shard_map/ppermute | solution.py:634
  240.0 6.4 %collective-permute-start.51 = (f32[256,256]{1,0:T(8,128)S(1)}, f32[256,256]{1,0:T(8,128)S(1)}, u32[]{:S(2)}, u32[]{:S(2)}) collective-permute-start(f32[256,256]{1,0:T(8,128)S(1)} %pad_maximum_fusion.13.refs_0_), channel_id=1, source_target_pairs={{0,2},{1,5},{2,0},{3,7},{4,6},{5,1},{6,4},{7,3},{8,10},{9,13},{10,... | collective-permute-start | bytes 786440 | tf_op jit(solution)/shard_map/ppermute | solution.py:634
  240.6 12.4 %collective-permute-start.54 = (f32[256,256]{1,0:T(8,128)S(1)}, f32[256,256]{1,0:T(8,128)S(1)}, u32[]{:S(2)}, u32[]{:S(2)}) collective-permute-start(f32[256,256]{1,0:T(8,128)S(1)} %pad_maximum_fusion.14.refs_1_), channel_id=1, source_target_pairs={{0,1},{1,0},{2,3},{3,2},{4,5},{5,4},{6,7},{7,6},{8,9},{9,8},{10,11... | collective-permute-start | bytes 786440 | tf_op jit(solution)/shard_map/ppermute | solution.py:635
  246.5 15.1 %collective-permute-start.59 = (f32[2,512,128]{2,1,0:T(8,128)S(1)}, f32[2,512,128]{2,1,0:T(8,128)S(1)}, u32[]{:S(2)}, u32[]{:S(2)}) collective-permute-start(f32[2,512,128]{2,1,0:T(8,128)S(1)} %get-tuple-element.73), channel_id=1, source_target_pairs={{4,0},{8,4},{12,8},{16,12},{20,16},{24,20},{28,24},{5,1},{9,5},{13... | collective-permute-start | bytes 1572872 | tf_op jit(solution)/shard_map/ppermute | solution.py:541
  247.8 25.0 %collective-permute-start.60 = (f32[2,512,128]{2,1,0:T(8,128)S(1)}, f32[2,512,128]{2,1,0:T(8,128)S(1)}, u32[]{:S(2)}, u32[]{:S(2)}) collective-permute-start(f32[2,512,128]{2,1,0:T(8,128)S(1)} %get-tuple-element.74), channel_id=1, source_target_pairs={{0,4},{4,8},{8,12},{12,16},{16,20},{20,24},{24,28},{1,5},{5,9},{9,... | collective-permute-start | bytes 1572872 | tf_op jit(solution)/shard_map/ppermute | solution.py:541
  (25 other events, 133.0 us)
